TPU v7x, 32 devices: a whole 2x2x4 slice. The times are simulated.
32 devices in a mesh: dp: 8 (over z, y), mp: 4 (over x, core).
Axes of the slice: x: 2, y: 2, z: 4, core: 2. Of those that a mesh axis runs over, the one named last changes fastest.
Arguments:
- post_stream: float32 [32768, 512], P(('dp', 'mp')), may hold values from -6 to 6
- pre_stream: float32 [32768, 512], P(('dp', 'mp')), may hold values from -6 to 6
- seq_lengths: int32 [8, 13], P('dp'), may hold values from 1 to 2048, 4096 in all within a row
- qkv_weight: bfloat16 [512, 3, 512], P(None, None, 'mp'), may hold values from -0.25 to 0.25
- query_bias: bfloat16 [512], P('mp'), may hold values from -3 to 3
- value_bias: bfloat16 [512], P('mp'), may hold values from -3 to 3
- out_weight: bfloat16 [512, 512], P('mp'), may hold values from -0.75 to 0.75
- out_bias: bfloat16 [512], replicated, may hold values from -2 to 2
- norm1_gain: bfloat16 [512], replicated, may hold values from 0.5 to 1.5
- norm1_shift: bfloat16 [512], replicated, may hold values from -2 to 2
- up_weight: bfloat16 [512, 2048], P(None, 'mp'), may hold values from -0.25 to 0.25
- up_bias: bfloat16 [2048], P('mp'), may hold values from -3 to 3
- down_weight: bfloat16 [2048, 512], P('mp'), may hold values from -0.1875 to 0.1875
- down_bias: bfloat16 [512], replicated, may hold values from -2 to 2
- norm2_gain: bfloat16 [512], replicated, may hold values from 0.5 to 1.5
- norm2_shift: bfloat16 [512], replicated, may hold values from -2 to 2
- post_cotan: float32 [32768, 512], P(('dp', 'mp')), may hold values from -6 to 6
- pre_cotan: float32 [32768, 512], P(('dp', 'mp')), may hold values from -6 to 6
Outputs:
- post_out: float32 [32768, 512], P(('dp', 'mp'))
- pre_out: float32 [32768, 512], P(('dp', 'mp'))
- post_grad: float32 [32768, 512], P(('dp', 'mp'))
- qkv_weight_grad: float32 [512, 3, 512], P(None, None, 'mp')
- query_bias_grad: float32 [512], P('mp')
- value_bias_grad: float32 [512], P('mp')
- out_weight_grad: float32 [512, 512], P('mp')
- out_bias_grad: float32 [512], replicated
- norm1_gain_grad: float32 [512], replicated
- norm1_shift_grad: float32 [512], replicated
- up_weight_grad: float32 [512, 2048], P(None, 'mp')
- up_bias_grad: float32 [2048], P('mp')
- down_weight_grad: float32 [2048, 512], P('mp')
- down_bias_grad: float32 [512], replicated
- norm2_gain_grad: float32 [512], replicated
- norm2_shift_grad: float32 [512], replicated
Inputs may be any that keep to these rules, and one draw needn't show every extreme that they name: `seq_lengths`: row g serves group g: its first 12 entries are the lengths of the sequences packed in order from the group's first position, its last entry the number of padded positions at the end; each row sums to 4096, and its largest entry is 2048.
All inputs are finite; a program needn't handle non-finite values.
Results may differ from a plain program's by a relative error of at most 0.011.
The roundings to bfloat16 on the way count: a program that leaves them out, or rounds other values in their place, can miss the bound.
Values may be sent and summed in bfloat16 or wider, within the bound.
A program may use at most 192 MiB of HBM per device.

v0:
```python
import jax
import jax.numpy as jnp
from jax import lax
from jax.sharding import PartitionSpec as P

HEAD_DIM = 64


EPSILON = 1e-05
MASKED = -1e30


def gelu_tanh(value):
    return jax.nn.gelu(value, approximate=True)


def gelu_backward(pre_act, hidden_grad):
    pullback = jax.vjp(gelu_tanh, pre_act)[1]
    return pullback(hidden_grad)[0]


def segment_ids(length_row, group_rows):
    count = length_row.shape[0] - 1
    bounds = jnp.cumsum(length_row[:count], dtype=jnp.int32)
    places = jnp.arange(group_rows, dtype=jnp.int32)
    segment = jnp.sum(
        (places[None, :] >= bounds[:, None]).astype(jnp.int32), axis=0, dtype=jnp.int32
    )
    return jnp.where(places >= bounds[count - 1], count + places, segment)


def block_mask(segment, start, block_rows):
    query_segment = lax.dynamic_slice_in_dim(segment, start, block_rows, 0)
    query_place = start + jnp.arange(block_rows, dtype=jnp.int32)
    key_place = jnp.arange(segment.shape[0], dtype=jnp.int32)
    return (query_segment[:, None] == segment[None, :]) & (
        key_place[None, :] <= query_place[:, None]
    )


def block_probs(query_block, keys, segment, start):
    raw = jnp.einsum("qhd,khd->hqk", query_block, keys, preferred_element_type=jnp.float32)
    raw = raw * query_block.shape[2] ** (-0.5)
    allowed = block_mask(segment, start, query_block.shape[0])
    return jax.nn.softmax(jnp.where(allowed[None], raw, MASKED), axis=-1)


def split_blocks(array, block_rows):
    count = array.shape[0] // block_rows
    return array.reshape(count, block_rows, array.shape[1], array.shape[2])


def attend_forward(query, keys, values, segment, block_rows):
    count = query.shape[0] // block_rows
    starts = jnp.arange(count, dtype=jnp.int32) * block_rows

    def one_block(packed):
        query_block, start = packed
        attention = block_probs(query_block, keys, segment, start).astype(jnp.bfloat16)
        return jnp.einsum("hqk,khd->qhd", attention, values, preferred_element_type=jnp.float32)

    result = lax.map(one_block, (split_blocks(query, block_rows), starts))
    return result.reshape(query.shape[0], query.shape[1] * query.shape[2])


def attend_backward(query, keys, values, attended_grad, segment, block_rows):
    count = query.shape[0] // block_rows
    starts = jnp.arange(count, dtype=jnp.int32) * block_rows
    scale = query.shape[2] ** (-0.5)

    def one_block(carry, packed):
        key_grad, value_grad = carry
        query_block, grad_block, start = packed
        attention = block_probs(query_block, keys, segment, start)
        attention_low = attention.astype(jnp.bfloat16)
        upstream = jnp.einsum(
            "qhd,khd->hqk", grad_block, values, preferred_element_type=jnp.float32
        )
        inner = jnp.sum(attention * upstream, axis=-1, keepdims=True)
        score_grad = (attention * (upstream - inner)).astype(jnp.bfloat16)
        query_grad = (
            jnp.einsum("hqk,khd->qhd", score_grad, keys, preferred_element_type=jnp.float32) * scale
        )
        key_grad = (
            key_grad
            + jnp.einsum(
                "hqk,qhd->khd", score_grad, query_block, preferred_element_type=jnp.float32
            )
            * scale
        )
        value_grad = value_grad + jnp.einsum(
            "hqk,qhd->khd", attention_low, grad_block, preferred_element_type=jnp.float32
        )
        return ((key_grad, value_grad), query_grad)

    zeros = jnp.zeros(keys.shape, jnp.float32)
    carried, query_grads = lax.scan(
        one_block,
        (zeros, zeros),
        (split_blocks(query, block_rows), split_blocks(attended_grad, block_rows), starts),
    )
    return (query_grads.reshape(query.shape), carried[0], carried[1])


def norm_forward(summed, norm_gain, norm_shift):
    center = summed - jnp.mean(summed, axis=-1, keepdims=True)
    inverse = lax.rsqrt(jnp.mean(center * center, axis=-1, keepdims=True) + EPSILON)
    normed = center * inverse
    return (normed, inverse, normed * norm_gain + norm_shift)


def norm_backward(cotangent, normed, inverse, norm_gain):
    scaled = cotangent * norm_gain
    return inverse * (
        scaled
        - jnp.mean(scaled, axis=-1, keepdims=True)
        - normed * jnp.mean(scaled * normed, axis=-1, keepdims=True)
    )


def body(
    post_stream,
    pre_stream,
    seq_lengths,
    qkv_weight,
    query_bias,
    value_bias,
    out_weight,
    out_bias,
    norm1_gain,
    norm1_shift,
    up_weight,
    up_bias,
    down_weight,
    down_bias,
    norm2_gain,
    norm2_shift,
    post_cotan,
    pre_cotan,
):
    model_width = post_stream.shape[1]
    local_width = out_weight.shape[0]
    local_heads = local_width // HEAD_DIM
    post_low = post_stream.astype(jnp.bfloat16)
    tokens_all = lax.all_gather(post_low, "mp", axis=0, tiled=True)
    group_rows = tokens_all.shape[0]
    block_rows = min(512, group_rows)
    segment = segment_ids(seq_lengths[0], group_rows)
    qkv_flat = qkv_weight.reshape(model_width, 3 * local_width)
    bias_stack = jnp.concatenate([query_bias, jnp.zeros_like(query_bias), value_bias])
    qkv_low = (
        jnp.dot(tokens_all, qkv_flat, preferred_element_type=jnp.float32) + bias_stack
    ).astype(jnp.bfloat16)
    qkv_low = qkv_low.reshape(group_rows, 3, local_heads, HEAD_DIM)
    query = qkv_low[:, 0]
    keys = qkv_low[:, 1]
    values = qkv_low[:, 2]
    attended = attend_forward(query, keys, values, segment, block_rows).astype(jnp.bfloat16)
    rows_part = attended
    branch = (
        lax.psum_scatter(
            jnp.dot(rows_part, out_weight, preferred_element_type=jnp.float32),
            "mp",
            scatter_dimension=0,
            tiled=True,
        )
        + out_bias
    )
    normed1, inverse1, mid = norm_forward(post_stream + branch, norm1_gain, norm1_shift)
    pre_mid = pre_stream + branch
    mid_low = mid.astype(jnp.bfloat16)
    mid_all = lax.all_gather(mid_low, "mp", axis=0, tiled=True)
    pre_act = jnp.dot(mid_all, up_weight, preferred_element_type=jnp.float32) + up_bias
    hidden = gelu_tanh(pre_act).astype(jnp.bfloat16)
    rows_part = hidden
    ffn = (
        lax.psum_scatter(
            jnp.dot(rows_part, down_weight, preferred_element_type=jnp.float32),
            "mp",
            scatter_dimension=0,
            tiled=True,
        )
        + down_bias
    )
    normed2, inverse2, post_out = norm_forward(mid + ffn, norm2_gain, norm2_shift)
    pre_out = pre_mid + ffn
    gain2_grad = jnp.sum(post_cotan * normed2, axis=0)
    shift2_grad = jnp.sum(post_cotan, axis=0)
    sum2_grad = norm_backward(post_cotan, normed2, inverse2, norm2_gain)
    ffn_grad = (sum2_grad + pre_cotan).astype(jnp.bfloat16)
    down_bias_grad = jnp.sum(ffn_grad.astype(jnp.float32), axis=0)
    grad_all = lax.all_gather(ffn_grad, "mp", axis=0, tiled=True)
    hidden_grad = jnp.einsum("td,fd->tf", grad_all, down_weight, preferred_element_type=jnp.float32)
    act_grad = gelu_backward(pre_act, hidden_grad).astype(jnp.bfloat16)
    down_weight_grad = jnp.einsum("tf,td->fd", hidden, grad_all, preferred_element_type=jnp.float32)
    up_weight_grad = jnp.einsum("td,tf->df", mid_all, act_grad, preferred_element_type=jnp.float32)
    up_bias_grad = jnp.sum(act_grad.astype(jnp.float32), axis=0)
    rows_part = act_grad
    mid_from_ffn = lax.psum_scatter(
        jnp.einsum("tf,df->td", rows_part, up_weight, preferred_element_type=jnp.float32),
        "mp",
        scatter_dimension=0,
        tiled=True,
    )
    mid_grad = sum2_grad + mid_from_ffn
    gain1_grad = jnp.sum(mid_grad * normed1, axis=0)
    shift1_grad = jnp.sum(mid_grad, axis=0)
    sum1_grad = norm_backward(mid_grad, normed1, inverse1, norm1_gain)
    branch_grad = (sum1_grad + pre_cotan).astype(jnp.bfloat16)
    out_bias_grad = jnp.sum(branch_grad.astype(jnp.float32), axis=0)
    branch_all = lax.all_gather(branch_grad, "mp", axis=0, tiled=True)
    out_weight_grad = jnp.einsum(
        "ta,td->ad", attended, branch_all, preferred_element_type=jnp.float32
    )
    attended_grad = jnp.einsum(
        "td,ad->ta", branch_all, out_weight, preferred_element_type=jnp.float32
    ).astype(jnp.bfloat16)
    attended_grad = attended_grad.reshape(group_rows, local_heads, HEAD_DIM)
    query_grad, key_grad, value_grad = attend_backward(
        query, keys, values, attended_grad, segment, block_rows
    )
    qkv_grad = jnp.stack([query_grad, key_grad, value_grad], axis=1)
    qkv_grad = qkv_grad.reshape(group_rows, 3 * local_width).astype(jnp.bfloat16)
    qkv_weight_grad = jnp.einsum(
        "td,tc->dc", tokens_all, qkv_grad, preferred_element_type=jnp.float32
    )
    qkv_weight_grad = qkv_weight_grad.reshape(model_width, 3, local_width)
    column_grad = jnp.sum(qkv_grad.astype(jnp.float32), axis=0)
    query_bias_grad = column_grad[:local_width]
    value_bias_grad = column_grad[2 * local_width :]
    rows_part = qkv_grad
    post_grad = sum1_grad + lax.psum_scatter(
        jnp.einsum("tc,dc->td", rows_part, qkv_flat, preferred_element_type=jnp.float32),
        "mp",
        scatter_dimension=0,
        tiled=True,
    )
    (
        qkv_weight_grad,
        query_bias_grad,
        value_bias_grad,
        out_weight_grad,
        up_weight_grad,
        up_bias_grad,
        down_weight_grad,
    ) = lax.psum(
        (
            qkv_weight_grad,
            query_bias_grad,
            value_bias_grad,
            out_weight_grad,
            up_weight_grad,
            up_bias_grad,
            down_weight_grad,
        ),
        "dp",
    )
    out_bias_grad, gain1_grad, shift1_grad, down_bias_grad, gain2_grad, shift2_grad = lax.psum(
        (out_bias_grad, gain1_grad, shift1_grad, down_bias_grad, gain2_grad, shift2_grad),
        ("dp", "mp"),
    )
    return (
        post_out,
        pre_out,
        post_grad,
        qkv_weight_grad,
        query_bias_grad,
        value_bias_grad,
        out_weight_grad,
        out_bias_grad,
        gain1_grad,
        shift1_grad,
        up_weight_grad,
        up_bias_grad,
        down_weight_grad,
        down_bias_grad,
        gain2_grad,
        shift2_grad,
    )


def solution(mesh):
    return jax.shard_map(
        body,
        mesh=mesh,
        in_specs=(
            P(("dp", "mp"), None),
            P(("dp", "mp"), None),
            P("dp", None),
            P(None, None, "mp"),
            P("mp"),
            P("mp"),
            P("mp", None),
            P(),
            P(),
            P(),
            P(None, "mp"),
            P("mp"),
            P("mp", None),
            P(),
            P(),
            P(),
            P(("dp", "mp"), None),
            P(("dp", "mp"), None),
        ),
        out_specs=(
            P(("dp", "mp"), None),
            P(("dp", "mp"), None),
            P(("dp", "mp"), None),
            P(None, None, "mp"),
            P("mp"),
            P("mp"),
            P("mp", None),
            P(),
            P(),
            P(),
            P(None, "mp"),
            P("mp"),
            P("mp", None),
            P(),
            P(),
            P(),
        ),
        check_vma=False,
    )
```

profile of v0, /device:TPU:0, one launch (start us, length us, event | category | flops | bytes accessed | tf_op | source)
XLA Modules:
  0.0 1389.9 jit_solution(581984948388294516)
XLA Ops:
  12.0 35.5 %all-gather.5.cloned.1.call-done = bf16[4096,512]{1,0:T(8,128)(2,1)} async-done(((bf16[1024,512]{1,0:T(8,128)(2,1)}), bf16[4096,512]{1,0:T(8,128)(2,1)}) %all-gather.5.cloned.1.call-update) | async-done | bytes 4194320 | tf_op jit(solution)/shard_map/all_gather | solution.py:145
  54.9 204.4 %while.25 = (s32[]{:T(128)}, bf16[8,512,2,64]{1,3,2,0:T(8,128)(2,1)}, s32[8]{0:T(128)S(1)}, s32[4096]{0:T(1024)S(1)}, bf16[8,512,2,64]{1,3,2,0:T(8,128)(2,1)}, /...) while((s32[]{:T(128)}, ...), condition=%wide.region_5.6_spmd, body=%wide.region_2.5_spmd.sunk | while | flops 1105203712 | bytes 40274088 | solution.py:62
  267.7 71.2 %reduce-scatter.5.cloned.1.call-done = f32[1024,512]{1,0:T(8,128)} async-done(((f32[4096,512]{1,0:T(8,128)}), f32[1024,512]{1,0:T(8,128)}) %reduce-scatter.5.cloned.1.call-update) | async-done | bytes 2097168 | tf_op jit(solution)/shard_map/reduce_scatter | solution.py:161
  343.4 34.6 %all-gather.7.cloned.1.call-done = bf16[4096,512]{1,0:T(8,128)(2,1)} async-done(((bf16[1024,512]{1,0:T(8,128)(2,1)}), bf16[4096,512]{1,0:T(8,128)(2,1)}) %all-gather.7.cloned.1.call-update) | async-done | bytes 4194320 | tf_op jit(solution)/shard_map/all_gather | solution.py:172
  393.9 71.2 %reduce-scatter.7.cloned.1.call-done = f32[1024,512]{1,0:T(8,128)} async-done(((f32[4096,512]{1,0:T(8,128)}), f32[1024,512]{1,0:T(8,128)}) %reduce-scatter.7.cloned.1.call-update) | async-done | bytes 2097168 | tf_op jit(solution)/shard_map/reduce_scatter | solution.py:177
  476.7 34.4 %all-gather.9.cloned.1.call-done = bf16[4096,512]{1,0:T(8,128)(2,1)} async-done(((bf16[1024,512]{1,0:T(8,128)(2,1)}), bf16[4096,512]{1,0:T(8,128)(2,1)}) %all-gather.9.cloned.1.call-update) | async-done | bytes 4194320 | tf_op jit(solution)/shard_map/all_gather | solution.py:192
  511.1 10.9 convert_reduce_fusion
  530.4 71.2 %reduce-scatter.9.cloned.1.call-done = f32[1024,512]{1,0:T(8,128)} async-done(((f32[4096,512]{1,0:T(8,128)}), f32[1024,512]{1,0:T(8,128)}) %reduce-scatter.9.cloned.1.call-update) | async-done | bytes 2097168 | tf_op jit(solution)/shard_map/reduce_scatter | solution.py:199
  609.5 34.6 %all-gather.11.cloned.1.call-done = bf16[4096,512]{1,0:T(8,128)(2,1)} async-done(((bf16[1024,512]{1,0:T(8,128)(2,1)}), bf16[4096,512]{1,0:T(8,128)(2,1)}) %all-gather.11.cloned.1.call-update) | async-done | bytes 4194320 | tf_op jit(solution)/shard_map/all_gather | solution.py:211
  659.4 495.9 %while.26 = (s32[]{:T(128)}, f32[4096,2,64]{0,2,1:T(8,128)S(1)}, f32[4096,2,64]{0,2,1:T(8,128)}, bf16[8,512,2,64]{1,0,3,2:T(8,128)(2,1)}, bf16[8,512,2,64]{1,3,2...) while((s32[]{:T(128)}, f32[4096,2,64]{0,2,1:T(8,128)S(1)}, ...), condition=%wide.region_21.22_spmd.clone, body=%wide.region_17.21_spmd.clone.sunk | while | flops 2747928064 | bytes 214092048 | solution.py:97
  697.2 12.1 multiply_convert_fusion.3
  759.2 12.1 multiply_convert_fusion.3
  821.3 12.1 multiply_convert_fusion.3
  851.9 10.9 fusion.176
  883.3 12.1 multiply_convert_fusion.3
  945.3 12.1 multiply_convert_fusion.3
  976.0 10.9 fusion.176
  1007.3 12.1 multiply_convert_fusion.3
  1069.3 12.1 multiply_convert_fusion.3
  1100.0 10.9 fusion.176
  1131.3 12.1 multiply_convert_fusion.3
  1186.8 40.0 %all-reduce = (f32[512]{0:T(512)}, f32[512]{0:T(512)}, f32[512]{0:T(512)}, f32[512]{0:T(512)}, f32[512]{0:T(512)}, /*index=5*/f32[512]{0:T(512)}) all-reduce(f32[512]{0:T(512)S(1)} %copy-done.39, f32[512]{0:T(512)S(1)} %copy-done.37, f32[512]{0:T(512)S(1)} %copy-done.38, ...), channel_id=1, replica_groups=mesh['dp'=8,'mp'=4] {'dp','mp'}, use_global_device_ids=true, to_apply=%region_29.30 | all-reduce | flops 3072 | bytes 24576 | tf_op jit(solution)/shard_map/psum | solution.py:258
  1226.9 22.1 %all-reduce.1 = (f32[128]{0:T(128)}, f32[128]{0:T(128)}, f32[512]{0:T(512)}) all-reduce(f32[128]{0:T(128)S(1)} %slice.35, f32[128]{0:T(128)S(1)} %slice.37, f32[512]{0:T(512)S(1)} %copy-done.40), channel_id=1, replica_groups=mesh['dp'=8,'mp'=4] {'dp'}, use_global_device_ids=true, to_apply=%region_25.26 | all-reduce | flops 768 | bytes 6144 | tf_op jit(solution)/shard_map/psum | solution.py:246
  1253.2 122.6 %all-reduce.5.cloned.1.call-done = (f32[512,3,128]{2,0,1:T(8,128)}, f32[128,512]{1,0:T(8,128)}, f32[512,512]{1,0:T(8,128)}, f32[512,512]{1,0:T(8,128)}) async-done(((f32[512,3,128]{2,0,1:T(8,128)}, f32[128,512]{1,0:T(8,128)}, f32[512,512]{1,0:T(8,128)}, f32[512,512]{1,0:T(8,128)}), (f32[512,3,128]{2,0,1:T(8,128)}, f32[128,512]{1,0:T(8,128)}, f32[512,512]{1,0:T(8,128)}, ...) | async-done | bytes 3145744 | tf_op jit(solution)/shard_map/psum | solution.py:246
  (350 shorter events, 665.3 us)
Async XLA Ops:
  7.2 370.8 %copy-start = (bf16[512,512]{1,0:T(8,128)(2,1)S(1)}, bf16[512,512]{1,0:T(8,128)(2,1)}, u32[]{:S(2)}) copy-start(bf16[512,512]{1,0:T(8,128)(2,1)} %param.32) | copy-start | bytes 1572868
  7.2 40.2 %all-gather.5.cloned.1.call-start = ((), (), s32[]{:S(2)}) async-start(), calls=%async_computation.4 | async-start | bytes 5242880 | tf_op jit(solution)/shard_map/all_gather | solution.py:145
  10.1 328.8 %reduce-scatter.5.cloned.1.call-start = ((), (), s32[]{:S(2)}) async-start(), calls=%async_computation.5 | async-start | bytes 10485760 | tf_op jit(solution)/shard_map/reduce_scatter | solution.py:161
  11.1 40.3 %copy-start.18 = (bf16[512,3,128]{0,2,1:T(8,128)(2,1)}, bf16[512,3,128]{0,2,1:T(8,128)(2,1)S(1)}, u32[]{:S(2)}) copy-start(bf16[512,3,128]{0,2,1:T(8,128)(2,1)S(1)} %copy.44) | copy-start | bytes 1179652
  267.0 110.9 %all-gather.7.cloned.1.call-start = ((), (), s32[]{:S(2)}) async-start(), calls=%async_computation.6 | async-start | bytes 5242880 | tf_op jit(solution)/shard_map/all_gather | solution.py:172
  267.7 339.4 %copy-start.28 = (f32[512]{0:T(512)}, f32[512]{0:T(512)S(1)}, u32[]{:S(2)}) copy-start(f32[512]{0:T(512)S(1)} %convert_element_type.106) | copy-start | bytes 6148
  341.4 265.6 %copy-start.3 = (f32[1024,512]{1,0:T(8,128)}, f32[1024,512]{1,0:T(8,128)S(1)}, u32[]{:S(2)}) copy-start(f32[1024,512]{1,0:T(8,128)S(1)} %get-tuple-element.255) | copy-start | bytes 6291460
  341.5 265.6 %copy-start.24 = (f32[1024]{0:T(1024)}, f32[1024]{0:T(1024)S(1)}, u32[]{:S(2)}) copy-start(f32[1024]{0:T(1024)S(1)} %broadcast_multiply_fusion.5) | copy-start | bytes 12292
  341.9 265.2 %copy-start.26 = (f32[1024]{0:T(1024)}, f32[1024]{0:T(1024)S(1)}, u32[]{:S(2)}) copy-start(f32[1024]{0:T(1024)S(1)} %add_rsqrt_fusion.1) | copy-start | bytes 12292
  343.3 121.8 %reduce-scatter.7.cloned.1.call-start = ((), (), s32[]{:S(2)}) async-start(), calls=%async_computation.7 | async-start | bytes 10485760 | tf_op jit(solution)/shard_map/reduce_scatter | solution.py:177
  343.4 44.3 %copy-start.22 = (bf16[512,512]{1,0:T(8,128)(2,1)S(1)}, bf16[512,512]{1,0:T(8,128)(2,1)}, u32[]{:S(2)}) copy-start(bf16[512,512]{1,0:T(8,128)(2,1)} %param.34) | copy-start | bytes 1572868
  393.3 117.9 %all-gather.9.cloned.1.call-start = ((), (), s32[]{:S(2)}) async-start(), calls=%async_computation.8 | async-start | bytes 5242880 | tf_op jit(solution)/shard_map/all_gather | solution.py:192
  476.5 125.1 %reduce-scatter.9.cloned.1.call-start = ((), (), s32[]{:S(2)}) async-start(), calls=%async_computation.9 | async-start | bytes 10485760 | tf_op jit(solution)/shard_map/reduce_scatter | solution.py:199
  529.7 114.4 %all-gather.11.cloned.1.call-start = ((), (), s32[]{:S(2)}) async-start(), calls=%async_computation.10 | async-start | bytes 5242880 | tf_op jit(solution)/shard_map/all_gather | solution.py:211
  609.5 639.6 %reduce-scatter.11.cloned.1.call-start = ((), (), s32[]{:S(2)}) async-start(), calls=%async_computation.11 | async-start | bytes 10485760 | tf_op jit(solution)/shard_map/reduce_scatter | solution.py:232
  1069.3 12.1 copy-start.6
  1167.2 208.6 %all-reduce.5.cloned.1.call-start = ((), (), s32[]{:S(2)}) async-start(), calls=%async_computation.12 | async-start | bytes 6291456 | tf_op jit(solution)/shard_map/psum | solution.py:246
  1182.4 44.5 %copy-start.40 = (f32[512]{0:T(512)S(1)}, f32[512]{0:T(512)}, u32[]{:S(2)}) copy-start(f32[512]{0:T(512)} %get-tuple-element.247) | copy-start | bytes 6148
  1182.4 66.7 %copy-start.4 = (f32[1024,512]{1,0:T(8,128)S(1)}, f32[1024,512]{1,0:T(8,128)}, u32[]{:S(2)}) copy-start(f32[1024,512]{1,0:T(8,128)} %copy-done.3) | copy-start | bytes 6291460
  1182.4 66.7 %copy-start.25 = (f32[1024]{0:T(1024)S(1)}, f32[1024]{0:T(1024)}, u32[]{:S(2)}) copy-start(f32[1024]{0:T(1024)} %copy-done.24) | copy-start | bytes 12292
  1182.4 66.6 %copy-start.27 = (f32[1024]{0:T(1024)S(1)}, f32[1024]{0:T(1024)}, u32[]{:S(2)}) copy-start(f32[1024]{0:T(1024)} %copy-done.26) | copy-start | bytes 12292
  1182.5 66.6 %copy-start.29 = (f32[512]{0:T(512)S(1)}, f32[512]{0:T(512)}, u32[]{:S(2)}) copy-start(f32[512]{0:T(512)} %copy-done.28) | copy-start | bytes 6148
  1182.5 66.6 %copy-start.31 = (f32[1024]{0:T(1024)S(1)}, f32[1024]{0:T(1024)}, u32[]{:S(2)}) copy-start(f32[1024]{0:T(1024)} %copy-done.30) | copy-start | bytes 12292
  1182.5 66.6 %copy-start.33 = (f32[1024]{0:T(1024)S(1)}, f32[1024]{0:T(1024)}, u32[]{:S(2)}) copy-start(f32[1024]{0:T(1024)} %copy-done.32) | copy-start | bytes 12292
  (51 other events, 298.9 us)
Sparse Core Ops, SparseCore 0:
  10.2 37.1 all-gather.4
  267.1 71.7 reduce-scatter.4
  343.4 34.4 all-gather.6
  393.4 71.6 reduce-scatter.6
  476.6 34.4 all-gather.8
  529.8 71.7 reduce-scatter.8
  609.6 34.4 all-gather.10
  1167.4 73.1 reduce-scatter.10
  1245.5 130.2 all-reduce.4
where the time goes:
time: 1400 us; the launch traced here: 1390 us
  matrix products  496 us (35%)
  waiting for transfers between devices  475 us (34%)
  other arithmetic  189 us (14%)
  local copies, waits for them, and re-layouts  120 us (9%)
  blocking collectives  62.1 us (4%)
  loops' own time  32 us (2%)
  between operations  14.9 us (1%)
    sub x16, matrix products, block_probs(): return jax.nn.softmax(jnp.where(allowed[None], raw, MASKED), axis=-1)  169 us
    psum x1, waiting for transfers between devices, body(): lax.psum((qkv_weight_grad, query_bias_grad, value_bias_grad, out_weight_g...  123 us
    convert_element_type x8, other arithmetic, one_block(): score_grad = (attention * (upstream - inner)).astype(jnp.bfloat16)  96.7 us
    dot_general x8, matrix products, one_block(): jnp.einsum('hqk,qhd->khd', attention_low, grad_block, preferred_element_t...  76.3 us
    dot_general x8, matrix products, one_block(): jnp.einsum('hqk,khd->qhd', attention, values, preferred_element_type=jnp....  75 us
    reduce_scatter x1, waiting for transfers between devices, body(): lax.psum_scatter(jnp.einsum('tf,df->td', rows_part, up_weight, preferred_...  71.2 us
    reduce_scatter x1, waiting for transfers between devices, body(): lax.psum_scatter(jnp.dot(rows_part, down_weight, preferred_element_type=j...  71.2 us
    reduce_scatter x1, waiting for transfers between devices, body(): lax.psum_scatter(jnp.dot(rows_part, out_weight, preferred_element_type=jn...  71.2 us
  transfers between devices with their start and end apart: 9, of which 8 were waited for; matrix products, arithmetic and copies ran while one was open for 2% of the time, Pallas kernels for 0%

commit v1 on v0

v1 whole, which is shorter than its diff:
```python
import functools

import jax
import jax.numpy as jnp
from jax import lax
from jax.experimental import pallas as pl
from jax.experimental.pallas import tpu as pltpu
from jax.sharding import PartitionSpec as P

HEAD_DIM = 64
EPSILON = 1e-05
MASKED = -1e30
MP = 4
TILE = 256
MESH = pl.DeviceIdType.MESH
BF16 = jnp.bfloat16
F32 = jnp.float32
ANY = pl.BlockSpec(memory_space=pl.ANY)
VMEM = pl.BlockSpec(memory_space=pltpu.VMEM)
NT = (((1,), (1,)), ((), ()))
TN = (((0,), (0,)), ((), ()))
SQRT_2_OVER_PI = 0.7978845608028654


def ds(start, size):
    return pl.ds(pl.multiple_of(start, size), size)


def mp_peers():
    me = lax.axis_index("mp")
    sib = me + 1 - 2 * (me % 2)
    across = (me + 2) % MP
    diagonal = (sib + 2) % MP
    return me, sib, across, diagonal


def greet(devices):
    barrier = pltpu.get_barrier_semaphore()
    for device in devices:
        pl.semaphore_signal(barrier, inc=1, device_id=device, device_id_type=MESH)
    pl.semaphore_wait(barrier, len(devices))


def remote(src, dst, send_sem, recv_sem, device):
    return pltpu.make_async_remote_copy(
        src_ref=src,
        dst_ref=dst,
        send_sem=send_sem,
        recv_sem=recv_sem,
        device_id=device,
        device_id_type=MESH,
    )


def dot(a, b, dims=(((1,), (0,)), ((), ()))):
    return lax.dot_general(a, b, dims, preferred_element_type=F32)


def dma_sems(*shape):
    return pltpu.SemaphoreType.DMA(shape)


def project_kernel(
    post, w, prm,
    tok_t_out, q_out, k_out, v_out, kt_out, vt_out,
    stage, tok, tok_t, q_s, k_s, v_s, kt_s, vt_s,
    in_sem, send_x, recv_x, send_c, recv_c, send_f, recv_f, out_sem,
):
    me, sib, across, diagonal = mp_peers()
    dp = lax.axis_index("dp")
    rows = post.shape[0]
    width = post.shape[1]
    chunk = TILE
    count = rows // chunk
    loads = [
        pltpu.make_async_copy(post.at[pl.ds(c * chunk, chunk)], stage.at[pl.ds(c * chunk, chunk)], in_sem.at[c])
        for c in range(count)
    ]
    for load in loads:
        load.start()
    greet([(dp, sib), (dp, across)])

    def piece(owner, c):
        return ds(owner * rows + c * chunk, chunk)

    def to_across(c):
        here = piece(me, c)
        return remote(tok.at[here], tok.at[here], send_x.at[c], recv_x.at[c], (dp, across))

    def to_sibling(c):
        here = piece(me, c)
        return remote(tok.at[here], tok.at[here], send_c.at[c], recv_c.at[c], (dp, sib))

    def forward(c):
        here = piece(across, c)
        return remote(tok.at[here], tok.at[here], send_f.at[c], recv_f.at[c], (dp, sib))

    def arrived(owner, sem, c):
        here = piece(owner, c)
        return pltpu.make_async_copy(tok.at[here], tok.at[here], sem.at[c])

    for c in range(count):
        loads[c].wait()
        tok[piece(me, c)] = stage[pl.ds(c * chunk, chunk)].astype(BF16)
        to_across(c).start()
        to_sibling(c).start()

    query_bias = prm[0:1, 0:128]
    value_bias = prm[0:1, 256:384]

    def project(owner, c):
        here = piece(owner, c)
        block = tok[here]
        tok_t[:, here] = block.T
        query = (dot(block, w[0]) + query_bias).astype(BF16)
        q_s[here] = (query.astype(F32) * HEAD_DIM ** (-0.5)).astype(BF16)
        keys = dot(block, w[1]).astype(BF16)
        k_s[here] = keys
        kt_s[:, here] = keys.T
        values = (dot(block, w[2]) + value_bias).astype(BF16)
        v_s[here] = values
        vt_s[:, here] = values.T

    def outs(g, owner):
        here = ds(owner * rows, rows)
        return [
            pltpu.make_async_copy(tok_t.at[:, here], tok_t_out.at[:, here], out_sem.at[g, 0]),
            pltpu.make_async_copy(q_s.at[here], q_out.at[here], out_sem.at[g, 1]),
            pltpu.make_async_copy(k_s.at[here], k_out.at[here], out_sem.at[g, 2]),
            pltpu.make_async_copy(v_s.at[here], v_out.at[here], out_sem.at[g, 3]),
            pltpu.make_async_copy(kt_s.at[:, here], kt_out.at[:, here], out_sem.at[g, 4]),
            pltpu.make_async_copy(vt_s.at[:, here], vt_out.at[:, here], out_sem.at[g, 5]),
        ]

    def own_step(c, _):
        project(me, c)
        return 0

    lax.fori_loop(0, count, own_step, 0)
    for copy in outs(0, me):
        copy.start()

    def sibling_step(c, _):
        arrived(sib, recv_c, c).wait()
        project(sib, c)
        return 0

    lax.fori_loop(0, count, sibling_step, 0)
    for copy in outs(1, sib):
        copy.start()

    def across_step(c, _):
        arrived(across, recv_x, c).wait()
        forward(c).start()
        project(across, c)
        arrived(diagonal, recv_f, c).wait()
        project(diagonal, c)
        return 0

    lax.fori_loop(0, count, across_step, 0)
    for copy in outs(2, across) + outs(3, diagonal):
        copy.start()
    for c in range(count):
        to_across(c).wait_send()
        to_sibling(c).wait_send()
        forward(c).wait_send()
    for g, owner in enumerate((me, sib, across, diagonal)):
        for copy in outs(g, owner):
            copy.wait()


def gather_and_project(post_stream, qkv3, prm):
    rows, width = post_stream.shape
    group = rows * MP
    local = qkv3.shape[2]
    count = rows // TILE
    tall = jax.ShapeDtypeStruct((group, local), BF16)
    wide = jax.ShapeDtypeStruct((local, group), BF16)
    return pl.pallas_call(
        project_kernel,
        out_shape=(jax.ShapeDtypeStruct((width, group), BF16), tall, tall, tall, wide, wide),
        in_specs=[ANY, VMEM, VMEM],
        out_specs=(ANY,) * 6,
        scratch_shapes=[
            pltpu.VMEM((rows, width), F32),
            pltpu.VMEM((group, width), BF16),
            pltpu.VMEM((width, group), BF16),
            pltpu.VMEM((group, local), BF16),
            pltpu.VMEM((group, local), BF16),
            pltpu.VMEM((group, local), BF16),
            pltpu.VMEM((local, group), BF16),
            pltpu.VMEM((local, group), BF16),
            dma_sems(count), dma_sems(count), dma_sems(count), dma_sems(count),
            dma_sems(count), dma_sems(count), dma_sems(count), dma_sems(4, 6),
        ],
        compiler_params=pltpu.CompilerParams(
            collective_id=0, has_side_effects=True, vmem_limit_bytes=40 << 20
        ),
        cost_estimate=pl.CostEstimate(flops=2 * group * width * 3 * local, bytes_accessed=12 << 20, transcendentals=0),
        name="gather_project",
    )(post_stream, qkv3, prm)


def first_of_segment(lengths, place):
    bound = jnp.int32(0)
    start = jnp.zeros_like(place)
    for s in range(lengths.shape[0] - 1):
        bound = bound + lengths[s]
        start = jnp.where(place >= bound, bound, start)
    return jnp.where(place >= bound, place, start)


def head_masked(block, h):
    lane = lax.broadcasted_iota(jnp.int32, block.shape, 1)
    return jnp.where((lane >= h * HEAD_DIM) & (lane < (h + 1) * HEAD_DIM), block, jnp.zeros_like(block))


def attend_kernel(lengths, q_ref, k_ref, vt_ref, att_ref, lse_ref):
    i = pl.program_id(0)
    base = i * TILE
    heads = q_ref.shape[1] // HEAD_DIM
    place = base + lax.broadcasted_iota(jnp.int32, (1, TILE), 1)
    start = first_of_segment(lengths, place)
    low = first_of_segment(lengths, base) // TILE
    query = q_ref[...]
    queries = [head_masked(query, h) for h in range(heads)]

    def tile(j, carry, diagonal):
        here = ds(j * TILE, TILE)
        keys = k_ref[here]
        values_t = vt_ref[:, here]
        key_place = lax.broadcasted_iota(jnp.int32, (TILE, TILE), 0)
        allowed = key_place >= start - j * TILE
        if diagonal:
            allowed = allowed & (key_place <= place - j * TILE)
        result = []
        for h in range(heads):
            top, total, acc = carry[h]
            score = jnp.where(allowed, dot(keys, queries[h], NT), MASKED)
            new_top = jnp.maximum(top, jnp.max(score, axis=0, keepdims=True))
            alpha = jnp.exp(top - new_top)
            prob = jnp.exp(score - new_top)
            total = total * alpha + jnp.sum(prob, axis=0, keepdims=True)
            acc = acc * alpha + dot(values_t[h * HEAD_DIM : (h + 1) * HEAD_DIM], prob.astype(BF16))
            result.append((new_top, total, acc))
        return tuple(result)

    init = tuple(
        (
            jnp.full((1, TILE), MASKED, F32),
            jnp.zeros((1, TILE), F32),
            jnp.zeros((HEAD_DIM, TILE), F32),
        )
        for _ in range(heads)
    )
    carry = tile(i, init, True)
    carry = lax.fori_loop(low, i, lambda j, c: tile(j, c, False), carry)
    out_t = jnp.concatenate([acc / total for _, total, acc in carry], axis=0)
    att_ref[...] = out_t.T.astype(BF16)
    for h in range(heads):
        top, total, _ = carry[h]
        lse_ref[0, h : h + 1, :] = top + jnp.log(total)


def attend(lengths, q, k, vt):
    group, local = q.shape
    count = group // TILE
    return pl.pallas_call(
        attend_kernel,
        grid_spec=pltpu.PrefetchScalarGridSpec(
            num_scalar_prefetch=1,
            grid=(count,),
            in_specs=[
                pl.BlockSpec((TILE, local), lambda i, n: (i, 0)),
                pl.BlockSpec((group, local), lambda i, n: (0, 0)),
                pl.BlockSpec((local, group), lambda i, n: (0, 0)),
            ],
            out_specs=[
                pl.BlockSpec((TILE, local), lambda i, n: (i, 0)),
                pl.BlockSpec((1, 8, TILE), lambda i, n: (i, 0, 0)),
            ],
        ),
        out_shape=(
            jax.ShapeDtypeStruct((group, local), BF16),
            jax.ShapeDtypeStruct((count, 8, TILE), F32),
        ),
        compiler_params=pltpu.CompilerParams(vmem_limit_bytes=32 << 20),
        cost_estimate=pl.CostEstimate(flops=12 << 30, bytes_accessed=4 << 20, transcendentals=8 << 20),
        name="attend",
    )(lengths, q, k, vt)


def attend_back_kernel(
    lengths, q_ref, do_ref, o_ref, lse_ref, k_ref, v_ref, kt_ref,
    dq_ref, dk_ref, dv_ref, dk_acc, dv_acc,
):
    i = pl.program_id(0)
    base = i * TILE
    heads = q_ref.shape[1] // HEAD_DIM

    @pl.when(i == 0)
    def _():
        dk_acc[...] = jnp.zeros_like(dk_acc)
        dv_acc[...] = jnp.zeros_like(dv_acc)

    place = base + lax.broadcasted_iota(jnp.int32, (1, TILE), 1)
    start = first_of_segment(lengths, place)
    low = first_of_segment(lengths, base) // TILE
    query = q_ref[...]
    grad = do_ref[...]
    inner = (grad.astype(F32) * o_ref[...].astype(F32)).T
    queries = [head_masked(query, h) for h in range(heads)]
    grads = [head_masked(grad, h) for h in range(heads)]
    delta = [
        jnp.sum(inner[h * HEAD_DIM : (h + 1) * HEAD_DIM], axis=0, keepdims=True) for h in range(heads)
    ]
    lse = [lse_ref[0, h : h + 1, :] for h in range(heads)]

    def tile(j, carry, diagonal):
        here = ds(j * TILE, TILE)
        keys = k_ref[here]
        values = v_ref[here]
        keys_t = kt_ref[:, here]
        key_place = lax.broadcasted_iota(jnp.int32, (TILE, TILE), 0)
        allowed = key_place >= start - j * TILE
        if diagonal:
            allowed = allowed & (key_place <= place - j * TILE)
        result = []
        dv = jnp.zeros((TILE, heads * HEAD_DIM), F32)
        dk = jnp.zeros((TILE, heads * HEAD_DIM), F32)
        for h in range(heads):
            score = jnp.where(allowed, dot(keys, queries[h], NT), MASKED)
            prob = jnp.exp(score - lse[h])
            upstream = dot(values, grads[h], NT)
            score_grad = (prob * (upstream - delta[h])).astype(BF16)
            dv = dv + dot(prob.astype(BF16), grads[h])
            dk = dk + dot(score_grad, queries[h])
            result.append(carry[h] + dot(keys_t[h * HEAD_DIM : (h + 1) * HEAD_DIM], score_grad))
        dv_acc[here] += dv
        dk_acc[here] += dk
        return tuple(result)

    carry = tuple(jnp.zeros((HEAD_DIM, TILE), F32) for _ in range(heads))
    carry = tile(i, carry, True)
    carry = lax.fori_loop(low, i, lambda j, c: tile(j, c, False), carry)
    dq_t = jnp.concatenate(carry, axis=0) * HEAD_DIM ** (-0.5)
    dq_ref[...] = dq_t.T.astype(BF16)

    @pl.when(i == pl.num_programs(0) - 1)
    def _():
        dk_ref[...] = dk_acc[...].astype(BF16)
        dv_ref[...] = dv_acc[...].astype(BF16)


def attend_back(lengths, q, k, v, kt, att, lse, att_grad):
    group, local = q.shape
    count = group // TILE
    block = pl.BlockSpec((TILE, local), lambda i, n: (i, 0))
    whole = pl.BlockSpec((group, local), lambda i, n: (0, 0))
    shape = jax.ShapeDtypeStruct((group, local), BF16)
    return pl.pallas_call(
        attend_back_kernel,
        grid_spec=pltpu.PrefetchScalarGridSpec(
            num_scalar_prefetch=1,
            grid=(count,),
            in_specs=[
                block, block, block,
                pl.BlockSpec((1, 8, TILE), lambda i, n: (i, 0, 0)),
                whole, whole,
                pl.BlockSpec((local, group), lambda i, n: (0, 0)),
            ],
            out_specs=[block, whole, whole],
            scratch_shapes=[pltpu.VMEM((group, local), F32), pltpu.VMEM((group, local), F32)],
        ),
        out_shape=(shape, shape, shape),
        compiler_params=pltpu.CompilerParams(vmem_limit_bytes=32 << 20),
        cost_estimate=pl.CostEstimate(flops=30 << 30, bytes_accessed=9 << 20, transcendentals=8 << 20),
        name="attend_back",
    )(lengths, q, att_grad, att, lse, k, v, kt)


def center_and_scale(summed):
    width = summed.shape[1]
    center = summed - jnp.sum(summed, axis=1, keepdims=True) * (1.0 / width)
    inverse = lax.rsqrt(jnp.sum(center * center, axis=1, keepdims=True) * (1.0 / width) + EPSILON)
    return center * inverse, inverse


def norm_backward(cotangent, normed, inverse, gain):
    width = normed.shape[1]
    scaled = cotangent * gain
    mean = jnp.sum(scaled, axis=1, keepdims=True) * (1.0 / width)
    along = jnp.sum(scaled * normed, axis=1, keepdims=True) * (1.0 / width)
    return inverse * (scaled - mean - normed * along)


def gelu_and_slope(value):
    square = value * value
    inner = value * (SQRT_2_OVER_PI + (SQRT_2_OVER_PI * 0.044715) * square)
    half = 0.5 + 0.5 * jnp.tanh(inner)
    rise = value * (2.0 * SQRT_2_OVER_PI + (6.0 * SQRT_2_OVER_PI * 0.044715) * square)
    return value * half, half * (1.0 + (1.0 - half) * rise)


def column_sum(block):
    return jnp.sum(block, axis=0, keepdims=True)


def middle_kernel(
    att, post, pre, post_cot, pre_cot, up_own, down_own, out_own, up_across, down_across, out_across, prm,
    post_out, pre_out, sum1_out, att_grad_out, keep_out, give_out, small_out,
    post_b, pre_b, post_cot_b, pre_cot_b, att_in, w_up, w_down, w_out, prm_all,
    mid_low, hidden, act_grad, ffn_grad, branch_grad, att_grad_b, slope_b,
    post_out_b, pre_out_b, sum1_b, send_b, recv_b, keep_b, give_b,
    in_sem, own_sem, weight_sem, send_w, recv_w, send_p, recv_p,
    send_a, recv_a, send_g, recv_g, send_r, recv_r, out_sem,
):
    me, sib, across, diagonal = mp_peers()
    dp = lax.axis_index("dp")
    rows, width = post.shape
    chunk = TILE
    count = rows // chunk
    local = att.shape[1]
    hid = up_own.shape[1]
    peers = (sib, across, diagonal)

    def stream(c):
        here = pl.ds(c * chunk, chunk)
        return [
            pltpu.make_async_copy(src.at[here], dst.at[here], in_sem.at[c, n])
            for n, (src, dst) in enumerate(
                ((post, post_b), (pre, pre_b), (post_cot, post_cot_b), (pre_cot, pre_cot_b))
            )
        ]

    def own_attended():
        return pltpu.make_async_copy(
            att.at[ds(me * rows, rows)], att_in.at[:, ds(me * local, local)], own_sem.at[0]
        )

    def local_weights():
        copies = []
        for n, (owner, parts) in enumerate(
            ((me, (up_own, down_own, out_own)), (across, (up_across, down_across, out_across)))
        ):
            places = (w_up.at[owner], w_down.at[owner], w_out.at[ds(owner * local, local)])
            copies += [
                pltpu.make_async_copy(src, dst, weight_sem.at[n, k])
                for k, (src, dst) in enumerate(zip(parts, places))
            ]
        return copies

    def sent_weights():
        copies = []
        for n, (owner, parts) in enumerate(
            ((me, (up_own, down_own, out_own)), (across, (up_across, down_across, out_across)))
        ):
            places = (w_up.at[owner], w_down.at[owner], w_out.at[ds(owner * local, local)])
            copies += [
                remote(src, dst, send_w.at[n, k], recv_w.at[n, k], (dp, sib))
                for k, (src, dst) in enumerate(zip(parts, places))
            ]
        return copies

    def arriving_weights():
        copies = []
        for n, owner in enumerate((sib, diagonal)):
            places = (w_up.at[owner], w_down.at[owner], w_out.at[ds(owner * local, local)])
            copies += [pltpu.make_async_copy(p, p, recv_w.at[n, k]) for k, p in enumerate(places)]
        return copies

    def sent_prm(n):
        return remote(prm, prm_all.at[me], send_p.at[n], recv_p.at[n], (dp, peers[n]))

    def sent_attended(n, c):
        peer = peers[n]
        return remote(
            att.at[ds(peer * rows + c * chunk, chunk)],
            att_in.at[ds(c * chunk, chunk), ds(me * local, local)],
            send_a.at[n, c],
            recv_a.at[n, c],
            (dp, peer),
        )

    def arriving_attended(n, c):
        place = att_in.at[ds(c * chunk, chunk), ds(peers[n] * local, local)]
        return pltpu.make_async_copy(place, place, recv_a.at[n, c])

    def sent_grad(n, c):
        peer = peers[n]
        return remote(
            att_grad_b.at[ds(c * chunk, chunk), ds(peer * local, local)],
            att_grad_out.at[ds(me * rows + c * chunk, chunk)],
            send_g.at[n, c],
            recv_g.at[n, c],
            (dp, peer),
        )

    def arriving_grad(n, c):
        place = att_grad_out.at[ds(peers[n] * rows + c * chunk, chunk)]
        return pltpu.make_async_copy(place, place, recv_g.at[n, c])

    def own_grad(c):
        return pltpu.make_async_copy(
            att_grad_b.at[ds(c * chunk, chunk), ds(me * local, local)],
            att_grad_out.at[ds(me * rows + c * chunk, chunk)],
            out_sem.at[c, 3],
        )

    def stored(c):
        here = ds(c * chunk, chunk)
        return [
            pltpu.make_async_copy(src.at[here], dst.at[here], out_sem.at[c, n])
            for n, (src, dst) in enumerate(((post_out_b, post_out), (pre_out_b, pre_out), (sum1_b, sum1_out)))
        ]

    for copy in stream(0) + [own_attended()] + local_weights():
        copy.start()
    greet([(dp, peer) for peer in peers])
    for n in range(3):
        sent_prm(n).start()
    for c in range(count):
        for n in (2, 1, 0):
            sent_attended(n, c).start()
    for copy in sent_weights():
        copy.start()
    for c in range(1, count):
        for copy in stream(c):
            copy.start()
    prm_all[ds(me, 1)] = prm[...][None]
    small_out[...] = jnp.zeros_like(small_out)
    own_attended().wait()
    for n in range(3):
        arrived = prm_all.at[peers[n]]
        pltpu.make_async_copy(arrived, arrived, recv_p.at[n]).wait()
    for copy in local_weights() + arriving_weights():
        copy.wait()

    out_bias, gain1, shift1 = prm[1:2], prm[2:3], prm[3:4]
    down_bias, gain2, shift2 = prm[4:5], prm[5:6], prm[6:7]

    def block_step(c, _):
        here = ds(c * chunk, chunk)
        for n in range(3):
            arriving_attended(n, c).wait()
        for n in range(4):
            pltpu.make_async_copy(post_b.at[here], post_b.at[here], in_sem.at[c, n]).wait()
        branch = dot(att_in[here], w_out[...]) + out_bias
        normed1, inverse1 = center_and_scale(post_b[here] + branch)
        mid = normed1 * gain1 + shift1
        pre_mid = pre_b[here] + branch
        low = mid.astype(BF16)
        mid_low[here] = low
        ffn = jnp.zeros((chunk, width), F32)
        for f in range(MP):
            pre_act = dot(low, w_up[f]) + prm_all[f, 7:8]
            value, slope = gelu_and_slope(pre_act)
            value = value.astype(BF16)
            hidden[f, here] = value
            slope_b[f] = slope
            ffn = ffn + dot(value, w_down[f])
        ffn = ffn + down_bias
        normed2, inverse2 = center_and_scale(mid + ffn)
        post_out_b[here] = normed2 * gain2 + shift2
        pre_out_b[here] = pre_mid + ffn
        cot = post_cot_b[here]
        small_out[4:5] += column_sum(cot * normed2)
        small_out[5:6] += column_sum(cot)
        sum2_grad = norm_backward(cot, normed2, inverse2, gain2)
        grad = (sum2_grad + pre_cot_b[here]).astype(BF16)
        ffn_grad[here] = grad
        small_out[3:4] += column_sum(grad.astype(F32))
        mid_grad = sum2_grad
        for f in range(MP):
            back = (dot(grad, w_down[f], NT) * slope_b[f]).astype(BF16)
            act_grad[f, here] = back
            small_out[8 + f : 9 + f] += column_sum(back.astype(F32))
            mid_grad = mid_grad + dot(back, w_up[f], NT)
        small_out[1:2] += column_sum(mid_grad * normed1)
        small_out[2:3] += column_sum(mid_grad)
        sum1 = norm_backward(mid_grad, normed1, inverse1, gain1)
        sum1_b[here] = sum1
        grad1 = (sum1 + pre_cot_b[here]).astype(BF16)
        branch_grad[here] = grad1
        small_out[0:1] += column_sum(grad1.astype(F32))
        att_grad_b[here] = dot(grad1, w_out[...], NT).astype(BF16)
        for n in (2, 1, 0):
            sent_grad(n, c).start()
        own_grad(c).start()
        for copy in stored(c):
            copy.start()
        return 0

    lax.fori_loop(0, count, block_step, 0)

    def weight_grads(s):
        up = dot(mid_low[...], act_grad[s], TN)
        down = dot(hidden[s], ffn_grad[...], TN)
        out = dot(att_in[:, ds(s * local, local)], branch_grad[...], TN)
        return up, down, out

    def sent_sums(n):
        return remote(send_b.at[n], recv_b.at[n], send_r.at[n], recv_r.at[n], (dp, sib))

    spans = (pl.ds(0, width), pl.ds(width, hid), pl.ds(width + hid, local))
    for n, owner in enumerate((diagonal, sib)):
        for span, part in zip(spans, weight_grads(owner)):
            send_b[n, span] = part.astype(BF16)
        sent_sums(n).start()
    for span, part in zip(spans, weight_grads(across)):
        keep_b[span] = part
    sent_sums(0).wait_recv()
    give_b[...] = (keep_b[...] + recv_b[0].astype(F32)).astype(BF16)
    give = pltpu.make_async_copy(give_b, give_out, own_sem.at[1])
    give.start()
    for span, part in zip(spans, weight_grads(me)):
        keep_b[span] = part
    sent_sums(1).wait_recv()
    keep_b[...] = keep_b[...] + recv_b[1].astype(F32)
    keep = pltpu.make_async_copy(keep_b, keep_out, own_sem.at[2])
    keep.start()
    for c in range(count):
        for copy in stored(c) + [own_grad(c)]:
            copy.wait()
        for n in range(3):
            sent_attended(n, c).wait_send()
            sent_grad(n, c).wait_send()
            arriving_grad(n, c).wait()
    for copy in sent_weights():
        copy.wait_send()
    for n in range(3):
        sent_prm(n).wait_send()
    for n in range(2):
        sent_sums(n).wait_send()
    give.wait()
    keep.wait()


def middle(att, post, pre, post_cot, pre_cot, own, across, prm):
    rows, width = post.shape
    local = att.shape[1]
    up, down, out = own
    hid = up.shape[1]
    count = rows // TILE
    tall = width + hid + local
    f32 = jax.ShapeDtypeStruct((rows, width), F32)
    return pl.pallas_call(
        middle_kernel,
        out_shape=(
            f32, f32, f32,
            jax.ShapeDtypeStruct(att.shape, BF16),
            jax.ShapeDtypeStruct((tall, width), F32),
            jax.ShapeDtypeStruct((tall, width), BF16),
            jax.ShapeDtypeStruct((16, width), F32),
        ),
        in_specs=[ANY] * 11 + [VMEM],
        out_specs=(ANY,) * 6 + (VMEM,),
        scratch_shapes=[
            pltpu.VMEM((rows, width), F32),
            pltpu.VMEM((rows, width), F32),
            pltpu.VMEM((rows, width), F32),
            pltpu.VMEM((rows, width), F32),
            pltpu.VMEM((rows, MP * local), BF16),
            pltpu.VMEM((MP, width, hid), BF16),
            pltpu.VMEM((MP, hid, width), BF16),
            pltpu.VMEM((MP * local, width), BF16),
            pltpu.VMEM((MP,) + prm.shape, F32),
            pltpu.VMEM((rows, width), BF16),
            pltpu.VMEM((MP, rows, hid), BF16),
            pltpu.VMEM((MP, rows, hid), BF16),
            pltpu.VMEM((rows, width), BF16),
            pltpu.VMEM((rows, width), BF16),
            pltpu.VMEM((rows, MP * local), BF16),
            pltpu.VMEM((MP, TILE, hid), F32),
            pltpu.VMEM((rows, width), F32),
            pltpu.VMEM((rows, width), F32),
            pltpu.VMEM((rows, width), F32),
            pltpu.VMEM((2, tall, width), BF16),
            pltpu.VMEM((2, tall, width), BF16),
            pltpu.VMEM((tall, width), F32),
            pltpu.VMEM((tall, width), BF16),
            dma_sems(count, 4), dma_sems(3), dma_sems(2, 3), dma_sems(2, 3), dma_sems(2, 3),
            dma_sems(3), dma_sems(3), dma_sems(3, count), dma_sems(3, count),
            dma_sems(3, count), dma_sems(3, count), dma_sems(2), dma_sems(2), dma_sems(count, 4),
        ],
        compiler_params=pltpu.CompilerParams(
            collective_id=1, has_side_effects=True, vmem_limit_bytes=60 << 20
        ),
        cost_estimate=pl.CostEstimate(flops=15 << 30, bytes_accessed=20 << 20, transcendentals=4 << 20),
        name="middle",
    )(att, post, pre, post_cot, pre_cot, up, down, out, *across, prm)


def tail_kernel(
    dp_size,
    dq, dk, dv, tok_t, w, sum1, keep, given, small,
    post_out, qkv_out, up_out, down_out, out_out, small_out,
    grads, tok_b, sum1_b, given_b, mine, far, send_far, recv_far, pass_far, land_far, send_near, recv_near,
    acc, flight, full, land, small_flight, small_land,
    in_sem, near_send, near_recv, far_send, far_recv, hop_send, hop_recv,
    step_send, step_recv, small_send, small_recv, out_sem,
):
    me, sib, across, diagonal = mp_peers()
    dp = lax.axis_index("dp")
    rows, width = sum1.shape
    local = dq.shape[1]
    chunk = TILE
    count = rows // chunk
    hid = up_out.shape[1]
    bits = dp_size.bit_length() - 1
    partners = [dp + (1 << b) - 2 * (1 << b) * ((dp // (1 << b)) % 2) for b in range(bits)]
    upper = [(dp // (1 << b)) % 2 for b in range(bits)]

    loads = [
        pltpu.make_async_copy(src, grads.at[n], in_sem.at[n]) for n, src in enumerate((dq, dk, dv))
    ] + [
        pltpu.make_async_copy(tok_t, tok_b, in_sem.at[3]),
        pltpu.make_async_copy(sum1, sum1_b, in_sem.at[4]),
        pltpu.make_async_copy(keep, acc.at[pl.ds(0, keep.shape[0])], in_sem.at[5]),
        pltpu.make_async_copy(given, given_b, in_sem.at[6]),
    ]
    for load in loads:
        load.start()
    greet([(dp, sib), (dp, across)] + [(p, me) for p in partners])

    pieces = ((0, width), (width, hid), (width + hid, local), (width + hid + local, 3 * width // 4))

    def plan(piece):
        start, size = piece
        sizes = []
        for b in range(bits):
            halved = size % 32 == 0
            sizes.append((b, size, halved))
            if halved:
                size //= 2
        return sizes

    offsets = {}
    for n, piece in enumerate(pieces):
        base = jnp.int32(piece[0])
        for b, size, halved in plan(piece):
            if halved:
                half = size // 2
                offsets[n, b] = (base + (1 - upper[b]) * half, base + upper[b] * half, half)
                base = base + upper[b] * half
            else:
                offsets[n, b] = (base, base, size)

    def reduce_copy(n, b):
        given_at, kept_at, size = offsets[n, b]
        return remote(
            flight.at[ds16(given_at, size)], land.at[b, ds16(given_at, size)],
            step_send.at[0, n, b], step_recv.at[0, n, b], (partners[b], me),
        )

    def reduce_start(n, b):
        given_at, kept_at, size = offsets[n, b]
        here = ds16(given_at, size)
        flight[here] = acc[here].astype(BF16)
        reduce_copy(n, b).start()

    def reduce_finish(n, b):
        given_at, kept_at, size = offsets[n, b]
        copy = reduce_copy(n, b)
        copy.wait_recv()
        here = ds16(kept_at, size)
        if plan(pieces[n])[b][2]:
            acc[here] = acc[here] + land[b, here].astype(F32)
        else:
            acc[here] = flight[here].astype(F32) + land[b, here].astype(F32)
        copy.wait_send()

    def spread_copy(n, b):
        given_at, kept_at, size = offsets[n, b]
        here = ds16(kept_at, size)
        return remote(full.at[here], full.at[here], step_send.at[1, n, b], step_recv.at[1, n, b], (partners[b], me))

    def spread_done(n, b):
        given_at, kept_at, size = offsets[n, b]
        there = ds16(given_at, size)
        copy = pltpu.make_async_copy(full.at[there], full.at[there], step_recv.at[1, n, b])
        copy.wait()

    def stage(n, t):
        if t <= bits:
            if t > 0:
                reduce_finish(n, t - 1)
            if t < bits:
                reduce_start(n, t)
                return
            _, kept_at, size = offsets[n, bits - 1]
            here = ds16(kept_at, size)
            full[here] = acc[here].astype(BF16)
            t = bits
        order = [b for b in range(bits - 1, -1, -1) if plan(pieces[n])[b][2]]
        k = t - bits
        if k > 0:
            spread_done(n, order[k - 1])
            spread_copy(n, order[k - 1]).wait_send()
        if k < len(order):
            spread_copy(n, order[k]).start()

    def last_stage(n):
        return bits + sum(1 for _, _, halved in plan(pieces[n]) if halved)

    small_peers = [(dp, sib), (dp, across)] + [(p, me) for p in partners]

    def small_copy(s):
        return remote(small_flight.at[s], small_land.at[s], small_send.at[s], small_recv.at[s], small_peers[s])

    def small_stage(s):
        if s > 0:
            small_copy(s - 1).wait()
            small_out[...] = small_out[...] + small_land[s - 1]
        if s < len(small_peers):
            small_flight[s] = small_out[...]
            small_copy(s).start()

    def part(owner, c):
        here = ds(owner * rows + c * chunk, chunk)
        return (
            dot(grads[0, here], w[0], NT) + dot(grads[1, here], w[1], NT) + dot(grads[2, here], w[2], NT)
        )

    def far_copy(c):
        return remote(send_far.at[c], recv_far.at[c], far_send.at[c], far_recv.at[c], (dp, sib))

    def hop_copy(c):
        return remote(pass_far.at[c], land_far.at[c], hop_send.at[c], hop_recv.at[c], (dp, across))

    def near_copy(c):
        return remote(send_near.at[c], recv_near.at[c], near_send.at[c], near_recv.at[c], (dp, sib))

    loads[5].wait()
    loads[6].wait()
    own = pl.ds(0, given_b.shape[0])
    acc[own] = acc[own] + given_b[...].astype(F32)
    stage(0, 0)
    for n in range(3):
        loads[n].wait()

    def far_step(c, _):
        send_far[c] = part(diagonal, c).astype(BF16)
        far_copy(c).start()
        far[c] = part(across, c)
        return 0

    def hop_step(c, _):
        far_copy(c).wait_recv()
        pass_far[c] = (far[c] + recv_far[c].astype(F32)).astype(BF16)
        hop_copy(c).start()
        return 0

    def near_step(c, _):
        send_near[c] = part(sib, c).astype(BF16)
        near_copy(c).start()
        mine[c] = part(me, c)
        return 0

    lax.fori_loop(0, count, far_step, 0)
    stage(1, 0)
    lax.fori_loop(0, count, hop_step, 0)
    stage(2, 0)
    lax.fori_loop(0, count, near_step, 0)
    small_out[...] = small[...]
    query_sum = column_sum(grads[0].astype(F32))
    value_sum = column_sum(grads[2].astype(F32))
    small_out[ds1(12 + me), :] = jnp.concatenate(
        [query_sum, value_sum, jnp.zeros((1, width - 2 * local), F32)], axis=1
    )
    small_stage(0)
    loads[3].wait()
    base = pieces[3][0]
    third = width // 4
    for n in range(3):
        block = dot(tok_b[...], grads[n])
        for s in range(4):
            acc[pl.ds(base + n * third, third), pl.ds(s * local, local)] = block[s * third : (s + 1) * third]
    stage(3, 0)

    last = max(last_stage(n) for n in range(len(pieces)))
    for t in range(1, last + 1):
        for n in range(len(pieces)):
            if t <= last_stage(n):
                stage(n, t)
        if t <= len(small_peers):
            small_stage(t)
        if t == last // 2:
            loads[4].wait()
            for c in range(count):
                near_copy(c).wait()
                mine[c] = mine[c] + recv_near[c].astype(F32)
    for t in range(last + 1, len(small_peers) + 1):
        small_stage(t)

    outs = []
    up_out[...] = full[pl.ds(0, width)].astype(F32)
    down_out[...] = full[pl.ds(width, hid)].astype(F32)
    out_out[...] = full[pl.ds(width + hid, local)].astype(F32)
    for n in range(3):
        for s in range(4):
            qkv_out[n, pl.ds(s * third, third)] = full[
                pl.ds(base + n * third, third), pl.ds(s * local, local)
            ].astype(F32)
    for c in range(count):
        far_copy(c).wait_send()
        hop_copy(c).wait()
        here = pl.ds(c * chunk, chunk)
        sum1_b[here] = sum1_b[here] + mine[c] + land_far[c].astype(F32)
        out = pltpu.make_async_copy(sum1_b.at[here], post_out.at[here], out_sem.at[c])
        out.start()
        outs.append(out)
    for out in outs:
        out.wait()


def ds16(start, size):
    return pl.ds(pl.multiple_of(start, 16), size)


def ds1(start):
    return pl.ds(start, 1)


def tail(dp_size, dq, dk, dv, tok_t, w, sum1, keep, given, small):
    rows, width = sum1.shape
    group, local = dq.shape
    tall = keep.shape[0]
    hid = tall - width - local
    count = rows // TILE
    bits = dp_size.bit_length() - 1
    assert 1 << bits == dp_size
    total = tall + 3 * width // 4
    blocks = (count, TILE, width)
    steps = bits + 2
    return pl.pallas_call(
        functools.partial(tail_kernel, dp_size),
        out_shape=(
            jax.ShapeDtypeStruct((rows, width), F32),
            jax.ShapeDtypeStruct((3, width, local), F32),
            jax.ShapeDtypeStruct((width, hid), F32),
            jax.ShapeDtypeStruct((hid, width), F32),
            jax.ShapeDtypeStruct((local, width), F32),
            jax.ShapeDtypeStruct(small.shape, F32),
        ),
        in_specs=[ANY] * 4 + [VMEM] + [ANY] * 3 + [VMEM],
        out_specs=(ANY,) + (VMEM,) * 5,
        scratch_shapes=[
            pltpu.VMEM((3, group, local), BF16),
            pltpu.VMEM((width, group), BF16),
            pltpu.VMEM((rows, width), F32),
            pltpu.VMEM((tall, width), BF16),
            pltpu.VMEM(blocks, F32),
            pltpu.VMEM(blocks, F32),
            pltpu.VMEM(blocks, BF16),
            pltpu.VMEM(blocks, BF16),
            pltpu.VMEM(blocks, BF16),
            pltpu.VMEM(blocks, BF16),
            pltpu.VMEM(blocks, BF16),
            pltpu.VMEM(blocks, BF16),
            pltpu.VMEM((total, width), F32),
            pltpu.VMEM((total, width), BF16),
            pltpu.VMEM((total, width), BF16),
            pltpu.VMEM((bits, total, width), BF16),
            pltpu.VMEM((steps,) + small.shape, F32),
            pltpu.VMEM((steps,) + small.shape, F32),
            dma_sems(7), dma_sems(count), dma_sems(count), dma_sems(count), dma_sems(count),
            dma_sems(count), dma_sems(count), dma_sems(2, 4, bits), dma_sems(2, 4, bits),
            dma_sems(steps), dma_sems(steps), dma_sems(count),
        ],
        compiler_params=pltpu.CompilerParams(
            collective_id=2, has_side_effects=True, vmem_limit_bytes=60 << 20
        ),
        cost_estimate=pl.CostEstimate(flops=4 << 30, bytes_accessed=20 << 20, transcendentals=0),
        name="tail",
    )(dq, dk, dv, tok_t, w, sum1, keep, given, small)


def body(
    dp_size,
    post_stream,
    pre_stream,
    seq_lengths,
    qkv_weight,
    query_bias,
    value_bias,
    out_weight,
    out_bias,
    norm1_gain,
    norm1_shift,
    up_weight,
    up_bias,
    down_weight,
    down_bias,
    norm2_gain,
    norm2_shift,
    post_cotan,
    pre_cotan,
):
    local = out_weight.shape[0]
    lengths = seq_lengths[0]
    qkv3 = jnp.transpose(qkv_weight, (1, 0, 2))
    pad = jnp.zeros_like(query_bias)
    prm = jnp.stack(
        [
            jnp.concatenate([query_bias, pad, value_bias, pad]),
            out_bias, norm1_gain, norm1_shift, down_bias, norm2_gain, norm2_shift, up_bias,
        ]
    ).astype(F32)
    tok_t, q, k, v, kt, vt = gather_and_project(post_stream, qkv3, prm)
    across = [(m, (m + 2) % MP) for m in range(MP)]
    own = (up_weight, down_weight, out_weight)
    own, _ = lax.optimization_barrier((own, tok_t))
    far = [lax.ppermute(part, "mp", across) for part in own]
    att, lse = attend(lengths, q, k, vt)
    post_out, pre_out, sum1, att_grad, keep, give, small = middle(
        att, post_stream, pre_stream, post_cotan, pre_cotan, own, far, prm
    )
    given = lax.ppermute(give, "mp", across)
    dq, dk, dv = attend_back(lengths, q, k, v, kt, att, lse, att_grad)
    post_grad, qkv_grad, up_grad, down_grad, out_grad, small = tail(
        dp_size, dq, dk, dv, tok_t, qkv3, sum1, keep, given, small
    )
    me = lax.axis_index("mp")
    own_row = lax.dynamic_slice_in_dim(small, 12 + me, 1, 0)[0]
    return (
        post_out,
        pre_out,
        post_grad,
        jnp.transpose(qkv_grad, (1, 0, 2)),
        own_row[:local],
        own_row[local : 2 * local],
        out_grad,
        small[0],
        small[1],
        small[2],
        up_grad,
        lax.dynamic_slice_in_dim(small, 8 + me, 1, 0)[0],
        down_grad,
        small[3],
        small[4],
        small[5],
    )


def solution(mesh):
    tokens = P(("dp", "mp"), None)
    vector = P()
    return jax.shard_map(
        functools.partial(body, mesh.shape["dp"]),
        mesh=mesh,
        in_specs=(
            tokens, tokens, P("dp", None), P(None, None, "mp"), P("mp"), P("mp"), P("mp", None),
            vector, vector, vector, P(None, "mp"), P("mp"), P("mp", None), vector, vector, vector,
            tokens, tokens,
        ),
        out_specs=(
            tokens, tokens, tokens, P(None, None, "mp"), P("mp"), P("mp"), P("mp", None),
            vector, vector, vector, P(None, "mp"), P("mp"), P("mp", None), vector, vector, vector,
        ),
        check_vma=False,
    )
```

time: 1400 us -> 256 us (0.18)
  matrix products: 496 us -> 0 us
  waiting for transfers between devices: 475 us -> 0.01 us
  Pallas kernels: 0 us -> 220 us
  other arithmetic: 189 us -> 0.69 us
  local copies, waits for them, and re-layouts: 120 us -> 29.3 us
  blocking collectives: 62.1 us -> 0 us
  loops' own time: 32 us -> 0 us
  between operations: 14.9 us -> 0.81 us
    dot_general x52 -> x0, matrix products: 327 us -> none  [the longest x8 76.3 us: one_block(): jnp.einsum('hqk,qhd->khd', attention_low, grad_block, preferred_element_t...]
    pallas_call x0 -> x5, Pallas kernels: none -> 220 us  [the longest x1 67.4 us: tail(): pl.pallas_call(functools.partial(tail_kernel, dp_size), out_shape=(jax.Sh...]
    reduce_scatter x4 -> x0, waiting for transfers between devices: 214 us -> none  [the longest x1 71.2 us: body(): lax.psum_scatter(jnp.einsum('tf,df->td', rows_part, up_weight, preferred_...]
    sub x16 -> x0, matrix products: 169 us -> none  [block_probs(): return jax.nn.softmax(jnp.where(allowed[None], raw, MASKED), axis=-1)]
    all_gather x4 -> x0, waiting for transfers between devices: 139 us -> none  [the longest x1 35.5 us: body(): tokens_all = lax.all_gather(post_low, 'mp', axis=0, tiled=True)]
    psum x1 -> x0, waiting for transfers between devices: 123 us -> none  [body(): lax.psum((qkv_weight_grad, query_bias_grad, value_bias_grad, out_weight_g...]
    convert_element_type x18 -> x1, other arithmetic: 101 us -> 0.01 us  [body(): prm = jnp.stack([jnp.concatenate([query_bias, pad, value_bias, pad]), out...]
    psum x2 -> x0, blocking collectives: 62.1 us -> none  [the longest x1 40 us: body(): lax.psum((out_bias_grad, gain1_grad, shift1_grad, down_bias_grad, gain2_g...]
  transfers between devices with their start and end apart: 9 -> 4, of which waited for: 8 -> 0; matrix products, arithmetic and copies ran while one was open for 2% -> 0% of each run, Pallas kernels for 0% -> 35%
where the time goes in v1:
time: 256 us; the launch traced here: 255 us
  Pallas kernels  220 us (86%)
  local copies, waits for them, and re-layouts  29.3 us (11%)
  starting transfers between devices  4.19 us (2%)
    pallas_call x1, Pallas kernels, tail(): pl.pallas_call(functools.partial(tail_kernel, dp_size), out_shape=(jax.Sh...  67.4 us
    pallas_call x1, Pallas kernels, attend(): pl.pallas_call(attend_kernel, grid_spec=pltpu.PrefetchScalarGridSpec(num_...  46 us
    pallas_call x1, Pallas kernels, attend_back(): pl.pallas_call(attend_back_kernel, grid_spec=pltpu.PrefetchScalarGridSpec...  42.5 us
    pallas_call x1, Pallas kernels, middle(): pl.pallas_call(middle_kernel, out_shape=(f32, f32, f32, jax.ShapeDtypeStr...  35 us
    pallas_call x1, Pallas kernels, gather_and_project(): pl.pallas_call(project_kernel, out_shape=(jax.ShapeDtypeStruct((width, gr...  29.5 us
    unnamed x53, local copies, waits for them, and re-layouts  21.7 us
  transfers between devices with their start and end apart: 4, of which 0 were waited for; matrix products, arithmetic and copies ran while one was open for 0% of the time, Pallas kernels for 35%

profile of v1, /device:TPU:0, one launch (start us, length us, event | category | flops | bytes accessed | tf_op | source)
XLA Modules:
  0.0 255.4 jit_solution(16250231611420092670)
XLA Ops:
  6.2 1.6 copy-done.1
  7.8 1.0 copy-done.2
  8.8 29.5 %gather_project.1 = (bf16[512,4096]{1,0:T(8,128)(2,1)S(1)}, bf16[4096,128]{1,0:T(8,128)(2,1)S(1)}, bf16[4096,128]{1,0:T(8,128)(2,1)S(1)}, bf16[4096,128]{1,0:T(8...) custom-call(f32[1024,512]{1,0:T(8,128)S(1)} %copy-done.1, ...), custom_call_target="tpu_custom_call" | custom-call | flops 1610612736 | bytes 12582912 | tf_op jit(solution)/shard_map/gather_project/pallas_call | solution.py:179
  38.9 1.5 collective-permute-start.1
  41.0 46.0 %attend.1 = (bf16[4096,128]{1,0:T(8,128)(2,1)S(1)}, f32[16,8,256]{2,1,0:T(8,128)S(1)}) custom-call(s32[13]{0:T(128)S(1)} %bitcast.16, bf16[4096,128]{1,0:T(8,128)(2,1)S(1)} %get-tuple-element.43.q_ref, bf16[4096,128]{1,0:T(8,128)(2,1)S(1)} %get-tuple-element.44.k_ref, bf16[128,4096]{1,0:T(8,128)(2,1)S(1)} %get-tuple-element.45.vt_ref), custom_call_target="tpu_custom_call" | custom-call | flops 12884901888 | bytes 4194304 | tf_op jit(solution)/shard_map/attend/pallas_call | solution.py:268
  88.6 35.0 %middle.1 = (f32[1024,512]{1,0:T(8,128)}, f32[1024,512]{1,0:T(8,128)}, f32[1024,512]{1,0:T(8,128)}, bf16[4096,128]{1,0:T(8,128)(2,1)}, f32[1152,512]{1,0:T(8,128...) custom-call(bf16[4096,128]{1,0:T(8,128)(2,1)} %copy-done.10, f32[1024,512]{1,0:T(8,128)} %post.3, f32[1024,512]{1,0:T(8,128)} %pre.1, ...), custom_call_target="tpu_custom_call" | custom-call | flops 16106127360 | bytes 20971520 | tf_op jit(solution)/shard_map/middle/pallas_call | solution.py:647
  123.6 1.5 collective-permute-start.3
  125.1 1.2 copy-done.9
  126.4 1.2 copy-done.11
  127.6 1.2 copy-done.12
  128.8 42.5 %attend_back.1 = (bf16[4096,128]{1,0:T(8,128)(2,1)S(1)}, bf16[4096,128]{1,0:T(8,128)(2,1)S(1)}, bf16[4096,128]{1,0:T(8,128)(2,1)S(1)}) custom-call(s32[13]{0:T(128)S(1)} %bitcast.17, bf16[4096,128]{1,0:T(8,128)(2,1)S(1)} %get-tuple-element.43.q_ref, bf16[4096,128]{1,0:T(8,128)(2,1)S(1)} %copy-done.12, bf16[4096,128]{1,0:T(8,128)(2,1)S(1)} %copy-done.11, ...), custom_call_target="tpu_custom_call" | custom-call | flops 32212254720 | bytes 9437184 | tf_op jit(solution)/shard_map/attend_back/pallas_call | solution.py:361
  172.3 1.0 copy-done.6
  173.2 1.0 copy-done.7
  174.2 1.0 copy-done.20
  175.2 67.4 %tail.1 = (f32[1024,512]{1,0:T(8,128)}, f32[3,512,128]{2,1,0:T(8,128)}, f32[512,512]{1,0:T(8,128)}, f32[512,512]{1,0:T(8,128)}, f32[128,512]{1,0:T(8,128)}, /*index=5*/f32[16,512]{1,0:T(8,128)}) custom-call(bf16[4096,128]{1,0:T(8,128)(2,1)} %copy-done.5, bf16[4096,128]{1,0:T(8,128)(2,1)} %copy-done.6, bf16[4096,128]{1,0:T(8,128)(2,1)} %copy-done.7, ...), custom_call_target="tpu_custom_call" | custom-call | flops 4294967296 | bytes 20971520 | tf_op jit(solution)/shard_map/tail/pallas_call | solution.py:936
  242.6 1.6 fusion
  244.2 1.3 dynamic-slice_bitcast_fusion
  245.5 1.3 copy.41
  246.8 1.0 copy-done.13
  247.8 1.3 copy.42
  249.1 1.0 copy-done.15
  250.2 1.3 copy.43
  253.4 1.0 copy.46
  254.4 1.0 copy.47
  (56 shorter events, 11.2 us)
Async XLA Ops:
  6.2 32.1 %copy-start = (f32[8,512]{1,0:T(8,128)}, f32[8,512]{1,0:T(8,128)S(1)}, u32[]{:S(2)}) copy-start(f32[8,512]{1,0:T(8,128)S(1)} %convert_element_type.3.prm) | copy-start | bytes 49156
  6.2 1.6 copy-start.1
  7.8 1.0 copy-start.2
  8.8 31.6 %copy-start.21 = (bf16[128,512]{1,0:T(8,128)(2,1)S(1)}, bf16[128,512]{1,0:T(8,128)(2,1)}, u32[]{:S(2)}) copy-start(bf16[128,512]{1,0:T(8,128)(2,1)} %out_own) | copy-start | bytes 393220
  8.8 32.2 %copy-start.3 = (s32[1,13]{1,0:T(1,128)S(1)}, s32[1,13]{1,0:T(1,128)}, u32[]{:S(2)}) copy-start(s32[1,13]{1,0:T(1,128)} %param.20) | copy-start | bytes 160
  38.3 48.6 %copy-start.4 = (bf16[512,4096]{1,0:T(8,128)(2,1)}, bf16[512,4096]{1,0:T(8,128)(2,1)S(1)}, u32[]{:S(2)}) copy-start(bf16[512,4096]{1,0:T(8,128)(2,1)S(1)} %get-tuple-element.47.tok_t) | copy-start | bytes 12582916
  38.3 48.6 %copy-start.8 = (bf16[128,4096]{1,0:T(8,128)(2,1)}, bf16[128,4096]{1,0:T(8,128)(2,1)S(1)}, u32[]{:S(2)}) copy-start(bf16[128,4096]{1,0:T(8,128)(2,1)S(1)} %get-tuple-element.56.kt_ref) | copy-start | bytes 3145732
  38.3 49.6 %collective-permute-start = (bf16[512,512]{1,0:T(8,128)(2,1)}, bf16[512,512]{1,0:T(8,128)(2,1)}, u32[]{:S(2)}, u32[]{:S(2)}) collective-permute-start(bf16[512,512]{1,0:T(8,128)(2,1)} %up_own), channel_id=1, source_target_pairs={{0,2},{1,3},{2,0},{3,1},{4,6},{5,7},{6,4},{7,5},{8,10},{9,11},{10,... | collective-permute-start | bytes 1572872 | tf_op jit(solution)/shard_map/ppermute | solution.py:1014
  38.9 49.0 %collective-permute-start.1 = (bf16[512,512]{1,0:T(8,128)(2,1)}, bf16[512,512]{1,0:T(8,128)(2,1)}, u32[]{:S(2)}, u32[]{:S(2)}) collective-permute-start(bf16[512,512]{1,0:T(8,128)(2,1)} %down_own), channel_id=1, source_target_pairs={{0,2},{1,3},{2,0},{3,1},{4,6},{5,7},{6,4},{7,5},{8,10},{9,11},{10,... | collective-permute-start | bytes 1572872 | tf_op jit(solution)/shard_map/ppermute | solution.py:1014
  40.4 47.5 %collective-permute-start.2 = (bf16[128,512]{1,0:T(8,128)(2,1)S(1)}, bf16[128,512]{1,0:T(8,128)(2,1)S(1)}, u32[]{:S(2)}, u32[]{:S(2)}) collective-permute-start(bf16[128,512]{1,0:T(8,128)(2,1)S(1)} %copy-done.21), channel_id=1, source_target_pairs={{0,2},{1,3},{2,0},{3,1},{4,6},{5,7},{6,4},{7,5},{8,10},{9,11},{10,... | collective-permute-start | bytes 393224 | tf_op jit(solution)/shard_map/ppermute | solution.py:1014
  87.0 1.0 copy-start.10
  123.6 50.6 %collective-permute-start.3 = (bf16[1152,512]{1,0:T(8,128)(2,1)}, bf16[1152,512]{1,0:T(8,128)(2,1)S(1)}, u32[]{:S(2)}, u32[]{:S(2)}) collective-permute-start(bf16[1152,512]{1,0:T(8,128)(2,1)} %get-tuple-element.62), channel_id=1, source_target_pairs={{0,2},{1,3},{2,0},{3,1},{4,6},{5,7},{6,4},{7,5},{8,10},{9,11},{10,... | collective-permute-start | bytes 3538952 | tf_op jit(solution)/shard_map/ppermute | solution.py:1019
  125.1 1.2 copy-start.9
  126.4 1.2 copy-start.11
  127.6 1.2 copy-start.12
  171.3 1.0 copy-start.5
  174.2 1.0 copy-start.20
  175.2 70.2 %copy-start.14 = (f32[1024,512]{1,0:T(8,128)S(1)}, f32[1024,512]{1,0:T(8,128)}, u32[]{:S(2)}) copy-start(f32[1024,512]{1,0:T(8,128)} %get-tuple-element.95) | copy-start | bytes 6291460
  245.4 2.3 copy-start.13
  247.8 2.3 copy-start.15
  250.1 1.7 copy-start.18
  250.1 2.6 %copy-start.19 = (f32[128,512]{1,0:T(8,128)S(1)}, f32[128,512]{1,0:T(8,128)}, u32[]{:S(2)}) copy-start(f32[128,512]{1,0:T(8,128)} %get-tuple-element.101) | copy-start | bytes 786436
  251.8 1.6 copy-start.17
  251.8 2.6 %copy-start.16 = (f32[512,512]{1,0:T(8,128)S(1)}, f32[512,512]{1,0:T(8,128)}, u32[]{:S(2)}) copy-start(f32[512,512]{1,0:T(8,128)} %get-tuple-element.107) | copy-start | bytes 3145732
  (3 other events, 2.6 us)

commit v2 on v1

v2 whole, which is shorter than its diff:
```python
import functools

import jax
import jax.numpy as jnp
from jax import lax
from jax.experimental import pallas as pl
from jax.experimental.pallas import tpu as pltpu
from jax.sharding import PartitionSpec as P

HEAD_DIM = 64
EPSILON = 1e-05
MASKED = -1e30
MP = 4
TILE = 256
MESH = pl.DeviceIdType.MESH
BF16 = jnp.bfloat16
F32 = jnp.float32
ANY = pl.BlockSpec(memory_space=pl.ANY)
VMEM = pl.BlockSpec(memory_space=pltpu.VMEM)
SMEM = pl.BlockSpec(memory_space=pltpu.SMEM)
NT = (((1,), (1,)), ((), ()))
TN = (((0,), (0,)), ((), ()))
SQRT_2_OVER_PI = 0.7978845608028654


def ds(start, size):
    return pl.ds(pl.multiple_of(start, size), size)


def mp_peers():
    me = lax.axis_index("mp")
    sib = me + 1 - 2 * (me % 2)
    across = (me + 2) % MP
    diagonal = (sib + 2) % MP
    return me, sib, across, diagonal


def greet(devices):
    barrier = pltpu.get_barrier_semaphore()
    for device in devices:
        pl.semaphore_signal(barrier, inc=1, device_id=device, device_id_type=MESH)
    pl.semaphore_wait(barrier, len(devices))


def remote(src, dst, send_sem, recv_sem, device):
    return pltpu.make_async_remote_copy(
        src_ref=src,
        dst_ref=dst,
        send_sem=send_sem,
        recv_sem=recv_sem,
        device_id=device,
        device_id_type=MESH,
    )


def dot(a, b, dims=(((1,), (0,)), ((), ()))):
    return lax.dot_general(a, b, dims, preferred_element_type=F32)


def column_sum(block):
    return jnp.sum(block, axis=0, keepdims=True)


def as_row(vector):
    return vector[...].astype(F32).reshape(1, vector.shape[0])


def dma_sems(*shape):
    return pltpu.SemaphoreType.DMA(shape)


def first_of_segment(bounds, place):
    start = jnp.zeros_like(place)
    for bound in bounds:
        start = jnp.where(place >= bound, bound, start)
    return jnp.where(place >= bounds[-1], place, start)


def head_masked(block, h):
    lane = lax.broadcasted_iota(jnp.int32, block.shape, 1)
    return jnp.where((lane >= h * HEAD_DIM) & (lane < (h + 1) * HEAD_DIM), block, jnp.zeros_like(block))


def project_kernel(
    lengths, post, w_any, query_bias_ref, value_bias_ref, up, down, out,
    tok_t_out, q_out, k_out, v_out, kt_out, vt_out, starts, limits, own_out,
    stage, w, own_b, tok, tok_t, q_s, k_s, v_s, kt_s, vt_s,
    w_sem, in_sem, send_x, recv_x, send_c, recv_c, send_f, recv_f, out_sem,
):
    me, sib, across, diagonal = mp_peers()
    dp = lax.axis_index("dp")
    rows = post.shape[0]
    width = post.shape[1]
    chunk = TILE
    count = rows // chunk
    heads = w.shape[2] // HEAD_DIM
    hid = up.shape[1]
    packs = []
    for n, (src, start) in enumerate(((up, 0), (down, width), (out, width + hid))):
        packs.append(pltpu.make_async_copy(src, own_b.at[pl.ds(start, src.shape[0])], w_sem.at[1 + n]))
    packed = pltpu.make_async_copy(own_b, own_out, w_sem.at[4])
    w_load = pltpu.make_async_copy(w_any, w, w_sem.at[0])
    loads = [
        pltpu.make_async_copy(post.at[pl.ds(c * chunk, chunk)], stage.at[pl.ds(c * chunk, chunk)], in_sem.at[c])
        for c in range(count)
    ]
    for load in loads + [w_load] + packs:
        load.start()
    greet([(dp, sib), (dp, across)])

    def piece(owner, c):
        return ds(owner * rows + c * chunk, chunk)

    def to_across(c):
        here = piece(me, c)
        return remote(tok.at[here], tok.at[here], send_x.at[c], recv_x.at[c], (dp, across))

    def to_sibling(c):
        here = piece(me, c)
        return remote(tok.at[here], tok.at[here], send_c.at[c], recv_c.at[c], (dp, sib))

    def forward(c):
        here = piece(across, c)
        return remote(tok.at[here], tok.at[here], send_f.at[c], recv_f.at[c], (dp, sib))

    def arrived(owner, sem, c):
        here = piece(owner, c)
        return pltpu.make_async_copy(tok.at[here], tok.at[here], sem.at[c])

    for c in range(count):
        loads[c].wait()
        tok[piece(me, c)] = stage[pl.ds(c * chunk, chunk)].astype(BF16)
        to_across(c).start()
        to_sibling(c).start()

    query_bias = as_row(query_bias_ref)
    value_bias = as_row(value_bias_ref)

    def project(owner, c):
        here = piece(owner, c)
        block = tok[here]
        tok_t[:, here] = block.T
        query = (dot(block, w[0]) + query_bias).astype(BF16)
        query = (query.astype(F32) * HEAD_DIM ** (-0.5)).astype(BF16)
        for h in range(heads):
            q_s[owner * count + c, pl.ds(h * TILE, TILE)] = head_masked(query, h)
        keys = dot(block, w[1]).astype(BF16)
        k_s[here] = keys
        kt_s[:, here] = keys.T
        values = (dot(block, w[2]) + value_bias).astype(BF16)
        v_s[here] = values
        vt_s[:, here] = values.T

    def outs(g, owner):
        here = ds(owner * rows, rows)
        return [
            pltpu.make_async_copy(tok_t.at[:, here], tok_t_out.at[:, here], out_sem.at[g, 0]),
            pltpu.make_async_copy(
                q_s.at[pl.ds(owner * count, count)], q_out.at[pl.ds(owner * count, count)], out_sem.at[g, 1]
            ),
            pltpu.make_async_copy(k_s.at[here], k_out.at[here], out_sem.at[g, 2]),
            pltpu.make_async_copy(v_s.at[here], v_out.at[here], out_sem.at[g, 3]),
            pltpu.make_async_copy(kt_s.at[:, here], kt_out.at[:, here], out_sem.at[g, 4]),
            pltpu.make_async_copy(vt_s.at[:, here], vt_out.at[:, here], out_sem.at[g, 5]),
        ]

    w_load.wait()
    bounds = [lengths[0, 0]]
    for s in range(1, lengths.shape[1] - 1):
        bounds.append(bounds[-1] + lengths[0, s])
    for i in range(starts.shape[0]):
        place = i * TILE + lax.broadcasted_iota(jnp.int32, (1, starts.shape[2]), 1) % TILE
        starts[i] = jnp.broadcast_to(first_of_segment(bounds, place), starts.shape[1:])
        limits[0, i] = first_of_segment(bounds, jnp.int32(i * TILE)) // TILE
        last = first_of_segment(bounds, jnp.int32(i * TILE + TILE - 1))
        limits[1, i] = jnp.minimum((last + TILE - 1) // TILE, i)

    def own_step(c, _):
        project(me, c)
        return 0

    lax.fori_loop(0, count, own_step, 0)
    for copy in outs(0, me):
        copy.start()
    for pack in packs:
        pack.wait()
    packed.start()

    def sibling_step(c, _):
        arrived(sib, recv_c, c).wait()
        project(sib, c)
        return 0

    lax.fori_loop(0, count, sibling_step, 0)
    for copy in outs(1, sib):
        copy.start()

    def across_step(c, _):
        arrived(across, recv_x, c).wait()
        forward(c).start()
        project(across, c)
        arrived(diagonal, recv_f, c).wait()
        project(diagonal, c)
        return 0

    lax.fori_loop(0, count, across_step, 0)
    for copy in outs(2, across) + outs(3, diagonal):
        copy.start()
    for c in range(count):
        to_across(c).wait_send()
        to_sibling(c).wait_send()
        forward(c).wait_send()
    for g, owner in enumerate((me, sib, across, diagonal)):
        for copy in outs(g, owner):
            copy.wait()
    packed.wait()


def gather_and_project(lengths, post_stream, qkv3, query_bias, value_bias, own):
    rows, width = post_stream.shape
    group = rows * MP
    local = qkv3.shape[2]
    count = rows // TILE
    tall = jax.ShapeDtypeStruct((group, local), BF16)
    wide = jax.ShapeDtypeStruct((local, group), BF16)
    blocks = group // TILE
    across = TILE * (local // HEAD_DIM)
    return pl.pallas_call(
        project_kernel,
        out_shape=(
            jax.ShapeDtypeStruct((width, group), BF16),
            jax.ShapeDtypeStruct((blocks, across, local), BF16),
            tall, tall, wide, wide,
            jax.ShapeDtypeStruct((blocks, 8, across), jnp.int32),
            jax.ShapeDtypeStruct((2, blocks), jnp.int32),
            jax.ShapeDtypeStruct((sum(part.shape[0] for part in own), width), BF16),
        ),
        in_specs=[SMEM, ANY, ANY, VMEM, VMEM, ANY, ANY, ANY],
        out_specs=(ANY,) * 6 + (VMEM, SMEM, ANY),
        scratch_shapes=[
            pltpu.VMEM((rows, width), F32),
            pltpu.VMEM(qkv3.shape, BF16),
            pltpu.VMEM((sum(part.shape[0] for part in own), width), BF16),
            pltpu.VMEM((group, width), BF16),
            pltpu.VMEM((width, group), BF16),
            pltpu.VMEM((blocks, across, local), BF16),
            pltpu.VMEM((group, local), BF16),
            pltpu.VMEM((group, local), BF16),
            pltpu.VMEM((local, group), BF16),
            pltpu.VMEM((local, group), BF16),
            dma_sems(5), dma_sems(count), dma_sems(count), dma_sems(count), dma_sems(count),
            dma_sems(count), dma_sems(count), dma_sems(count), dma_sems(4, 6),
        ],
        compiler_params=pltpu.CompilerParams(
            collective_id=0, has_side_effects=True, vmem_limit_bytes=60 << 20
        ),
        cost_estimate=pl.CostEstimate(flops=2 * group * width * 3 * local, bytes_accessed=12 << 20, transcendentals=0),
        name="gather_project",
    )(lengths, post_stream, qkv3, query_bias, value_bias, *own)


UNROLL = 8


def list_tiles(limits, tiles, counts, blocks):
    spare = jnp.int32(blocks * 65536)
    tiles[0] = spare
    tiles[1] = spare

    def put(code, first, last, at):
        def step(j, at):
            tiles[at] = code + j
            return at + 1

        return lax.fori_loop(first, last, step, at)

    def diagonal(i, at):
        tiles[at] = i * 65536 + i * 257
        return at + 1

    def edge_row(i, at):
        return put(i * 65536 + i * 256, limits[0, i], limits[1, i], at)

    def whole_row(i, at):
        return put(i * 65536 + i * 256, jnp.maximum(limits[0, i], limits[1, i]), i, at)

    at = jnp.int32(2)
    for kind, row in enumerate((diagonal, edge_row, whole_row)):
        at = lax.fori_loop(0, blocks, row, at)
        counts[kind] = (at - 2 + (1 if kind < 2 else 2) + UNROLL - 1) // UNROLL
    for u in range(2 * UNROLL + 2):
        tiles[at + u] = spare


def for_tiles(tiles, counts, heads, products, probabilities, sums):
    for kind in range(3):

        def step(n, _):
            codes = [tiles[n * UNROLL + u] for u in range(UNROLL + 2)]
            entries = [(code // 65536, (code // 256) % 256, code % 256) for code in codes]
            for u in range(UNROLL):
                for h in range(heads):
                    if products is not None:
                        products(u % 2, h, *entries[u + 2])
                    sums(u % 2, h, *entries[u])
                    probabilities((u + 1) % 2, h, kind, *entries[u + 1])
            return 0

        lax.fori_loop(counts[kind - 1] if kind else 0, counts[kind], step, 0)


def masked_score(score, kind, starts, i, j, lanes):
    if kind == 2:
        return score
    keys, queries = score.shape
    score = score.reshape(keys // 8, 8, queries)
    row = 8 * lax.broadcasted_iota(jnp.int32, score.shape, 0)
    key = lax.broadcasted_iota(jnp.int32, (8, queries), 0) + j * TILE
    allowed = (key - starts[i, :, lanes])[None] >= -row
    if kind == 0:
        query = lax.broadcasted_iota(jnp.int32, (8, queries), 1) + i * TILE
        allowed = allowed & ((key - query)[None] <= -row)
    return jnp.where(allowed, score, MASKED).reshape(keys, queries)


def tile_limit(blocks):
    return blocks * (blocks + 1) // 2 + 4 * UNROLL


def attend_kernel(
    limits, starts_ref, q_ref, k_ref, vt_ref, att_ref, lse_ref, tiles, counts,
    queries, k, vt, top, total, acc, scores, probs, alphas, att_b, sem, out_sem,
):
    blocks, wide, local = queries.shape
    heads = local // HEAD_DIM
    one = pl.ds(0, 1)
    loads = [
        pltpu.make_async_copy(src, dst, sem.at[n])
        for n, (src, dst) in enumerate(((q_ref, queries), (k_ref, k), (vt_ref, vt)))
    ]
    for load in loads:
        load.start()
    list_tiles(limits, tiles, counts, blocks)
    top[...] = jnp.full_like(top, MASKED)
    total[...] = jnp.zeros_like(total)
    acc[...] = jnp.zeros_like(acc)
    for load in loads:
        load.wait()

    def products(b, h, slot, i, j):
        lanes = pl.ds(h * TILE, TILE)
        scores[b, :, lanes] = dot(k[ds(j * TILE, TILE)], queries[i, lanes], NT)

    def probabilities(b, h, kind, slot, i, j):
        lanes = pl.ds(h * TILE, TILE)
        score = scores[b, :, lanes]
        score = masked_score(score, kind, starts_ref, i, j, lanes)
        old = top[slot, one, lanes]
        new = jnp.maximum(old, jnp.max(score, axis=0, keepdims=True))
        top[slot, one, lanes] = new
        alpha = jnp.exp(old - new)
        prob = jnp.exp(score - new)
        total[slot, one, lanes] = total[slot, one, lanes] * alpha + jnp.sum(prob, axis=0, keepdims=True)
        probs[b, :, lanes] = prob.astype(BF16)
        alphas[b, one, lanes] = alpha

    def sums(b, h, slot, i, j):
        lanes = pl.ds(h * TILE, TILE)
        values_t = vt[pl.ds(h * HEAD_DIM, HEAD_DIM), ds(j * TILE, TILE)]
        acc[slot, :, lanes] = acc[slot, :, lanes] * alphas[b, one, lanes] + dot(values_t, probs[b, :, lanes])

    for_tiles(tiles, counts, heads, products, probabilities, sums)

    def finish(i, _):
        lse_ref[i, one] = top[i, one] + jnp.log(total[i, one])
        out_t = acc[i] / total[i, one]
        here = ds(i * TILE, TILE)
        parts = [out_t[:, h * TILE : (h + 1) * TILE] for h in range(heads)]
        att_b[here] = jnp.concatenate(parts, axis=0).T.astype(BF16)
        pltpu.make_async_copy(att_b.at[here], att_ref.at[here], out_sem.at[i]).start()
        return 0

    lax.fori_loop(0, blocks, finish, 0, unroll=4)
    for i in range(blocks):
        here = pl.ds(i * TILE, TILE)
        pltpu.make_async_copy(att_b.at[here], att_ref.at[here], out_sem.at[i]).wait()


def attend(limits, starts, queries, k, vt):
    group, local = k.shape
    blocks, wide, _ = queries.shape
    return pl.pallas_call(
        attend_kernel,
        in_specs=[SMEM, VMEM, ANY, ANY, ANY],
        out_specs=[ANY, VMEM, SMEM, SMEM],
        out_shape=(
            jax.ShapeDtypeStruct((group, local), BF16),
            jax.ShapeDtypeStruct((blocks, 8, wide), F32),
            jax.ShapeDtypeStruct((tile_limit(blocks),), jnp.int32),
            jax.ShapeDtypeStruct((3,), jnp.int32),
        ),
        scratch_shapes=[
            pltpu.VMEM((blocks, wide, local), BF16),
            pltpu.VMEM((group, local), BF16),
            pltpu.VMEM((local, group), BF16),
            pltpu.VMEM((blocks + 1, 8, wide), F32),
            pltpu.VMEM((blocks + 1, 8, wide), F32),
            pltpu.VMEM((blocks + 1, HEAD_DIM, wide), F32),
            pltpu.VMEM((2, TILE, wide), F32),
            pltpu.VMEM((2, TILE, wide), BF16),
            pltpu.VMEM((2, 8, wide), F32),
            pltpu.VMEM((group, local), BF16),
            dma_sems(3), dma_sems(blocks),
        ],
        compiler_params=pltpu.CompilerParams(vmem_limit_bytes=60 << 20),
        cost_estimate=pl.CostEstimate(flops=12 << 30, bytes_accessed=4 << 20, transcendentals=8 << 20),
        name="attend",
    )(limits, starts, queries, k, vt)


def attend_back_kernel(
    tiles, counts, starts_ref, lse, q_ref, do_ref, o_ref, k_ref, v_ref, kt_ref, post_mid, pre_mid,
    dq_ref, dk_ref, dv_ref, post_out, pre_out,
    queries, do, o, k, v, kt, grads, delta, dq_acc, dk_acc, dv_acc,
    probs, score_grads, passed_b, out_b, sem, out_sem,
):
    blocks, wide, local = queries.shape
    heads = local // HEAD_DIM
    one = pl.ds(0, 1)
    loads = [
        pltpu.make_async_copy(src, dst, sem.at[n])
        for n, (src, dst) in enumerate(((do_ref, do), (o_ref, o), (q_ref, queries), (k_ref, k), (v_ref, v), (kt_ref, kt)))
    ]
    passed_in = [
        pltpu.make_async_copy(src, passed_b.at[n], sem.at[6 + n]) for n, src in enumerate((post_mid, pre_mid))
    ]
    passed_out = [
        pltpu.make_async_copy(passed_b.at[n], dst, sem.at[8 + n]) for n, dst in enumerate((post_out, pre_out))
    ]
    for load in loads + passed_in:
        load.start()
    dq_acc[...] = jnp.zeros_like(dq_acc)
    dk_acc[...] = jnp.zeros_like(dk_acc)
    dv_acc[...] = jnp.zeros_like(dv_acc)
    for load in loads[:2]:
        load.wait()

    def prepare(i, _):
        here = ds(i * TILE, TILE)
        block = do[here]
        for h in range(heads):
            grads[i, pl.ds(h * TILE, TILE)] = head_masked(block, h)
        along = (block.astype(F32) * o[here].astype(F32)).T
        parts = [column_sum(along[h * HEAD_DIM : (h + 1) * HEAD_DIM]) for h in range(heads)]
        delta[i, one] = jnp.concatenate(parts, axis=1)
        return 0

    lax.fori_loop(0, blocks, prepare, 0, unroll=4)
    for load in loads[2:]:
        load.wait()
    for copy_in, copy_out in zip(passed_in, passed_out):
        copy_in.wait()
        copy_out.start()

    def probabilities(b, h, kind, slot, i, j):
        lanes = pl.ds(h * TILE, TILE)
        here = ds(j * TILE, TILE)
        score = dot(k[here], queries[i, lanes], NT)
        score = masked_score(score, kind, starts_ref, i, j, lanes)
        rise = dot(v[here], grads[i, lanes], NT)
        prob = jnp.exp(score - lse[i, one, lanes])
        probs[b, :, lanes] = prob.astype(BF16)
        score_grads[b, :, lanes] = (prob * (rise - delta[i, one, lanes])).astype(BF16)

    def sums(b, h, slot, i, j):
        lanes = pl.ds(h * TILE, TILE)
        spot = ds(jnp.where(slot == blocks, blocks, j) * TILE, TILE)
        if h == 0:
            dv_acc[spot] += dot(probs[b], grads[i])
        else:
            dk_acc[spot] += dot(score_grads[b], queries[i])
        keys_t = kt[pl.ds(h * HEAD_DIM, HEAD_DIM), ds(j * TILE, TILE)]
        dq_acc[slot, :, lanes] += dot(keys_t, score_grads[b, :, lanes])

    for_tiles(tiles, counts, heads, None, probabilities, sums)

    outs = (dq_ref, dk_ref, dv_ref)

    def out_copy(n, i):
        here = ds(i * TILE, TILE)
        return pltpu.make_async_copy(out_b.at[n, here], outs[n].at[here], out_sem.at[n, i])

    def finish(i, _):
        here = ds(i * TILE, TILE)
        dq_t = dq_acc[i] * HEAD_DIM ** (-0.5)
        parts = [dq_t[:, h * TILE : (h + 1) * TILE] for h in range(heads)]
        out_b[0, here] = jnp.concatenate(parts, axis=0).T.astype(BF16)
        out_b[1, here] = dk_acc[here].astype(BF16)
        out_b[2, here] = dv_acc[here].astype(BF16)
        for n in range(3):
            out_copy(n, i).start()
        return 0

    lax.fori_loop(0, blocks, finish, 0, unroll=4)
    for i in range(blocks):
        for n in range(3):
            out_copy(n, i).wait()
    for copy in passed_out:
        copy.wait()


def attend_back(tiles, counts, starts, lse, queries, k, v, kt, att, att_grad, post_mid, pre_mid):
    group, local = k.shape
    blocks, wide, _ = queries.shape
    shape = jax.ShapeDtypeStruct((group, local), BF16)
    tall = pltpu.VMEM((group, local), BF16)
    return pl.pallas_call(
        attend_back_kernel,
        in_specs=[SMEM, SMEM, VMEM, VMEM] + [ANY] * 8,
        out_specs=[ANY] * 5,
        out_shape=(shape, shape, shape, jax.ShapeDtypeStruct(post_mid.shape, F32), jax.ShapeDtypeStruct(pre_mid.shape, F32)),
        scratch_shapes=[
            pltpu.VMEM((blocks, wide, local), BF16),
            tall, tall, tall, tall,
            pltpu.VMEM((local, group), BF16),
            pltpu.VMEM((blocks, wide, local), BF16),
            pltpu.VMEM((blocks, 8, wide), F32),
            pltpu.VMEM((blocks + 1, HEAD_DIM, wide), F32),
            pltpu.VMEM((group + TILE, local), F32),
            pltpu.VMEM((group + TILE, local), F32),
            pltpu.VMEM((2, TILE, wide), BF16),
            pltpu.VMEM((2, TILE, wide), BF16),
            pltpu.VMEM((2,) + post_mid.shape, F32),
            pltpu.VMEM((3, group, local), BF16),
            dma_sems(10), dma_sems(3, blocks),
        ],
        compiler_params=pltpu.CompilerParams(vmem_limit_bytes=60 << 20),
        cost_estimate=pl.CostEstimate(flops=30 << 30, bytes_accessed=9 << 20, transcendentals=8 << 20),
        name="attend_back",
    )(tiles, counts, starts, lse, queries, att_grad, att, k, v, kt, post_mid, pre_mid)


def center_and_scale(summed):
    width = summed.shape[1]
    center = summed - jnp.sum(summed, axis=1, keepdims=True) * (1.0 / width)
    inverse = lax.rsqrt(jnp.sum(center * center, axis=1, keepdims=True) * (1.0 / width) + EPSILON)
    return center * inverse, inverse


def norm_backward(cotangent, normed, inverse, gain):
    width = normed.shape[1]
    scaled = cotangent * gain
    mean = jnp.sum(scaled, axis=1, keepdims=True) * (1.0 / width)
    along = jnp.sum(scaled * normed, axis=1, keepdims=True) * (1.0 / width)
    return inverse * (scaled - mean - normed * along)


def gelu_and_slope(value):
    square = value * value
    inner = value * (SQRT_2_OVER_PI + (SQRT_2_OVER_PI * 0.044715) * square)
    half = 0.5 + 0.5 * jnp.tanh(inner)
    rise = value * (2.0 * SQRT_2_OVER_PI + (6.0 * SQRT_2_OVER_PI * 0.044715) * square)
    return value * half, half * (1.0 + (1.0 - half) * rise)


def middle_kernel(
    att, post, pre, post_cot, pre_cot, own, far, out_bias_ref, gain1_ref, shift1_ref, down_bias_ref, gain2_ref, shift2_ref, up_bias_ref,
    post_out, pre_out, sum1_out, att_grad_out, keep_out, give_out, small_out,
    post_b, pre_b, post_cot_b, pre_cot_b, att_in, w_up, w_down, w_out, up_bias, up_bias_all,
    mid_low, hidden, act_grad, ffn_grad, branch_grad, att_grad_b, slope_b,
    post_out_b, pre_out_b, sum1_b, send_b, recv_b, keep_b, give_b,
    in_sem, own_sem, weight_sem, send_w, recv_w, send_p, recv_p,
    send_a, recv_a, send_g, recv_g, send_r, recv_r, out_sem,
):
    me, sib, across, diagonal = mp_peers()
    dp = lax.axis_index("dp")
    rows, width = post.shape
    chunk = TILE
    count = rows // chunk
    local = att.shape[1]
    hid = w_up.shape[2]
    spans = (pl.ds(0, width), pl.ds(width, hid), pl.ds(width + hid, local))
    peers = (sib, across, diagonal)

    def stream(c):
        here = pl.ds(c * chunk, chunk)
        return [
            pltpu.make_async_copy(src.at[here], dst.at[here], in_sem.at[c, n])
            for n, (src, dst) in enumerate(
                ((post, post_b), (pre, pre_b), (post_cot, post_cot_b), (pre_cot, pre_cot_b))
            )
        ]

    def own_attended():
        return pltpu.make_async_copy(
            att.at[ds(me * rows, rows)], att_in.at[:, ds(me * local, local)], own_sem.at[0]
        )

    def local_weights():
        copies = []
        for n, (owner, packed) in enumerate(((me, own), (across, far))):
            places = (w_up.at[owner], w_down.at[owner], w_out.at[ds(owner * local, local)])
            copies += [
                pltpu.make_async_copy(packed.at[span], dst, weight_sem.at[n, k])
                for k, (span, dst) in enumerate(zip(spans, places))
            ]
        return copies

    def sent_weights():
        copies = []
        for n, (owner, packed) in enumerate(((me, own), (across, far))):
            places = (w_up.at[owner], w_down.at[owner], w_out.at[ds(owner * local, local)])
            copies += [
                remote(packed.at[span], dst, send_w.at[n, k], recv_w.at[n, k], (dp, sib))
                for k, (span, dst) in enumerate(zip(spans, places))
            ]
        return copies

    def arriving_weights():
        copies = []
        for n, owner in enumerate((sib, diagonal)):
            places = (w_up.at[owner], w_down.at[owner], w_out.at[ds(owner * local, local)])
            copies += [pltpu.make_async_copy(p, p, recv_w.at[n, k]) for k, p in enumerate(places)]
        return copies

    def sent_prm(n):
        return remote(up_bias, up_bias_all.at[me], send_p.at[n], recv_p.at[n], (dp, peers[n]))

    def sent_attended(n, c):
        peer = peers[n]
        return remote(
            att.at[ds(peer * rows + c * chunk, chunk)],
            att_in.at[ds(c * chunk, chunk), ds(me * local, local)],
            send_a.at[n, c],
            recv_a.at[n, c],
            (dp, peer),
        )

    def arriving_attended(n, c):
        place = att_in.at[ds(c * chunk, chunk), ds(peers[n] * local, local)]
        return pltpu.make_async_copy(place, place, recv_a.at[n, c])

    def sent_grad(n, c):
        peer = peers[n]
        return remote(
            att_grad_b.at[ds(c * chunk, chunk), ds(peer * local, local)],
            att_grad_out.at[ds(me * rows + c * chunk, chunk)],
            send_g.at[n, c],
            recv_g.at[n, c],
            (dp, peer),
        )

    def arriving_grad(n, c):
        place = att_grad_out.at[ds(peers[n] * rows + c * chunk, chunk)]
        return pltpu.make_async_copy(place, place, recv_g.at[n, c])

    def own_grad(c):
        return pltpu.make_async_copy(
            att_grad_b.at[ds(c * chunk, chunk), ds(me * local, local)],
            att_grad_out.at[ds(me * rows + c * chunk, chunk)],
            out_sem.at[c, 3],
        )

    def stored(c):
        here = ds(c * chunk, chunk)
        return [
            pltpu.make_async_copy(src.at[here], dst.at[here], out_sem.at[c, n])
            for n, (src, dst) in enumerate(((post_out_b, post_out), (pre_out_b, pre_out), (sum1_b, sum1_out)))
        ]

    for copy in stream(0) + [own_attended()] + local_weights():
        copy.start()
    up_bias[...] = jnp.broadcast_to(as_row(up_bias_ref), up_bias.shape)
    greet([(dp, peer) for peer in peers])
    for n in range(3):
        sent_prm(n).start()
    for c in range(count):
        for n in (2, 1, 0):
            sent_attended(n, c).start()
    for copy in sent_weights():
        copy.start()
    for c in range(1, count):
        for copy in stream(c):
            copy.start()
    up_bias_all[ds(me, 1)] = up_bias[...][None]
    small_out[...] = jnp.zeros_like(small_out)
    own_attended().wait()
    for n in range(3):
        arrived = up_bias_all.at[peers[n]]
        pltpu.make_async_copy(arrived, arrived, recv_p.at[n]).wait()
    for copy in local_weights() + arriving_weights():
        copy.wait()

    out_bias, gain1, shift1 = as_row(out_bias_ref), as_row(gain1_ref), as_row(shift1_ref)
    down_bias, gain2, shift2 = as_row(down_bias_ref), as_row(gain2_ref), as_row(shift2_ref)

    def block_step(c, _):
        here = ds(c * chunk, chunk)
        for n in range(3):
            arriving_attended(n, c).wait()
        for n in range(4):
            pltpu.make_async_copy(post_b.at[here], post_b.at[here], in_sem.at[c, n]).wait()
        branch = dot(att_in[here], w_out[...]) + out_bias
        normed1, inverse1 = center_and_scale(post_b[here] + branch)
        mid = normed1 * gain1 + shift1
        pre_mid = pre_b[here] + branch
        low = mid.astype(BF16)
        mid_low[here] = low
        ffn = jnp.zeros((chunk, width), F32)
        for f in range(MP):
            pre_act = dot(low, w_up[f]) + up_bias_all[f, 0:1]
            value, slope = gelu_and_slope(pre_act)
            value = value.astype(BF16)
            hidden[f, here] = value
            slope_b[f] = slope
            ffn = ffn + dot(value, w_down[f])
        ffn = ffn + down_bias
        normed2, inverse2 = center_and_scale(mid + ffn)
        post_out_b[here] = normed2 * gain2 + shift2
        pre_out_b[here] = pre_mid + ffn
        cot = post_cot_b[here]
        small_out[4:5] += column_sum(cot * normed2)
        small_out[5:6] += column_sum(cot)
        sum2_grad = norm_backward(cot, normed2, inverse2, gain2)
        grad = (sum2_grad + pre_cot_b[here]).astype(BF16)
        ffn_grad[here] = grad
        small_out[3:4] += column_sum(grad.astype(F32))
        mid_grad = sum2_grad
        for f in range(MP):
            back = (dot(grad, w_down[f], NT) * slope_b[f]).astype(BF16)
            act_grad[f, here] = back
            small_out[8 + f : 9 + f] += column_sum(back.astype(F32))
            mid_grad = mid_grad + dot(back, w_up[f], NT)
        small_out[1:2] += column_sum(mid_grad * normed1)
        small_out[2:3] += column_sum(mid_grad)
        sum1 = norm_backward(mid_grad, normed1, inverse1, gain1)
        sum1_b[here] = sum1
        grad1 = (sum1 + pre_cot_b[here]).astype(BF16)
        branch_grad[here] = grad1
        small_out[0:1] += column_sum(grad1.astype(F32))
        att_grad_b[here] = dot(grad1, w_out[...], NT).astype(BF16)
        for n in (2, 1, 0):
            sent_grad(n, c).start()
        own_grad(c).start()
        for copy in stored(c):
            copy.start()
        return 0

    lax.fori_loop(0, count, block_step, 0)

    def weight_grads(s):
        up = dot(mid_low[...], act_grad[s], TN)
        down = dot(hidden[s], ffn_grad[...], TN)
        out = dot(att_in[:, ds(s * local, local)], branch_grad[...], TN)
        return up, down, out

    def sent_sums(n):
        return remote(send_b.at[n], recv_b.at[n], send_r.at[n], recv_r.at[n], (dp, sib))

    for n, owner in enumerate((diagonal, sib)):
        for span, part in zip(spans, weight_grads(owner)):
            send_b[n, span] = part.astype(BF16)
        sent_sums(n).start()
    for span, part in zip(spans, weight_grads(across)):
        keep_b[span] = part
    sent_sums(0).wait_recv()
    give_b[...] = (keep_b[...] + recv_b[0].astype(F32)).astype(BF16)
    give = pltpu.make_async_copy(give_b, give_out, own_sem.at[1])
    give.start()
    for span, part in zip(spans, weight_grads(me)):
        keep_b[span] = part
    sent_sums(1).wait_recv()
    keep_b[...] = keep_b[...] + recv_b[1].astype(F32)
    keep = pltpu.make_async_copy(keep_b, keep_out, own_sem.at[2])
    keep.start()
    for c in range(count):
        for copy in stored(c) + [own_grad(c)]:
            copy.wait()
        for n in range(3):
            sent_attended(n, c).wait_send()
            sent_grad(n, c).wait_send()
            arriving_grad(n, c).wait()
    for copy in sent_weights():
        copy.wait_send()
    for n in range(3):
        sent_prm(n).wait_send()
    for n in range(2):
        sent_sums(n).wait_send()
    give.wait()
    keep.wait()


def middle(att, post, pre, post_cot, pre_cot, own, far, vectors):
    rows, width = post.shape
    local = att.shape[1]
    tall = own.shape[0]
    hid = tall - width - local
    count = rows // TILE
    f32 = jax.ShapeDtypeStruct((rows, width), F32)
    return pl.pallas_call(
        middle_kernel,
        out_shape=(
            f32, f32, f32,
            jax.ShapeDtypeStruct(att.shape, BF16),
            jax.ShapeDtypeStruct((tall, width), F32),
            jax.ShapeDtypeStruct((tall, width), BF16),
            jax.ShapeDtypeStruct((16, width), F32),
        ),
        in_specs=[ANY] * 7 + [VMEM] * len(vectors),
        out_specs=(ANY,) * 6 + (VMEM,),
        scratch_shapes=[
            pltpu.VMEM((rows, width), F32),
            pltpu.VMEM((rows, width), F32),
            pltpu.VMEM((rows, width), F32),
            pltpu.VMEM((rows, width), F32),
            pltpu.VMEM((rows, MP * local), BF16),
            pltpu.VMEM((MP, width, hid), BF16),
            pltpu.VMEM((MP, hid, width), BF16),
            pltpu.VMEM((MP * local, width), BF16),
            pltpu.VMEM((8, hid), F32),
            pltpu.VMEM((MP, 8, hid), F32),
            pltpu.VMEM((rows, width), BF16),
            pltpu.VMEM((MP, rows, hid), BF16),
            pltpu.VMEM((MP, rows, hid), BF16),
            pltpu.VMEM((rows, width), BF16),
            pltpu.VMEM((rows, width), BF16),
            pltpu.VMEM((rows, MP * local), BF16),
            pltpu.VMEM((MP, TILE, hid), F32),
            pltpu.VMEM((rows, width), F32),
            pltpu.VMEM((rows, width), F32),
            pltpu.VMEM((rows, width), F32),
            pltpu.VMEM((2, tall, width), BF16),
            pltpu.VMEM((2, tall, width), BF16),
            pltpu.VMEM((tall, width), F32),
            pltpu.VMEM((tall, width), BF16),
            dma_sems(count, 4), dma_sems(3), dma_sems(2, 3), dma_sems(2, 3), dma_sems(2, 3),
            dma_sems(3), dma_sems(3), dma_sems(3, count), dma_sems(3, count),
            dma_sems(3, count), dma_sems(3, count), dma_sems(2), dma_sems(2), dma_sems(count, 4),
        ],
        compiler_params=pltpu.CompilerParams(
            collective_id=1, has_side_effects=True, vmem_limit_bytes=60 << 20
        ),
        cost_estimate=pl.CostEstimate(flops=15 << 30, bytes_accessed=20 << 20, transcendentals=4 << 20),
        name="middle",
    )(att, post, pre, post_cot, pre_cot, own, far, *vectors)


ROW_TIME = 0.0209
HOP_TIME = 2.5


def sum_plan(dp_size, width, hid, local):
    bits = dp_size.bit_length() - 1
    near_first = tuple(range(bits))
    swapped = (1, 0) + near_first[2:] if bits > 1 else near_first
    far_first = near_first[2:] + near_first[:2]
    half, sixth = width // 2, 3 * width // 8
    rows = [
        (half, near_first, 1.0), (half, near_first, 1.0), (hid // 2, swapped, 1.0), (hid // 2, far_first, 1.0),
        (local, far_first, 1.0), (sixth, near_first, 6.0), (sixth, swapped, 6.0),
    ]
    pieces, start = [], 0
    for size, order, ready in rows:
        steps = []
        left = size
        for b in order:
            halved = left % 32 == 0
            steps.append((b, left, halved))
            left = left // 2 if halved else left
        pieces.append((start, size, ready, steps))
        start += size
    return pieces, start


def plan_length(steps):
    return len(steps) + sum(halved for _, _, halved in steps)


def step_times(pieces, bits):
    free = [0.0] * bits
    waiting = [(ready, n, 0) for n, (_, _, ready, _) in enumerate(pieces)]
    times = []
    while waiting:
        now, n, t = min(waiting)
        waiting.remove((now, n, t))
        times.append((now, n, t))
        steps = pieces[n][3]
        if t == plan_length(steps):
            continue
        back = [s for s in reversed(steps) if s[2]]
        b, size, halved = steps[t] if t < len(steps) else back[t - len(steps)]
        cost = (size // 2 if halved else size) * ROW_TIME * (2 if b == 2 else 1)
        free[b] = max(now, free[b]) + cost
        waiting.append((free[b] + HOP_TIME, n, t + 1))
    return times


def tail_kernel(
    dp_size,
    dq, dk, dv, tok_t, w, sum1, keep, given, small,
    post_out, full_out, small_out,
    grads, tok_b, sum1_b, given_b, mine, far, send_far, recv_far, pass_far, land_far, send_near, recv_near,
    acc, flight, full, land, small_flight, small_land,
    in_sem, near_send, near_recv, far_send, far_recv, hop_send, hop_recv,
    step_send, step_recv, small_send, small_recv, out_sem, full_sem,
):
    me, sib, across, diagonal = mp_peers()
    dp = lax.axis_index("dp")
    rows, width = sum1.shape
    local = dq.shape[1]
    chunk = TILE
    count = rows // chunk
    tall = keep.shape[0]
    hid = tall - width - local
    bits = dp_size.bit_length() - 1
    partners = [dp + (1 << b) - 2 * (1 << b) * ((dp // (1 << b)) % 2) for b in range(bits)]
    upper = [(dp // (1 << b)) % 2 for b in range(bits)]
    pieces, total = sum_plan(dp_size, width, hid, local)

    loads = [
        pltpu.make_async_copy(src, grads.at[n], in_sem.at[n]) for n, src in enumerate((dq, dk, dv))
    ] + [
        pltpu.make_async_copy(tok_t, tok_b, in_sem.at[3]),
        pltpu.make_async_copy(keep, acc.at[pl.ds(0, tall)], in_sem.at[5]),
        pltpu.make_async_copy(given, given_b, in_sem.at[6]),
        pltpu.make_async_copy(sum1, sum1_b, in_sem.at[4]),
    ]
    for n in (4, 5, 0, 1, 2, 3, 6):
        loads[n].start()
    greet([(dp, sib), (dp, across)] + [(p, me) for p in partners])

    offsets = {}
    for n, (base, _, _, steps) in enumerate(pieces):
        base = jnp.int32(base)
        for t, (b, size, halved) in enumerate(steps):
            if halved:
                half = size // 2
                offsets[n, t] = (base + (1 - upper[b]) * half, base + upper[b] * half, half)
                base = base + upper[b] * half
            else:
                offsets[n, t] = (base, base, size)

    def reduce_copy(n, t):
        given_at, _, size = offsets[n, t]
        here = ds16(given_at, size)
        return remote(
            flight.at[here], land.at[t, here],
            step_send.at[0, n, t], step_recv.at[0, n, t], (partners[pieces[n][3][t][0]], me),
        )

    def reduce_start(n, t):
        given_at, _, size = offsets[n, t]
        here = ds16(given_at, size)
        flight[here] = acc[here].astype(BF16)
        reduce_copy(n, t).start()

    def reduce_finish(n, t):
        _, kept_at, size = offsets[n, t]
        copy = reduce_copy(n, t)
        copy.wait_recv()
        here = ds16(kept_at, size)
        if pieces[n][3][t][2]:
            acc[here] = acc[here] + land[t, here].astype(F32)
        else:
            acc[here] = flight[here].astype(F32) + land[t, here].astype(F32)
        copy.wait_send()

    def spread_copy(n, t):
        _, kept_at, size = offsets[n, t]
        here = ds16(kept_at, size)
        return remote(
            full.at[here], full.at[here],
            step_send.at[1, n, t], step_recv.at[1, n, t], (partners[pieces[n][3][t][0]], me),
        )

    def spread_done(n, t):
        given_at, _, size = offsets[n, t]
        there = ds16(given_at, size)
        pltpu.make_async_copy(full.at[there], full.at[there], step_recv.at[1, n, t]).wait()
        spread_copy(n, t).wait_send()

    def full_copy(n):
        here = pl.ds(pieces[n][0], pieces[n][1])
        return pltpu.make_async_copy(full.at[here], full_out.at[here], full_sem.at[n])

    def stage(n, t):
        steps = pieces[n][3]
        back = [s for s in range(len(steps) - 1, -1, -1) if steps[s][2]]
        if 0 < t <= len(steps):
            reduce_finish(n, t - 1)
        if t < len(steps):
            reduce_start(n, t)
            return
        if t == len(steps):
            _, kept_at, size = offsets[n, len(steps) - 1]
            here = ds16(kept_at, size)
            full[here] = acc[here].astype(BF16)
        else:
            spread_done(n, back[t - len(steps) - 1])
        if t < plan_length(steps):
            spread_copy(n, back[t - len(steps)]).start()
        else:
            full_copy(n).start()

    small_peers = [(dp, sib), (dp, across)] + [(p, me) for p in partners]

    def small_copy(s):
        return remote(small_flight.at[s], small_land.at[s], small_send.at[s], small_recv.at[s], small_peers[s])

    def small_stage(s):
        if s == 0:
            small_out[...] = small[...]
            query_sum = column_sum(grads[0].astype(F32))
            value_sum = column_sum(grads[2].astype(F32))
            small_out[ds1(12 + me), :] = jnp.concatenate(
                [query_sum, value_sum, jnp.zeros((1, width - 2 * local), F32)], axis=1
            )
        else:
            small_copy(s - 1).wait()
            small_out[...] = small_out[...] + small_land[s - 1]
        if s < len(small_peers):
            small_flight[s] = small_out[...]
            small_copy(s).start()

    def part(owner, c):
        here = ds(owner * rows + c * chunk, chunk)
        return (
            dot(grads[0, here], w[0], NT) + dot(grads[1, here], w[1], NT) + dot(grads[2, here], w[2], NT)
        )

    def far_copy(c):
        return remote(send_far.at[c], recv_far.at[c], far_send.at[c], far_recv.at[c], (dp, sib))

    def hop_copy(c):
        return remote(pass_far.at[c], land_far.at[c], hop_send.at[c], hop_recv.at[c], (dp, across))

    def near_copy(c):
        return remote(send_near.at[c], recv_near.at[c], near_send.at[c], near_recv.at[c], (dp, sib))

    def post_copy(c):
        here = pl.ds(c * chunk, chunk)
        return pltpu.make_async_copy(sum1_b.at[here], post_out.at[here], out_sem.at[c])

    def far_step(c):
        if c == 0:
            for n in range(3):
                loads[n].wait()
        send_far[c] = part(diagonal, c).astype(BF16)
        far_copy(c).start()
        far[c] = part(across, c)

    def hop_step(c):
        far_copy(c).wait_recv()
        pass_far[c] = (far[c] + recv_far[c].astype(F32)).astype(BF16)
        hop_copy(c).start()

    def near_step(c):
        send_near[c] = part(sib, c).astype(BF16)
        near_copy(c).start()
        mine[c] = part(me, c)

    def near_add(c):
        near_copy(c).wait_recv()
        mine[c] = mine[c] + recv_near[c].astype(F32)

    def post_step(c):
        if c == 0:
            loads[6].wait()
        hop_copy(c).wait_recv()
        here = pl.ds(c * chunk, chunk)
        sum1_b[here] = sum1_b[here] + mine[c] + land_far[c].astype(F32)
        post_copy(c).start()

    def own_sums(_):
        loads[4].wait()
        loads[5].wait()
        own = pl.ds(0, tall)
        acc[own] = acc[own] + given_b[...].astype(F32)

    def weight_step(_):
        loads[3].wait()
        third = width // 4
        for n in range(3):
            block = dot(tok_b[...], grads[n])
            for s in range(4):
                acc[pl.ds(tall + n * third, third), pl.ds(s * local, local)] = block[s * third : (s + 1) * third]

    events = [(now, 5, stage, (n, t)) for now, n, t in step_times(pieces, bits)]
    events += [(0.9, 0, own_sums, (0,)), (5.9, 0, weight_step, (0,))]
    for c in range(count):
        events.append((1.5 + 0.7 * c, 1, far_step, (c,)))
        events.append((2.9 + 0.7 * c, 2, hop_step, (c,)))
        events.append((6.5 + 0.7 * c, 3, near_step, (c,)))
        events.append((11.0 + 0.7 * c, 3, near_add, (c,)))
        events.append((12.5 + 5.3 * c, 6, post_step, (c,)))
    for s in range(len(small_peers) + 1):
        events.append((9.5 + 3.5 * s, 4, small_stage, (s,)))
    for _, _, act, where in sorted(events, key=lambda event: event[:2] + (event[3],)):
        act(*where)

    for c in range(count):
        far_copy(c).wait_send()
        hop_copy(c).wait_send()
        near_copy(c).wait_send()
        post_copy(c).wait()
    for n in range(len(pieces)):
        full_copy(n).wait()


def ds16(start, size):
    return pl.ds(pl.multiple_of(start, 16), size)


def ds1(start):
    return pl.ds(start, 1)


def tail(dp_size, dq, dk, dv, tok_t, w, sum1, keep, given, small):
    rows, width = sum1.shape
    group, local = dq.shape
    tall = keep.shape[0]
    hid = tall - width - local
    count = rows // TILE
    bits = dp_size.bit_length() - 1
    assert 1 << bits == dp_size
    pieces, total = sum_plan(dp_size, width, hid, local)
    blocks = (count, TILE, width)
    steps = bits + 2
    return pl.pallas_call(
        functools.partial(tail_kernel, dp_size),
        out_shape=(
            jax.ShapeDtypeStruct((rows, width), F32),
            jax.ShapeDtypeStruct((total, width), BF16),
            jax.ShapeDtypeStruct(small.shape, F32),
        ),
        in_specs=[ANY] * 4 + [VMEM] + [ANY] * 3 + [VMEM],
        out_specs=(ANY, ANY, VMEM),
        scratch_shapes=[
            pltpu.VMEM((3, group, local), BF16),
            pltpu.VMEM((width, group), BF16),
            pltpu.VMEM((rows, width), F32),
            pltpu.VMEM((tall, width), BF16),
            pltpu.VMEM(blocks, F32),
            pltpu.VMEM(blocks, F32),
            pltpu.VMEM(blocks, BF16),
            pltpu.VMEM(blocks, BF16),
            pltpu.VMEM(blocks, BF16),
            pltpu.VMEM(blocks, BF16),
            pltpu.VMEM(blocks, BF16),
            pltpu.VMEM(blocks, BF16),
            pltpu.VMEM((total, width), F32),
            pltpu.VMEM((total, width), BF16),
            pltpu.VMEM((total, width), BF16),
            pltpu.VMEM((bits, total, width), BF16),
            pltpu.VMEM((steps,) + small.shape, F32),
            pltpu.VMEM((steps,) + small.shape, F32),
            dma_sems(7), dma_sems(count), dma_sems(count), dma_sems(count), dma_sems(count),
            dma_sems(count), dma_sems(count), dma_sems(2, len(pieces), bits), dma_sems(2, len(pieces), bits),
            dma_sems(steps), dma_sems(steps), dma_sems(count), dma_sems(len(pieces)),
        ],
        compiler_params=pltpu.CompilerParams(
            collective_id=2, has_side_effects=True, vmem_limit_bytes=60 << 20
        ),
        cost_estimate=pl.CostEstimate(flops=4 << 30, bytes_accessed=20 << 20, transcendentals=0),
        name="tail",
    )(dq, dk, dv, tok_t, w, sum1, keep, given, small)


def finish_kernel(
    post_sum, full, small,
    post_grad, qkv_grad, up_grad, down_grad, out_grad,
    query_grad, value_grad, out_bias, gain1, shift1, up_bias, down_bias, gain2, shift2,
    post_b, full_b, grad_b, qkv_b, sem, out_sem,
):
    me = lax.axis_index("mp")
    total, width = full.shape
    local = query_grad.shape[0]
    hid = down_grad.shape[0]
    tall = width + hid + local
    third = width // 4
    post_in = pltpu.make_async_copy(post_sum, post_b, sem.at[0])
    post = pltpu.make_async_copy(post_b, post_grad, sem.at[5])
    post_in.start()
    spans = ((0, width, up_grad), (width, hid, down_grad), (width + hid, local, out_grad), (tall, total - tall, None))
    loads = []
    for n, (start, size, _) in enumerate(spans):
        here = pl.ds(start, size)
        loads.append(pltpu.make_async_copy(full.at[here], full_b.at[here], sem.at[1 + n]))
        loads[-1].start()
    for row, vector in enumerate((out_bias, gain1, shift1, down_bias, gain2, shift2)):
        vector[...] = small[row]
    own = small[pl.ds(12 + me, 1), :]
    query_grad[...] = own[0, :local]
    value_grad[...] = own[0, local : 2 * local]
    up_bias[...] = small[pl.ds(8 + me, 1), :][0]
    stores = []
    post_in.wait()
    post.start()
    for n, (start, size, dst) in enumerate(spans):
        loads[n].wait()
        here = pl.ds(start, size)
        if dst is not None:
            grad_b[here] = full_b[here].astype(F32)
            stores.append(pltpu.make_async_copy(grad_b.at[here], dst, out_sem.at[n]))
        else:
            for m in range(3):
                for s in range(4):
                    qkv_b[m, pl.ds(s * third, third)] = full_b[
                        pl.ds(start + m * third, third), pl.ds(s * local, local)
                    ].astype(F32)
            stores.append(pltpu.make_async_copy(qkv_b, qkv_grad, out_sem.at[n]))
        stores[-1].start()
    for store in stores + [post]:
        store.wait()


def finish(post_sum, full, small, hid, local):
    rows, width = post_sum.shape
    total = full.shape[0]
    vector = lambda size: jax.ShapeDtypeStruct((size,), F32)
    return pl.pallas_call(
        finish_kernel,
        out_shape=(
            jax.ShapeDtypeStruct((rows, width), F32),
            jax.ShapeDtypeStruct((3, width, local), F32),
            jax.ShapeDtypeStruct((width, hid), F32),
            jax.ShapeDtypeStruct((hid, width), F32),
            jax.ShapeDtypeStruct((local, width), F32),
            vector(local), vector(local), vector(width), vector(width), vector(width),
            vector(hid), vector(width), vector(width), vector(width),
        ),
        in_specs=[ANY, ANY, VMEM],
        out_specs=(ANY,) * 5 + (VMEM,) * 9,
        scratch_shapes=[
            pltpu.VMEM((rows, width), F32),
            pltpu.VMEM((total, width), BF16),
            pltpu.VMEM((total, width), F32),
            pltpu.VMEM((3, width, local), F32),
            dma_sems(6), dma_sems(4),
        ],
        compiler_params=pltpu.CompilerParams(vmem_limit_bytes=60 << 20),
        name="results",
    )(post_sum, full, small)


def body(
    dp_size,
    post_stream,
    pre_stream,
    seq_lengths,
    qkv_weight,
    query_bias,
    value_bias,
    out_weight,
    out_bias,
    norm1_gain,
    norm1_shift,
    up_weight,
    up_bias,
    down_weight,
    down_bias,
    norm2_gain,
    norm2_shift,
    post_cotan,
    pre_cotan,
):
    local = out_weight.shape[0]
    hid = down_weight.shape[0]
    qkv3 = jnp.transpose(qkv_weight, (1, 0, 2))
    tok_t, queries, k, v, kt, vt, starts, limits, own = gather_and_project(
        seq_lengths, post_stream, qkv3, query_bias, value_bias, (up_weight, down_weight, out_weight)
    )
    across = [(m, (m + 2) % MP) for m in range(MP)]
    far = lax.ppermute(own, "mp", across)
    att, lse, tiles, counts = attend(limits, starts, queries, k, vt)
    vectors = (out_bias, norm1_gain, norm1_shift, down_bias, norm2_gain, norm2_shift, up_bias)
    post_mid, pre_mid, sum1, att_grad, keep, give, small = middle(
        att, post_stream, pre_stream, post_cotan, pre_cotan, own, far, vectors
    )
    given = lax.ppermute(give, "mp", across)
    dq, dk, dv, post_out, pre_out = attend_back(
        tiles, counts, starts, lse, queries, k, v, kt, att, att_grad, post_mid, pre_mid
    )
    post_sum, full, small = tail(dp_size, dq, dk, dv, tok_t, qkv3, sum1, keep, given, small)
    (
        post_grad, qkv_grad, up_grad, down_grad, out_grad,
        query_grad, value_grad, out_bias_grad, gain1, shift1, up_bias_grad, down_bias_grad, gain2, shift2,
    ) = finish(post_sum, full, small, hid, local)
    return (
        post_out, pre_out, post_grad, jnp.transpose(qkv_grad, (1, 0, 2)), query_grad, value_grad, out_grad,
        out_bias_grad, gain1, shift1, up_grad, up_bias_grad, down_grad, down_bias_grad, gain2, shift2,
    )


def solution(mesh):
    tokens = P(("dp", "mp"), None)
    vector = P()
    return jax.shard_map(
        functools.partial(body, mesh.shape["dp"]),
        mesh=mesh,
        in_specs=(
            tokens, tokens, P("dp", None), P(None, None, "mp"), P("mp"), P("mp"), P("mp", None),
            vector, vector, vector, P(None, "mp"), P("mp"), P("mp", None), vector, vector, vector,
            tokens, tokens,
        ),
        out_specs=(
            tokens, tokens, tokens, P(None, None, "mp"), P("mp"), P("mp"), P("mp", None),
            vector, vector, vector, P(None, "mp"), P("mp"), P("mp", None), vector, vector, vector,
        ),
        check_vma=False,
    )
```

time: 256 us -> 192 us (0.75)
  Pallas kernels: 220 us -> 176 us
  local copies, waits for them, and re-layouts: 29.3 us -> 2.03 us
  waiting for transfers between devices: 0.01 us -> 11.4 us
  starting transfers between devices: 4.19 us -> 1.33 us
    pallas_call x2 -> x3, Pallas kernels: 88.4 us -> 50 us  [the longest x1 27.4 us: attend_back(): pl.pallas_call(attend_back_kernel, in_specs=[SMEM, SMEM, VMEM, VMEM] + [A...]
    unnamed x53 -> x4, local copies, waits for them, and re-layouts: 21.7 us -> 2.03 us
    ppermute x3 -> x1, waiting for transfers between devices: 0.01 us -> 11.1 us  [body(): far = lax.ppermute(own, 'mp', across)]
    pallas_call x1, Pallas kernels: 67.4 us -> 58.8 us  [tail(): pl.pallas_call(functools.partial(tail_kernel, dp_size), out_shape=(jax.Sh...]
    another operation x9 -> x0, local copies, waits for them, and re-layouts: 4.81 us -> none  [body(): jnp.stack([jnp.concatenate([query_bias, pad, value_bias, pad]), out_bias,...]
    pallas_call x1, Pallas kernels: 29.5 us -> 32.4 us  [gather_and_project(): pl.pallas_call(project_kernel, out_shape=(jax.ShapeDtypeStruct((width, gr...]
    slice x2 -> x0, local copies, waits for them, and re-layouts: 2.82 us -> none  [the longest x1 1.55 us: body(): small[5]]
  transfers between devices with their start and end apart: 4 -> 2, of which waited for: 0 -> 2; matrix products, arithmetic and copies ran while one was open for 0% -> 0% of each run, Pallas kernels for 35% -> 23%
where the time goes in v2:
time: 192 us
  Pallas kernels  176 us (92%)
  waiting for transfers between devices  11.4 us (6%)
  local copies, waits for them, and re-layouts  2.03 us (1%)
    pallas_call x1, Pallas kernels, tail(): pl.pallas_call(functools.partial(tail_kernel, dp_size), out_shape=(jax.Sh...  58.8 us
    pallas_call x1, Pallas kernels, middle(): pl.pallas_call(middle_kernel, out_shape=(f32, f32, f32, jax.ShapeDtypeStr...  35.2 us
    pallas_call x1, Pallas kernels, gather_and_project(): pl.pallas_call(project_kernel, out_shape=(jax.ShapeDtypeStruct((width, gr...  32.4 us
    pallas_call x1, Pallas kernels, attend_back(): pl.pallas_call(attend_back_kernel, in_specs=[SMEM, SMEM, VMEM, VMEM] + [A...  27.4 us
    pallas_call x1, Pallas kernels, attend(): pl.pallas_call(attend_kernel, in_specs=[SMEM, VMEM, ANY, ANY, ANY], out_s...  17.2 us
    ppermute x1, waiting for transfers between devices, body(): far = lax.ppermute(own, 'mp', across)  11.1 us
    pallas_call x1, Pallas kernels, finish(): pl.pallas_call(finish_kernel, out_shape=(jax.ShapeDtypeStruct((rows, widt...  5.4 us
  transfers between devices with their start and end apart: 2, of which 2 were waited for; matrix products, arithmetic and copies ran while one was open for 0% of the time, Pallas kernels for 23%

profile of v2, /device:TPU:0, one launch (start us, length us, event | category | flops | bytes accessed | tf_op | source)
XLA Modules:
  0.0 192.0 jit_solution(3283547821456534425)
XLA Ops:
  0.6 32.4 %gather_project.1 = (bf16[512,4096]{1,0:T(8,128)(2,1)}, bf16[16,512,128]{2,1,0:T(8,128)(2,1)}, bf16[4096,128]{1,0:T(8,128)(2,1)}, bf16[4096,128]{1,0:T(8,128)(2,...) custom-call(s32[1,13]{1,0:T(1,128)} %lengths.1, ...), custom_call_target="tpu_custom_call" | custom-call | flops 1610612736 | bytes 12582912 | tf_op jit(solution)/shard_map/gather_project/pallas_call | solution.py:228
  33.0 0.7 collective-permute-start
  33.7 17.2 %attend.1 = (bf16[4096,128]{1,0:T(8,128)(2,1)}, f32[16,8,512]{2,1,0:T(8,128)}, s32[168]{0:T(256)}, s32[3]{0:T(128)}) custom-call(s32[2,16]{1,0:T(2,128)} %get-tuple-element.58.limits, s32[16,8,512]{2,1,0:T(8,128)} %get-tuple-element.59.starts_ref, bf16[16,512,128]{2,1,0:T(8,128)(2,1)} %get-tuple-element.60.q_ref, bf16[4096,128]{1,0:T(8,128)(2,1)} %get-tuple-element.61.k_ref, ...), custom_call_target="tpu_custom_call" | custom-call | flops 12884901888 | bytes 4194304 | tf_op jit(solution)/shard_map/attend/pallas_call | solution.py:392
  50.9 11.1 %collective-permute-done.far = bf16[1152,512]{1,0:T(8,128)(2,1)S(1)} collective-permute-done((bf16[1152,512]{1,0:T(8,128)(2,1)}, bf16[1152,512]{1,0:T(8,128)(2,1)S(1)}, u32[]{:S(2)}, u32[]{:S(2)}) %collective-permute-start) | collective-permute-done | bytes 1179680 | tf_op jit(solution)/shard_map/ppermute | solution.py:1274
  62.0 0.0 copy-start.1
  62.0 1.0 copy-done.1
  63.0 35.2 %middle.1 = (f32[1024,512]{1,0:T(8,128)}, f32[1024,512]{1,0:T(8,128)}, f32[1024,512]{1,0:T(8,128)}, bf16[4096,128]{1,0:T(8,128)(2,1)}, f32[1152,512]{1,0:T(8,128...) custom-call(bf16[4096,128]{1,0:T(8,128)(2,1)} %get-tuple-element.66.att.o_ref, f32[1024,512]{1,0:T(8,128)} %post.3, ...), custom_call_target="tpu_custom_call" | custom-call | flops 16106127360 | bytes 20971520 | tf_op jit(solution)/shard_map/middle/pallas_call | solution.py:800
  98.2 0.7 collective-permute-start.1
  98.9 27.4 %attend_back.1 = (bf16[4096,128]{1,0:T(8,128)(2,1)}, bf16[4096,128]{1,0:T(8,128)(2,1)}, bf16[4096,128]{1,0:T(8,128)(2,1)}, f32[1024,512]{1,0:T(8,128)}, f32[1024,512]{1,0:T(8,128)}) custom-call(s32[168]{0:T(256)} %get-tuple-element.63.tiles, s32[3]{0:T(128)} %get-tuple-element.64.counts, s32[16,8,512]{2,1,0:T(8,128)} %get-tuple-element.59.starts_ref, ...), custom_call_target="tpu_custom_call" | custom-call | flops 32212254720 | bytes 9437184 | tf_op jit(solution)/shard_map/attend_back/pallas_call | solution.py:517
  126.3 0.3 collective-permute-done.1.given
  126.6 0.0 copy-start
  126.6 1.0 copy-done
  127.6 58.8 %tail.1 = (f32[1024,512]{1,0:T(8,128)}, bf16[1536,512]{1,0:T(8,128)(2,1)}, f32[16,512]{1,0:T(8,128)}) custom-call(bf16[4096,128]{1,0:T(8,128)(2,1)} %get-tuple-element.75.dq, bf16[4096,128]{1,0:T(8,128)(2,1)} %get-tuple-element.76.dk, bf16[4096,128]{1,0:T(8,128)(2,1)} %get-tuple-element.77.dv, bf16[512,4096]{1,0:T(8,128)(2,1)} %get-tuple-element.78.tok_t, ...), custom_call_target="tpu_custom_call" | custom-call | flops 4294967296 | bytes 20971520 | tf_op jit(solution)/shard_map/tail/pallas_call | solution.py:1129
  186.4 5.4 %results.1 = (f32[1024,512]{1,0:T(8,128)}, f32[3,512,128]{2,1,0:T(8,128)}, f32[512,512]{1,0:T(8,128)}, f32[512,512]{1,0:T(8,128)}, f32[128,512]{1,0:T(8,128)}, /...) custom-call(f32[1024,512]{1,0:T(8,128)} %get-tuple-element.83.post_s, ...), custom_call_target="tpu_custom_call" | custom-call | tf_op jit(solution)/shard_map/results/pallas_call | solution.py:1221
Async XLA Ops:
  33.0 29.0 %collective-permute-start = (bf16[1152,512]{1,0:T(8,128)(2,1)}, bf16[1152,512]{1,0:T(8,128)(2,1)S(1)}, u32[]{:S(2)}, u32[]{:S(2)}) collective-permute-start(bf16[1152,512]{1,0:T(8,128)(2,1)} %get-tuple-element.67.own), channel_id=1, source_target_pairs={{0,2},{1,3},{2,0},{3,1},{4,6},{5,7},{6,4},{7,5},{8,10},{9,11},{10,... | collective-permute-start | bytes 3538952 | tf_op jit(solution)/shard_map/ppermute | solution.py:1274
  62.0 1.0 copy-start.1
  98.2 28.4 %collective-permute-start.1 = (bf16[1152,512]{1,0:T(8,128)(2,1)}, bf16[1152,512]{1,0:T(8,128)(2,1)S(1)}, u32[]{:S(2)}, u32[]{:S(2)}) collective-permute-start(bf16[1152,512]{1,0:T(8,128)(2,1)} %get-tuple-element.81), channel_id=1, source_target_pairs={{0,2},{1,3},{2,0},{3,1},{4,6},{5,7},{6,4},{7,5},{8,10},{9,11},{10,... | collective-permute-start | bytes 3538952 | tf_op jit(solution)/shard_map/ppermute | solution.py:1280
  126.6 1.0 copy-start

commit v3 on v2

--- a/solution.py
+++ b/solution.py
@@ -42,6 +42,10 @@
     pl.semaphore_wait(barrier, len(devices))
 
 
+def ds16(start, size):
+    return pl.ds(pl.multiple_of(start, 16), size)
+
+
 def remote(src, dst, send_sem, recv_sem, device):
     return pltpu.make_async_remote_copy(
         src_ref=src,
@@ -81,17 +85,22 @@
     return jnp.where((lane >= h * HEAD_DIM) & (lane < (h + 1) * HEAD_DIM), block, jnp.zeros_like(block))
 
 
+def dp_slices(dp_size):
+    return min(dp_size, 8)
+
+
 def project_kernel(
+    dp_size,
     lengths, post, w_any, query_bias_ref, value_bias_ref, up, down, out,
-    tok_t_out, q_out, k_out, v_out, kt_out, vt_out, starts, limits, own_out,
-    stage, w, own_b, tok, tok_t, q_s, k_s, v_s, kt_s, vt_s,
-    w_sem, in_sem, send_x, recv_x, send_c, recv_c, send_f, recv_f, out_sem,
+    tok_t_out, q_out, k_out, v_out, kt_out, vt_out, starts, limits, own_out, line_out,
+    stage, w, own_b, line_b, tok, tok_t, q_s, k_s, v_s, kt_s, vt_s,
+    w_sem, line_send, line_recv, in_sem, send_x, recv_x, send_c, recv_c, send_f, recv_f, out_sem,
 ):
     me, sib, across, diagonal = mp_peers()
     dp = lax.axis_index("dp")
     rows = post.shape[0]
     width = post.shape[1]
-    chunk = TILE
+    chunk = TILE // 2
     count = rows // chunk
     heads = w.shape[2] // HEAD_DIM
     hid = up.shape[1]
@@ -106,7 +115,32 @@
     ]
     for load in loads + [w_load] + packs:
         load.start()
-    greet([(dp, sib), (dp, across)])
+    slices = dp_slices(dp_size)
+    line = slices // 2
+    spot = (dp // 2) % line
+    part = own_b.shape[0] // slices
+    line_peers = []
+    for mask in range(1, line):
+        peer = dp
+        for b in range(line.bit_length() - 1):
+            if mask >> b & 1:
+                peer = peer + (2 << b) - 2 * (2 << b) * ((dp // (2 << b)) % 2)
+        line_peers.append(peer)
+    greet([(dp, sib), (dp, across)] + [(peer, me) for peer in line_peers])
+
+    def slice_over():
+        return remote(
+            own_b.at[ds16(((dp % 2) * line + spot) * part, part)], line_b.at[ds16(spot * part, part)],
+            line_send.at[0], line_recv.at[0], (dp, across),
+        )
+
+    def slice_along(n):
+        here = ds16(spot * part, part)
+        return remote(line_b.at[here], line_b.at[here], line_send.at[1 + n], line_recv.at[1 + n], (line_peers[n], me))
+
+    def slice_arrived(n):
+        here = ds16(((line_peers[n] // 2) % line) * part, part)
+        return pltpu.make_async_copy(line_b.at[here], line_b.at[here], line_recv.at[1 + n])
 
     def piece(owner, c):
         return ds(owner * rows + c * chunk, chunk)
@@ -132,6 +166,11 @@
         tok[piece(me, c)] = stage[pl.ds(c * chunk, chunk)].astype(BF16)
         to_across(c).start()
         to_sibling(c).start()
+        if c == 0:
+            for pack in packs:
+                pack.wait()
+            slice_over().start()
+            packed.start()
 
     query_bias = as_row(query_bias_ref)
     value_bias = as_row(value_bias_ref)
@@ -143,7 +182,7 @@
         query = (dot(block, w[0]) + query_bias).astype(BF16)
         query = (query.astype(F32) * HEAD_DIM ** (-0.5)).astype(BF16)
         for h in range(heads):
-            q_s[owner * count + c, pl.ds(h * TILE, TILE)] = head_masked(query, h)
+            q_s[owner * (rows // TILE) + c // 2, ds(h * TILE + (c % 2) * chunk, chunk)] = head_masked(query, h)
         keys = dot(block, w[1]).astype(BF16)
         k_s[here] = keys
         kt_s[:, here] = keys.T
@@ -151,17 +190,16 @@
         v_s[here] = values
         vt_s[:, here] = values.T
 
-    def outs(g, owner):
-        here = ds(owner * rows, rows)
+    def outs(g, owner, c):
+        here = ds(owner * rows + c * TILE, TILE)
+        block = owner * (rows // TILE) + c
         return [
-            pltpu.make_async_copy(tok_t.at[:, here], tok_t_out.at[:, here], out_sem.at[g, 0]),
-            pltpu.make_async_copy(
-                q_s.at[pl.ds(owner * count, count)], q_out.at[pl.ds(owner * count, count)], out_sem.at[g, 1]
-            ),
-            pltpu.make_async_copy(k_s.at[here], k_out.at[here], out_sem.at[g, 2]),
-            pltpu.make_async_copy(v_s.at[here], v_out.at[here], out_sem.at[g, 3]),
-            pltpu.make_async_copy(kt_s.at[:, here], kt_out.at[:, here], out_sem.at[g, 4]),
-            pltpu.make_async_copy(vt_s.at[:, here], vt_out.at[:, here], out_sem.at[g, 5]),
+            pltpu.make_async_copy(tok_t.at[:, here], tok_t_out.at[:, here], out_sem.at[g, c, 0]),
+            pltpu.make_async_copy(q_s.at[block], q_out.at[block], out_sem.at[g, c, 1]),
+            pltpu.make_async_copy(k_s.at[here], k_out.at[here], out_sem.at[g, c, 2]),
+            pltpu.make_async_copy(v_s.at[here], v_out.at[here], out_sem.at[g, c, 3]),
+            pltpu.make_async_copy(kt_s.at[:, here], kt_out.at[:, here], out_sem.at[g, c, 4]),
+            pltpu.make_async_copy(vt_s.at[:, here], vt_out.at[:, here], out_sem.at[g, c, 5]),
         ]
 
     w_load.wait()
@@ -176,71 +214,93 @@
         limits[1, i] = jnp.minimum((last + TILE - 1) // TILE, i)
 
     def own_step(c, _):
-        project(me, c)
+        project(me, 2 * c)
+        project(me, 2 * c + 1)
+        for copy in outs(0, me, c):
+            copy.start()
         return 0
 
-    lax.fori_loop(0, count, own_step, 0)
-    for copy in outs(0, me):
-        copy.start()
-    for pack in packs:
-        pack.wait()
-    packed.start()
+    lax.fori_loop(0, count // 2, own_step, 0)
 
     def sibling_step(c, _):
-        arrived(sib, recv_c, c).wait()
-        project(sib, c)
+        for n in (0, 1):
+            arrived(sib, recv_c, 2 * c + n).wait()
+            project(sib, 2 * c + n)
+        for copy in outs(1, sib, c):
+            copy.start()
         return 0
 
-    lax.fori_loop(0, count, sibling_step, 0)
-    for copy in outs(1, sib):
-        copy.start()
+    lax.fori_loop(0, count // 2, sibling_step, 0)
+
+    def slices_on(_):
+        slice_over().wait_recv()
+        for n in range(len(line_peers)):
+            slice_along(n).start()
+
+    slices_on(0)
 
     def across_step(c, _):
-        arrived(across, recv_x, c).wait()
-        forward(c).start()
-        project(across, c)
-        arrived(diagonal, recv_f, c).wait()
-        project(diagonal, c)
+        for n in (0, 1):
+            arrived(across, recv_x, 2 * c + n).wait()
+            forward(2 * c + n).start()
+            project(across, 2 * c + n)
+        for copy in outs(2, across, c):
+            copy.start()
+        for n in (0, 1):
+            arrived(diagonal, recv_f, 2 * c + n).wait()
+            project(diagonal, 2 * c + n)
+        for copy in outs(3, diagonal, c):
+            copy.start()
         return 0
 
-    lax.fori_loop(0, count, across_step, 0)
-    for copy in outs(2, across) + outs(3, diagonal):
-        copy.start()
+    lax.fori_loop(0, count // 2, across_step, 0)
     for c in range(count):
         to_across(c).wait_send()
         to_sibling(c).wait_send()
         forward(c).wait_send()
+    packed.wait()
+    slice_over().wait_send()
+    for n in range(len(line_peers)):
+        slice_along(n).wait_send()
+        slice_arrived(n).wait()
+    line_copy = pltpu.make_async_copy(line_b, line_out, w_sem.at[5])
+    line_copy.start()
     for g, owner in enumerate((me, sib, across, diagonal)):
-        for copy in outs(g, owner):
-            copy.wait()
-    packed.wait()
-
-
-def gather_and_project(lengths, post_stream, qkv3, query_bias, value_bias, own):
+        for c in range(count // 2):
+            for copy in outs(g, owner, c):
+                copy.wait()
+    line_copy.wait()
+
+
+def gather_and_project(dp_size, lengths, post_stream, qkv3, query_bias, value_bias, own):
     rows, width = post_stream.shape
     group = rows * MP
     local = qkv3.shape[2]
-    count = rows // TILE
+    count = 2 * rows // TILE
     tall = jax.ShapeDtypeStruct((group, local), BF16)
     wide = jax.ShapeDtypeStruct((local, group), BF16)
     blocks = group // TILE
     across = TILE * (local // HEAD_DIM)
+    tall_rows = sum(part.shape[0] for part in own)
+    line = dp_slices(dp_size) // 2
     return pl.pallas_call(
-        project_kernel,
+        functools.partial(project_kernel, dp_size),
         out_shape=(
             jax.ShapeDtypeStruct((width, group), BF16),
             jax.ShapeDtypeStruct((blocks, across, local), BF16),
             tall, tall, wide, wide,
             jax.ShapeDtypeStruct((blocks, 8, across), jnp.int32),
             jax.ShapeDtypeStruct((2, blocks), jnp.int32),
-            jax.ShapeDtypeStruct((sum(part.shape[0] for part in own), width), BF16),
+            jax.ShapeDtypeStruct((tall_rows, width), BF16),
+            jax.ShapeDtypeStruct((tall_rows // 2, width), BF16),
         ),
         in_specs=[SMEM, ANY, ANY, VMEM, VMEM, ANY, ANY, ANY],
-        out_specs=(ANY,) * 6 + (VMEM, SMEM, ANY),
+        out_specs=(ANY,) * 6 + (VMEM, SMEM, ANY, ANY),
         scratch_shapes=[
             pltpu.VMEM((rows, width), F32),
             pltpu.VMEM(qkv3.shape, BF16),
-            pltpu.VMEM((sum(part.shape[0] for part in own), width), BF16),
+            pltpu.VMEM((tall_rows, width), BF16),
+            pltpu.VMEM((tall_rows // 2, width), BF16),
             pltpu.VMEM((group, width), BF16),
             pltpu.VMEM((width, group), BF16),
             pltpu.VMEM((blocks, across, local), BF16),
@@ -248,8 +308,8 @@
             pltpu.VMEM((group, local), BF16),
             pltpu.VMEM((local, group), BF16),
             pltpu.VMEM((local, group), BF16),
-            dma_sems(5), dma_sems(count), dma_sems(count), dma_sems(count), dma_sems(count),
-            dma_sems(count), dma_sems(count), dma_sems(count), dma_sems(4, 6),
+            dma_sems(6), dma_sems(line), dma_sems(line), dma_sems(count), dma_sems(count), dma_sems(count), dma_sems(count),
+            dma_sems(count), dma_sems(count), dma_sems(count), dma_sems(4, count // 2, 6),
         ],
         compiler_params=pltpu.CompilerParams(
             collective_id=0, has_side_effects=True, vmem_limit_bytes=60 << 20
@@ -564,11 +624,11 @@
 
 
 def middle_kernel(
-    att, post, pre, post_cot, pre_cot, own, far, out_bias_ref, gain1_ref, shift1_ref, down_bias_ref, gain2_ref, shift2_ref, up_bias_ref,
-    post_out, pre_out, sum1_out, att_grad_out, keep_out, give_out, small_out,
-    post_b, pre_b, post_cot_b, pre_cot_b, att_in, w_up, w_down, w_out, up_bias, up_bias_all,
+    att, post, pre, post_cot, pre_cot, own, far_line, far_side, out_bias_ref, gain1_ref, shift1_ref, down_bias_ref, gain2_ref, shift2_ref, up_bias_ref,
+    post_out, pre_out, sum1_out, att_grad_out, keep_out, to_across_out, to_beside_out, to_corner_out, small_out,
+    post_b, pre_b, post_cot_b, pre_cot_b, att_in, w_all, w_out, up_bias, up_bias_all,
     mid_low, hidden, act_grad, ffn_grad, branch_grad, att_grad_b, slope_b,
-    post_out_b, pre_out_b, sum1_b, send_b, recv_b, keep_b, give_b,
+    post_out_b, pre_out_b, sum1_b, send_b, recv_b, keep_b, give_b, beside_b,
     in_sem, own_sem, weight_sem, send_w, recv_w, send_p, recv_p,
     send_a, recv_a, send_g, recv_g, send_r, recv_r, out_sem,
 ):
@@ -578,7 +638,9 @@
     chunk = TILE
     count = rows // chunk
     local = att.shape[1]
-    hid = w_up.shape[2]
+    tall = own.shape[0]
+    hid = tall - width - local
+    up_rows, down_rows = pl.ds(0, width), pl.ds(width, hid)
     spans = (pl.ds(0, width), pl.ds(width, hid), pl.ds(width + hid, local))
     peers = (sib, across, diagonal)
 
@@ -596,32 +658,24 @@
             att.at[ds(me * rows, rows)], att_in.at[:, ds(me * local, local)], own_sem.at[0]
         )
 
+    half = tall // 2
+    line_at = ds16((dp % 2) * half, half)
+    side_at = ds16((1 - dp % 2) * half, half)
+    weight_parts = (
+        (own, w_all.at[me]), (far_line, w_all.at[across, line_at]), (far_side, w_all.at[across, side_at])
+    )
+
     def local_weights():
-        copies = []
-        for n, (owner, packed) in enumerate(((me, own), (across, far))):
-            places = (w_up.at[owner], w_down.at[owner], w_out.at[ds(owner * local, local)])
-            copies += [
-                pltpu.make_async_copy(packed.at[span], dst, weight_sem.at[n, k])
-                for k, (span, dst) in enumerate(zip(spans, places))
-            ]
-        return copies
+        return [pltpu.make_async_copy(src, dst, weight_sem.at[n]) for n, (src, dst) in enumerate(weight_parts)]
 
     def sent_weights():
-        copies = []
-        for n, (owner, packed) in enumerate(((me, own), (across, far))):
-            places = (w_up.at[owner], w_down.at[owner], w_out.at[ds(owner * local, local)])
-            copies += [
-                remote(packed.at[span], dst, send_w.at[n, k], recv_w.at[n, k], (dp, sib))
-                for k, (span, dst) in enumerate(zip(spans, places))
-            ]
-        return copies
+        return [
+            remote(src, dst, send_w.at[n], recv_w.at[n], (dp, sib)) for n, (src, dst) in enumerate(weight_parts)
+        ]
 
     def arriving_weights():
-        copies = []
-        for n, owner in enumerate((sib, diagonal)):
-            places = (w_up.at[owner], w_down.at[owner], w_out.at[ds(owner * local, local)])
-            copies += [pltpu.make_async_copy(p, p, recv_w.at[n, k]) for k, p in enumerate(places)]
-        return copies
+        places = (w_all.at[sib], w_all.at[diagonal, line_at], w_all.at[diagonal, side_at])
+        return [pltpu.make_async_copy(p, p, recv_w.at[n]) for n, p in enumerate(places)]
 
     def sent_prm(n):
         return remote(up_bias, up_bias_all.at[me], send_p.at[n], recv_p.at[n], (dp, peers[n]))
@@ -690,6 +744,8 @@
         pltpu.make_async_copy(arrived, arrived, recv_p.at[n]).wait()
     for copy in local_weights() + arriving_weights():
         copy.wait()
+    for f in range(MP):
+        w_out[pl.ds(f * local, local)] = w_all[f, pl.ds(width + hid, local)]
 
     out_bias, gain1, shift1 = as_row(out_bias_ref), as_row(gain1_ref), as_row(shift1_ref)
     down_bias, gain2, shift2 = as_row(down_bias_ref), as_row(gain2_ref), as_row(shift2_ref)
@@ -708,12 +764,12 @@
         mid_low[here] = low
         ffn = jnp.zeros((chunk, width), F32)
         for f in range(MP):
-            pre_act = dot(low, w_up[f]) + up_bias_all[f, 0:1]
+            pre_act = dot(low, w_all[f, up_rows]) + up_bias_all[f, 0:1]
             value, slope = gelu_and_slope(pre_act)
             value = value.astype(BF16)
             hidden[f, here] = value
             slope_b[f] = slope
-            ffn = ffn + dot(value, w_down[f])
+            ffn = ffn + dot(value, w_all[f, down_rows])
         ffn = ffn + down_bias
         normed2, inverse2 = center_and_scale(mid + ffn)
         post_out_b[here] = normed2 * gain2 + shift2
@@ -727,10 +783,10 @@
         small_out[3:4] += column_sum(grad.astype(F32))
         mid_grad = sum2_grad
         for f in range(MP):
-            back = (dot(grad, w_down[f], NT) * slope_b[f]).astype(BF16)
+            back = (dot(grad, w_all[f, down_rows], NT) * slope_b[f]).astype(BF16)
             act_grad[f, here] = back
             small_out[8 + f : 9 + f] += column_sum(back.astype(F32))
-            mid_grad = mid_grad + dot(back, w_up[f], NT)
+            mid_grad = mid_grad + dot(back, w_all[f, up_rows], NT)
         small_out[1:2] += column_sum(mid_grad * normed1)
         small_out[2:3] += column_sum(mid_grad)
         sum1 = norm_backward(mid_grad, normed1, inverse1, gain1)
@@ -764,15 +820,26 @@
     for span, part in zip(spans, weight_grads(across)):
         keep_b[span] = part
     sent_sums(0).wait_recv()
+    ours = ds((dp % 2) * (width // 2), width // 2)
+    theirs = ds((1 - dp % 2) * (width // 2), width // 2)
     give_b[...] = (keep_b[...] + recv_b[0].astype(F32)).astype(BF16)
-    give = pltpu.make_async_copy(give_b, give_out, own_sem.at[1])
-    give.start()
+    gives = [
+        pltpu.make_async_copy(give_b.at[:, ours], to_across_out, own_sem.at[1]),
+        pltpu.make_async_copy(give_b.at[:, theirs], to_corner_out, own_sem.at[2]),
+    ]
+    for give in gives:
+        give.start()
     for span, part in zip(spans, weight_grads(me)):
         keep_b[span] = part
     sent_sums(1).wait_recv()
     keep_b[...] = keep_b[...] + recv_b[1].astype(F32)
-    keep = pltpu.make_async_copy(keep_b, keep_out, own_sem.at[2])
-    keep.start()
+    beside_b[...] = keep_b[:, theirs].astype(BF16)
+    gives += [
+        pltpu.make_async_copy(keep_b.at[:, ours], keep_out, own_sem.at[3]),
+        pltpu.make_async_copy(beside_b, to_beside_out, own_sem.at[4]),
+    ]
+    for give in gives[2:]:
+        give.start()
     for c in range(count):
         for copy in stored(c) + [own_grad(c)]:
             copy.wait()
@@ -786,11 +853,11 @@
         sent_prm(n).wait_send()
     for n in range(2):
         sent_sums(n).wait_send()
-    give.wait()
-    keep.wait()
-
-
-def middle(att, post, pre, post_cot, pre_cot, own, far, vectors):
+    for give in gives:
+        give.wait()
+
+
+def middle(att, post, pre, post_cot, pre_cot, own, far_line, far_side, vectors):
     rows, width = post.shape
     local = att.shape[1]
     tall = own.shape[0]
@@ -802,20 +869,21 @@
         out_shape=(
             f32, f32, f32,
             jax.ShapeDtypeStruct(att.shape, BF16),
-            jax.ShapeDtypeStruct((tall, width), F32),
-            jax.ShapeDtypeStruct((tall, width), BF16),
+            jax.ShapeDtypeStruct((tall, width // 2), F32),
+            jax.ShapeDtypeStruct((tall, width // 2), BF16),
+            jax.ShapeDtypeStruct((tall, width // 2), BF16),
+            jax.ShapeDtypeStruct((tall, width // 2), BF16),
             jax.ShapeDtypeStruct((16, width), F32),
         ),
-        in_specs=[ANY] * 7 + [VMEM] * len(vectors),
-        out_specs=(ANY,) * 6 + (VMEM,),
+        in_specs=[ANY] * 8 + [VMEM] * len(vectors),
+        out_specs=(ANY,) * 8 + (VMEM,),
         scratch_shapes=[
             pltpu.VMEM((rows, width), F32),
             pltpu.VMEM((rows, width), F32),
             pltpu.VMEM((rows, width), F32),
             pltpu.VMEM((rows, width), F32),
             pltpu.VMEM((rows, MP * local), BF16),
-            pltpu.VMEM((MP, width, hid), BF16),
-            pltpu.VMEM((MP, hid, width), BF16),
+            pltpu.VMEM((MP, tall, width), BF16),
             pltpu.VMEM((MP * local, width), BF16),
             pltpu.VMEM((8, hid), F32),
             pltpu.VMEM((MP, 8, hid), F32),
@@ -833,7 +901,8 @@
             pltpu.VMEM((2, tall, width), BF16),
             pltpu.VMEM((tall, width), F32),
             pltpu.VMEM((tall, width), BF16),
-            dma_sems(count, 4), dma_sems(3), dma_sems(2, 3), dma_sems(2, 3), dma_sems(2, 3),
+            pltpu.VMEM((tall, width // 2), BF16),
+            dma_sems(count, 4), dma_sems(5), dma_sems(3), dma_sems(3), dma_sems(3),
             dma_sems(3), dma_sems(3), dma_sems(3, count), dma_sems(3, count),
             dma_sems(3, count), dma_sems(3, count), dma_sems(2), dma_sems(2), dma_sems(count, 4),
         ],
@@ -842,43 +911,65 @@
         ),
         cost_estimate=pl.CostEstimate(flops=15 << 30, bytes_accessed=20 << 20, transcendentals=4 << 20),
         name="middle",
-    )(att, post, pre, post_cot, pre_cot, own, far, *vectors)
-
-
-ROW_TIME = 0.0209
-HOP_TIME = 2.5
+    )(att, post, pre, post_cot, pre_cot, own, far_line, far_side, *vectors)
+
+
+ROW_TIME = 0.0105
+HOP_TIME = 2.8
+HALF = 256
 
 
 def sum_plan(dp_size, width, hid, local):
     bits = dp_size.bit_length() - 1
-    near_first = tuple(range(bits))
-    swapped = (1, 0) + near_first[2:] if bits > 1 else near_first
-    far_first = near_first[2:] + near_first[:2]
-    half, sixth = width // 2, 3 * width // 8
+    rest = tuple((b,) for b in range(3, bits))
+
+    def order(*groups):
+        groups = tuple(tuple(b for b in group if b < bits) for group in groups)
+        return tuple(group for group in groups if group) + rest
+
+    below = hid + local
     rows = [
-        (half, near_first, 1.0), (half, near_first, 1.0), (hid // 2, swapped, 1.0), (hid // 2, far_first, 1.0),
-        (local, far_first, 1.0), (sixth, near_first, 6.0), (sixth, swapped, 6.0),
+        (width // 2, order((0,), *PLANS[0]), 1.5, 1), (width // 2, order((0,), *PLANS[1]), 1.6, 1),
+        (below // 2, order((0,), *PLANS[2]), 1.7, 1), (below // 2, order((0,), *PLANS[3]), 1.8, 1),
+        (width // 2, order(*PLANS[4]), 3.2, 0), (width // 2, order(*PLANS[5]), 3.3, 0),
+        (width // 2, order(*PLANS[6]), 3.4, 0),
     ]
     pieces, start = [], 0
-    for size, order, ready in rows:
+    for size, groups, ready, done in rows:
         steps = []
-        left = size
-        for b in order:
-            halved = left % 32 == 0
-            steps.append((b, left, halved))
-            left = left // 2 if halved else left
-        pieces.append((start, size, ready, steps))
+        remaining = size
+        for n, group in enumerate(groups):
+            ways = 1 << len(group)
+            if n < done:
+                steps.append((group, ways * size, True))
+            elif remaining % (16 * ways) == 0:
+                steps.append((group, remaining, True))
+                remaining //= ways
+            else:
+                steps += [((b,), remaining, False) for b in group]
+        pieces.append((start, size, ready, steps, done))
         start += size
+        if start == width + below:
+            start *= 2
     return pieces, start
 
 
+NEAR, SWAP, FAR = ((0,), (1,), (2,)), ((1,), (0,), (2,)), ((2,), (0,), (1,))
+PAIR, ALL = ((0,), (1, 2)), ((0, 1, 2),)
+LINE, BACK = ((1,), (2,)), ((2,), (1,))
+BOTH = ((1, 2),)
+PLANS = (BACK, LINE, BOTH, LINE, NEAR, NEAR, NEAR)
+POST_TIME = (34.0, 34.1, 34.2, 38.0)
+SMALL_TIME = (0.0, 2.0, 90.0)
+
+
 def plan_length(steps):
-    return len(steps) + sum(halved for _, _, halved in steps)
-
-
-def step_times(pieces, bits):
-    free = [0.0] * bits
-    waiting = [(ready, n, 0) for n, (_, _, ready, _) in enumerate(pieces)]
+    return len(steps) + sum(split for _, _, split in steps)
+
+
+def step_times(pieces):
+    free = {}
+    waiting = [(piece[2], n, piece[4]) for n, piece in enumerate(pieces)]
     times = []
     while waiting:
         now, n, t = min(waiting)
@@ -888,20 +979,31 @@
         if t == plan_length(steps):
             continue
         back = [s for s in reversed(steps) if s[2]]
-        b, size, halved = steps[t] if t < len(steps) else back[t - len(steps)]
-        cost = (size // 2 if halved else size) * ROW_TIME * (2 if b == 2 else 1)
-        free[b] = max(now, free[b]) + cost
-        waiting.append((free[b] + HOP_TIME, n, t + 1))
+        group, size, split = steps[t] if t < len(steps) else back[t - len(steps)]
+        begin = max([now] + [free.get(b, 0.0) for b in group])
+        end = begin
+        for b in group:
+            cost = size * ROW_TIME * (0.5 if split else 1.0) * (1.0 if b == 0 else 1.5 if len(group) > 1 else b)
+            free[b] = begin + cost
+            end = max(end, free[b])
+        waiting.append((end + HOP_TIME, n, t + 1))
     return times
+
+
+def flipped(place, mask, bits):
+    for b in range(bits):
+        if mask >> b & 1:
+            place = place + (1 << b) - 2 * (1 << b) * ((place // (1 << b)) % 2)
+    return place
 
 
 def tail_kernel(
     dp_size,
-    dq, dk, dv, tok_t, w, sum1, keep, given, small,
+    dq, dk, dv, tok_t, w, sum1, keep, given0, given1, given2, small,
     post_out, full_out, small_out,
-    grads, tok_b, sum1_b, given_b, mine, far, send_far, recv_far, pass_far, land_far, send_near, recv_near,
+    grads, tok_b, w_t, sum1_b, keep_b, given_b, mine, far, send_far, recv_far, pass_far, land_far, send_near, recv_near,
     acc, flight, full, land, small_flight, small_land,
-    in_sem, near_send, near_recv, far_send, far_recv, hop_send, hop_recv,
+    in_sem, grad_sem, near_send, near_recv, far_send, far_recv, hop_send, hop_recv,
     step_send, step_recv, small_send, small_recv, out_sem, full_sem,
 ):
     me, sib, across, diagonal = mp_peers()
@@ -913,120 +1015,164 @@
     tall = keep.shape[0]
     hid = tall - width - local
     bits = dp_size.bit_length() - 1
-    partners = [dp + (1 << b) - 2 * (1 << b) * ((dp // (1 << b)) % 2) for b in range(bits)]
-    upper = [(dp // (1 << b)) % 2 for b in range(bits)]
     pieces, total = sum_plan(dp_size, width, hid, local)
 
     loads = [
-        pltpu.make_async_copy(src, grads.at[n], in_sem.at[n]) for n, src in enumerate((dq, dk, dv))
-    ] + [
+        pltpu.make_async_copy(keep, keep_b, in_sem.at[0]),
+        pltpu.make_async_copy(given0, given_b.at[0], in_sem.at[1]),
+        pltpu.make_async_copy(given1, given_b.at[1], in_sem.at[2]),
+        pltpu.make_async_copy(given2, given_b.at[2], in_sem.at[5]),
         pltpu.make_async_copy(tok_t, tok_b, in_sem.at[3]),
-        pltpu.make_async_copy(keep, acc.at[pl.ds(0, tall)], in_sem.at[5]),
-        pltpu.make_async_copy(given, given_b, in_sem.at[6]),
         pltpu.make_async_copy(sum1, sum1_b, in_sem.at[4]),
     ]
-    for n in (4, 5, 0, 1, 2, 3, 6):
-        loads[n].start()
-    greet([(dp, sib), (dp, across)] + [(p, me) for p in partners])
-
-    offsets = {}
-    for n, (base, _, _, steps) in enumerate(pieces):
+
+    def grad_loads(g, owner):
+        here = ds(owner * rows, rows)
+        return [
+            pltpu.make_async_copy(src.at[here], grads.at[here, pl.ds(n * local, local)], grad_sem.at[g, n])
+            for n, src in enumerate((dq, dk, dv))
+        ]
+
+    owners = (diagonal, across, sib, me)
+    for load in grad_loads(0, diagonal) + loads[:4] + grad_loads(1, across):
+        load.start()
+    for load in grad_loads(2, sib) + grad_loads(3, me) + loads[4:]:
+        load.start()
+    for n in range(3):
+        w_t[pl.ds(n * local, local)] = w[n].T
+    greet([(dp, sib), (dp, across), (dp, diagonal)] + [(flipped(dp, mask, bits), me) for mask in partner_masks(pieces, bits)])
+
+    spots = {}
+    ids = {}
+    for n, (base, _, _, steps, done) in enumerate(pieces):
         base = jnp.int32(base)
-        for t, (b, size, halved) in enumerate(steps):
-            if halved:
-                half = size // 2
-                offsets[n, t] = (base + (1 - upper[b]) * half, base + upper[b] * half, half)
-                base = base + upper[b] * half
-            else:
-                offsets[n, t] = (base, base, size)
-
-    def reduce_copy(n, t):
-        given_at, _, size = offsets[n, t]
-        here = ds16(given_at, size)
+        for t, (group, size, split) in enumerate(steps):
+            ways = 1 << len(group)
+            part = size // ways if split else size
+            places = []
+            for m in range(ways):
+                mask = sum(1 << b for k, b in enumerate(group) if m >> k & 1)
+                there = flipped(dp, mask, bits)
+                rank = sum((there // (1 << b)) % 2 * (1 << k) for k, b in enumerate(group))
+                places.append((there, base + rank * (tall if t < done else part) if split else base))
+                ids[n, t, m] = len(ids)
+            spots[n, t] = (places, part)
+            base = places[0][1]
+
+    def reduce_copy(n, t, m):
+        places, part = spots[n, t]
+        there, at = places[m]
+        own = places[0][1]
         return remote(
-            flight.at[here], land.at[t, here],
-            step_send.at[0, n, t], step_recv.at[0, n, t], (partners[pieces[n][3][t][0]], me),
+            flight.at[ds16(at, part)], land.at[t, ds16(own, part)],
+            step_send.at[0, ids[n, t, m]], step_recv.at[0, ids[n, t, m]], (there, me),
         )
 
     def reduce_start(n, t):
-        given_at, _, size = offsets[n, t]
-        here = ds16(given_at, size)
-        flight[here] = acc[here].astype(BF16)
-        reduce_copy(n, t).start()
+        places, part = spots[n, t]
+        for m in range(1, len(places)):
+            here = ds16(places[m][1], part)
+            flight[here] = acc[here].astype(BF16)
+            reduce_copy(n, t, m).start()
 
     def reduce_finish(n, t):
-        _, kept_at, size = offsets[n, t]
-        copy = reduce_copy(n, t)
-        copy.wait_recv()
-        here = ds16(kept_at, size)
-        if pieces[n][3][t][2]:
-            acc[here] = acc[here] + land[t, here].astype(F32)
+        places, part = spots[n, t]
+        split = pieces[n][3][t][2]
+        own = ds16(places[0][1], part)
+        if split:
+            value = acc[own]
         else:
-            acc[here] = flight[here].astype(F32) + land[t, here].astype(F32)
-        copy.wait_send()
-
-    def spread_copy(n, t):
-        _, kept_at, size = offsets[n, t]
-        here = ds16(kept_at, size)
+            value = flight[own].astype(F32)
+        for m in range(1, len(places)):
+            there = ds16(places[m][1], part)
+            pltpu.make_async_copy(land.at[t, there], land.at[t, there], step_recv.at[0, ids[n, t, m]]).wait()
+            value = value + land[t, there].astype(F32)
+        acc[own] = value
+        for m in range(1, len(places)):
+            reduce_copy(n, t, m).wait_send()
+
+    def spread_copy(n, t, m):
+        places, part = spots[n, t]
+        own = ds16(places[0][1], part)
         return remote(
-            full.at[here], full.at[here],
-            step_send.at[1, n, t], step_recv.at[1, n, t], (partners[pieces[n][3][t][0]], me),
+            full.at[own], full.at[own],
+            step_send.at[1, ids[n, t, m]], step_recv.at[1, ids[n, t, m]], (places[m][0], me),
         )
 
+    def spread_start(n, t):
+        for m in range(1, len(spots[n, t][0])):
+            spread_copy(n, t, m).start()
+
     def spread_done(n, t):
-        given_at, _, size = offsets[n, t]
-        there = ds16(given_at, size)
-        pltpu.make_async_copy(full.at[there], full.at[there], step_recv.at[1, n, t]).wait()
-        spread_copy(n, t).wait_send()
-
-    def full_copy(n):
-        here = pl.ds(pieces[n][0], pieces[n][1])
-        return pltpu.make_async_copy(full.at[here], full_out.at[here], full_sem.at[n])
+        places, part = spots[n, t]
+        for m in range(1, len(places)):
+            there = ds16(places[m][1], part)
+            pltpu.make_async_copy(full.at[there], full.at[there], step_recv.at[1, ids[n, t, m]]).wait()
+            spread_copy(n, t, m).wait_send()
+
+    def full_copies(n):
+        starts = [pieces[n][0] + s * tall for s in range(1 + pieces[n][4])]
+        return [
+            pltpu.make_async_copy(full.at[pl.ds(start, pieces[n][1])], full_out.at[pl.ds(start, pieces[n][1])], full_sem.at[n, s])
+            for s, start in enumerate(starts)
+        ]
 
     def stage(n, t):
         steps = pieces[n][3]
         back = [s for s in range(len(steps) - 1, -1, -1) if steps[s][2]]
-        if 0 < t <= len(steps):
+        if pieces[n][4] < t <= len(steps):
             reduce_finish(n, t - 1)
         if t < len(steps):
             reduce_start(n, t)
             return
         if t == len(steps):
-            _, kept_at, size = offsets[n, len(steps) - 1]
-            here = ds16(kept_at, size)
+            places, part = spots[n, len(steps) - 1]
+            here = ds16(places[0][1], part)
             full[here] = acc[here].astype(BF16)
         else:
             spread_done(n, back[t - len(steps) - 1])
         if t < plan_length(steps):
-            spread_copy(n, back[t - len(steps)]).start()
+            spread_start(n, back[t - len(steps)])
         else:
-            full_copy(n).start()
-
-    small_peers = [(dp, sib), (dp, across)] + [(p, me) for p in partners]
-
-    def small_copy(s):
-        return remote(small_flight.at[s], small_land.at[s], small_send.at[s], small_recv.at[s], small_peers[s])
+            for copy in full_copies(n):
+                copy.start()
+
+    phases = [[(dp, peer) for peer in (sib, across, diagonal)]]
+    for low in range(0, bits, 3):
+        high = min(low + 3, bits)
+        phases.append([(flipped(dp, mask << low, bits), me) for mask in range(1, 1 << (high - low))])
+
+    def small_copy(s, n):
+        return remote(small_flight.at[s], small_land.at[s, n], small_send.at[s, n], small_recv.at[s, n], phases[s][n])
+
+    def ranked(own, arrived, place, ways):
+        values = [own] + arrived
+        total = None
+        for rank in range(ways):
+            value = values[0]
+            for n in range(1, ways):
+                value = jnp.where((place ^ n) == rank, values[n], value)
+            total = value if total is None else total + value
+        return total
 
     def small_stage(s):
         if s == 0:
             small_out[...] = small[...]
-            query_sum = column_sum(grads[0].astype(F32))
-            value_sum = column_sum(grads[2].astype(F32))
-            small_out[ds1(12 + me), :] = jnp.concatenate(
-                [query_sum, value_sum, jnp.zeros((1, width - 2 * local), F32)], axis=1
+        else:
+            for n in range(len(phases[s - 1])):
+                small_copy(s - 1, n).wait()
+            arrived = [small_land[s - 1, n] for n in range(len(phases[s - 1]))]
+            place = me if s == 1 else (dp // (1 << (3 * (s - 2)))) % 8
+            small_out[...] = ranked(small_out[...], arrived, place, len(arrived) + 1)
+        if s == 1:
+            sums = column_sum(grads[...].astype(F32))
+            small_out[12:13] = jnp.concatenate(
+                [sums[:, :local], sums[:, 2 * local :], jnp.zeros((1, width - 2 * local), F32)], axis=1
             )
-        else:
-            small_copy(s - 1).wait()
-            small_out[...] = small_out[...] + small_land[s - 1]
-        if s < len(small_peers):
+        if s < len(phases):
             small_flight[s] = small_out[...]
-            small_copy(s).start()
-
-    def part(owner, c):
-        here = ds(owner * rows + c * chunk, chunk)
-        return (
-            dot(grads[0, here], w[0], NT) + dot(grads[1, here], w[1], NT) + dot(grads[2, here], w[2], NT)
-        )
+            for n in range(len(phases[s])):
+                small_copy(s, n).start()
 
     def far_copy(c):
         return remote(send_far.at[c], recv_far.at[c], far_send.at[c], far_recv.at[c], (dp, sib))
@@ -1041,60 +1187,72 @@
         here = pl.ds(c * chunk, chunk)
         return pltpu.make_async_copy(sum1_b.at[here], post_out.at[here], out_sem.at[c])
 
-    def far_step(c):
-        if c == 0:
-            for n in range(3):
-                loads[n].wait()
-        send_far[c] = part(diagonal, c).astype(BF16)
-        far_copy(c).start()
-        far[c] = part(across, c)
+    def arrive(g):
+        for load in grad_loads(g, owners[g]):
+            load.wait()
+
+    def part(g):
+        if g < 2:
+            arrive(g)
+        return dot(grads[ds(owners[g] * rows, rows)], w_t[...]).reshape(count, chunk, width)
+
+    def far_step(n):
+        if n == 0:
+            send_far[...] = part(0).astype(BF16)
+            for c in range(count):
+                far_copy(c).start()
+        else:
+            far[...] = part(1)
 
     def hop_step(c):
         far_copy(c).wait_recv()
         pass_far[c] = (far[c] + recv_far[c].astype(F32)).astype(BF16)
         hop_copy(c).start()
 
-    def near_step(c):
-        send_near[c] = part(sib, c).astype(BF16)
-        near_copy(c).start()
-        mine[c] = part(me, c)
-
-    def near_add(c):
-        near_copy(c).wait_recv()
-        mine[c] = mine[c] + recv_near[c].astype(F32)
+    def near_step(_):
+        send_near[...] = part(2).astype(BF16)
+        for c in range(count):
+            near_copy(c).start()
+        mine[...] = part(3)
 
     def post_step(c):
         if c == 0:
-            loads[6].wait()
+            loads[5].wait()
+        near_copy(c).wait_recv()
         hop_copy(c).wait_recv()
         here = pl.ds(c * chunk, chunk)
-        sum1_b[here] = sum1_b[here] + mine[c] + land_far[c].astype(F32)
+        sum1_b[here] = sum1_b[here] + (mine[c] + recv_near[c].astype(F32)) + land_far[c].astype(F32)
         post_copy(c).start()
 
     def own_sums(_):
+        for load in loads[:4]:
+            load.wait()
+        total = keep_b[...]
+        for n in range(3):
+            total = total + given_b[n].astype(F32)
+        acc[ds16((dp % 2) * tall, tall)] = total
+
+    def weight_step(_):
         loads[4].wait()
-        loads[5].wait()
-        own = pl.ds(0, tall)
-        acc[own] = acc[own] + given_b[...].astype(F32)
-
-    def weight_step(_):
-        loads[3].wait()
-        third = width // 4
-        for n in range(3):
-            block = dot(tok_b[...], grads[n])
-            for s in range(4):
-                acc[pl.ds(tall + n * third, third), pl.ds(s * local, local)] = block[s * third : (s + 1) * third]
-
-    events = [(now, 5, stage, (n, t)) for now, n, t in step_times(pieces, bits)]
-    events += [(0.9, 0, own_sums, (0,)), (5.9, 0, weight_step, (0,))]
+        block = dot(tok_b[...], grads[...])
+        base = 2 * tall
+        acc[pl.ds(base, width)] = block[:, : 2 * local]
+        for s in range(2):
+            acc[pl.ds(base + width, width // 2), pl.ds(s * local, local)] = block[
+                s * width // 2 : (s + 1) * width // 2, 2 * local :
+            ]
+
+    events = [(now, 5, stage, (n, t)) for now, n, t in step_times(pieces)]
+    events += [
+        (1.0, 0, far_step, (0,)), (1.1, 0, own_sums, (0,)), (2.0, 0, far_step, (1,)),
+        (2.8, 0, arrive, (2,)), (2.8, 0, arrive, (3,)),
+        (3.2, 0, weight_step, (0,)), (3.3, 0, near_step, (0,)),
+    ]
     for c in range(count):
-        events.append((1.5 + 0.7 * c, 1, far_step, (c,)))
-        events.append((2.9 + 0.7 * c, 2, hop_step, (c,)))
-        events.append((6.5 + 0.7 * c, 3, near_step, (c,)))
-        events.append((11.0 + 0.7 * c, 3, near_add, (c,)))
-        events.append((12.5 + 5.3 * c, 6, post_step, (c,)))
-    for s in range(len(small_peers) + 1):
-        events.append((9.5 + 3.5 * s, 4, small_stage, (s,)))
+        events.append((2.1 + 0.3 * c, 1, hop_step, (c,)))
+        events.append((POST_TIME[c], 7, post_step, (c,)))
+    for s in range(len(phases) + 1):
+        events.append((SMALL_TIME[min(s, 2)] + s, 4, small_stage, (s,)))
     for _, _, act, where in sorted(events, key=lambda event: event[:2] + (event[3],)):
         act(*where)
 
@@ -1104,15 +1262,22 @@
         near_copy(c).wait_send()
         post_copy(c).wait()
     for n in range(len(pieces)):
-        full_copy(n).wait()
-
-
-def ds16(start, size):
-    return pl.ds(pl.multiple_of(start, 16), size)
+        for copy in full_copies(n):
+            copy.wait()
 
 
 def ds1(start):
     return pl.ds(start, 1)
+
+
+def partner_masks(pieces, bits):
+    masks = {mask << low for low in range(0, bits, 3) for mask in range(1, 1 << min(3, bits - low))}
+    for _, _, _, steps, _ in pieces:
+        for group, _, _ in steps:
+            for m in range(1, 1 << len(group)):
+                masks.add(sum(1 << b for k, b in enumerate(group) if m >> k & 1))
+            masks.update(1 << b for b in group)
+    return sorted(masks)
 
 
 def tail(dp_size, dq, dk, dv, tok_t, w, sum1, keep, given, small):
@@ -1122,24 +1287,28 @@
     hid = tall - width - local
     count = rows // TILE
     bits = dp_size.bit_length() - 1
-    assert 1 << bits == dp_size
+    assert 1 << bits == dp_size and bits > 0
     pieces, total = sum_plan(dp_size, width, hid, local)
     blocks = (count, TILE, width)
-    steps = bits + 2
+    phases = 1 + (bits + 2) // 3
+    longest = max(len(piece[3]) for piece in pieces)
+    copies = sum(1 << len(step[0]) for piece in pieces for step in piece[3])
     return pl.pallas_call(
         functools.partial(tail_kernel, dp_size),
         out_shape=(
             jax.ShapeDtypeStruct((rows, width), F32),
-            jax.ShapeDtypeStruct((total, width), BF16),
+            jax.ShapeDtypeStruct((total, HALF), BF16),
             jax.ShapeDtypeStruct(small.shape, F32),
         ),
-        in_specs=[ANY] * 4 + [VMEM] + [ANY] * 3 + [VMEM],
+        in_specs=[ANY] * 4 + [VMEM] + [ANY] * 5 + [VMEM],
         out_specs=(ANY, ANY, VMEM),
         scratch_shapes=[
-            pltpu.VMEM((3, group, local), BF16),
+            pltpu.VMEM((group, 3 * local), BF16),
             pltpu.VMEM((width, group), BF16),
+            pltpu.VMEM((3 * local, width), BF16),
             pltpu.VMEM((rows, width), F32),
-            pltpu.VMEM((tall, width), BF16),
+            pltpu.VMEM((tall, HALF), F32),
+            pltpu.VMEM((3, tall, HALF), BF16),
             pltpu.VMEM(blocks, F32),
             pltpu.VMEM(blocks, F32),
             pltpu.VMEM(blocks, BF16),
@@ -1148,75 +1317,92 @@
             pltpu.VMEM(blocks, BF16),
             pltpu.VMEM(blocks, BF16),
             pltpu.VMEM(blocks, BF16),
-            pltpu.VMEM((total, width), F32),
-            pltpu.VMEM((total, width), BF16),
-            pltpu.VMEM((total, width), BF16),
-            pltpu.VMEM((bits, total, width), BF16),
-            pltpu.VMEM((steps,) + small.shape, F32),
-            pltpu.VMEM((steps,) + small.shape, F32),
-            dma_sems(7), dma_sems(count), dma_sems(count), dma_sems(count), dma_sems(count),
-            dma_sems(count), dma_sems(count), dma_sems(2, len(pieces), bits), dma_sems(2, len(pieces), bits),
-            dma_sems(steps), dma_sems(steps), dma_sems(count), dma_sems(len(pieces)),
+            pltpu.VMEM((total, HALF), F32),
+            pltpu.VMEM((total, HALF), BF16),
+            pltpu.VMEM((total, HALF), BF16),
+            pltpu.VMEM((longest, total, HALF), BF16),
+            pltpu.VMEM((phases,) + small.shape, F32),
+            pltpu.VMEM((phases, 7) + small.shape, F32),
+            dma_sems(6), dma_sems(4, 3), dma_sems(count), dma_sems(count), dma_sems(count), dma_sems(count),
+            dma_sems(count), dma_sems(count), dma_sems(2, copies), dma_sems(2, copies),
+            dma_sems(phases, 7), dma_sems(phases, 7), dma_sems(count), dma_sems(len(pieces), 2),
         ],
         compiler_params=pltpu.CompilerParams(
             collective_id=2, has_side_effects=True, vmem_limit_bytes=60 << 20
         ),
         cost_estimate=pl.CostEstimate(flops=4 << 30, bytes_accessed=20 << 20, transcendentals=0),
         name="tail",
-    )(dq, dk, dv, tok_t, w, sum1, keep, given, small)
+    )(dq, dk, dv, tok_t, w, sum1, keep, *given, small)
 
 
 def finish_kernel(
     post_sum, full, small,
     post_grad, qkv_grad, up_grad, down_grad, out_grad,
     query_grad, value_grad, out_bias, gain1, shift1, up_bias, down_bias, gain2, shift2,
-    post_b, full_b, grad_b, qkv_b, sem, out_sem,
+    post_b, full_b, grad_b, qkv_b, sem, post_sem, out_sem,
 ):
     me = lax.axis_index("mp")
-    total, width = full.shape
+    total, _ = full.shape
+    rows, width = post_sum.shape
     local = query_grad.shape[0]
     hid = down_grad.shape[0]
     tall = width + hid + local
-    third = width // 4
-    post_in = pltpu.make_async_copy(post_sum, post_b, sem.at[0])
-    post = pltpu.make_async_copy(post_b, post_grad, sem.at[5])
-    post_in.start()
-    spans = ((0, width, up_grad), (width, hid, down_grad), (width + hid, local, out_grad), (tall, total - tall, None))
-    loads = []
-    for n, (start, size, _) in enumerate(spans):
+    count = 4
+
+    def post_in(c):
+        here = pl.ds(c * rows // count, rows // count)
+        return pltpu.make_async_copy(post_sum.at[here], post_b.at[here], post_sem.at[0, c])
+
+    def post_out(c):
+        here = pl.ds(c * rows // count, rows // count)
+        return pltpu.make_async_copy(post_b.at[here], post_grad.at[here], post_sem.at[1, c])
+
+    spans = ((0, width, up_grad), (width, hid, down_grad), (width + hid, local, out_grad))
+
+    def full_in(s, n):
+        start, size = (s * tall + spans[n][0], spans[n][1]) if n < 3 else (2 * tall, total - 2 * tall)
         here = pl.ds(start, size)
-        loads.append(pltpu.make_async_copy(full.at[here], full_b.at[here], sem.at[1 + n]))
-        loads[-1].start()
+        return pltpu.make_async_copy(full.at[here], full_b.at[here], sem.at[s, n])
+
+    parts = [(s, n) for n in range(3) for s in range(2)] + [(0, 3)]
+    for c in range(count):
+        post_in(c).start()
+    for s, n in parts:
+        full_in(s, n).start()
     for row, vector in enumerate((out_bias, gain1, shift1, down_bias, gain2, shift2)):
         vector[...] = small[row]
-    own = small[pl.ds(12 + me, 1), :]
+    own = small[12:13]
     query_grad[...] = own[0, :local]
     value_grad[...] = own[0, local : 2 * local]
     up_bias[...] = small[pl.ds(8 + me, 1), :][0]
     stores = []
-    post_in.wait()
-    post.start()
+    for c in range(count):
+        post_in(c).wait()
+        stores.append(post_out(c))
+        stores[-1].start()
     for n, (start, size, dst) in enumerate(spans):
-        loads[n].wait()
-        here = pl.ds(start, size)
-        if dst is not None:
-            grad_b[here] = full_b[here].astype(F32)
-            stores.append(pltpu.make_async_copy(grad_b.at[here], dst, out_sem.at[n]))
-        else:
-            for m in range(3):
-                for s in range(4):
-                    qkv_b[m, pl.ds(s * third, third)] = full_b[
-                        pl.ds(start + m * third, third), pl.ds(s * local, local)
-                    ].astype(F32)
-            stores.append(pltpu.make_async_copy(qkv_b, qkv_grad, out_sem.at[n]))
+        for s in range(2):
+            full_in(s, n).wait()
+            grad_b[pl.ds(start, size), pl.ds(s * HALF, HALF)] = full_b[pl.ds(s * tall + start, size)].astype(F32)
+        stores.append(pltpu.make_async_copy(grad_b.at[pl.ds(start, size)], dst, out_sem.at[n]))
         stores[-1].start()
-    for store in stores + [post]:
+    full_in(0, 3).wait()
+    for m in range(2):
+        qkv_b[m] = full_b[pl.ds(2 * tall, width), pl.ds(m * local, local)].astype(F32)
+    for s in range(2):
+        qkv_b[2, pl.ds(s * width // 2, width // 2)] = full_b[
+            pl.ds(2 * tall + width, width // 2), pl.ds(s * local, local)
+        ].astype(F32)
+    stores.append(pltpu.make_async_copy(qkv_b, qkv_grad, out_sem.at[3]))
+    stores[-1].start()
+    for store in stores:
         store.wait()
 
 
 def finish(post_sum, full, small, hid, local):
     rows, width = post_sum.shape
     total = full.shape[0]
+    tall = width + hid + local
     vector = lambda size: jax.ShapeDtypeStruct((size,), F32)
     return pl.pallas_call(
         finish_kernel,
@@ -1233,10 +1419,10 @@
         out_specs=(ANY,) * 5 + (VMEM,) * 9,
         scratch_shapes=[
             pltpu.VMEM((rows, width), F32),
-            pltpu.VMEM((total, width), BF16),
-            pltpu.VMEM((total, width), F32),
+            pltpu.VMEM((total, HALF), BF16),
+            pltpu.VMEM((tall, width), F32),
             pltpu.VMEM((3, width, local), F32),
-            dma_sems(6), dma_sems(4),
+            dma_sems(2, 4), dma_sems(2, 4), dma_sems(4),
         ],
         compiler_params=pltpu.CompilerParams(vmem_limit_bytes=60 << 20),
         name="results",
@@ -1267,17 +1453,23 @@
     local = out_weight.shape[0]
     hid = down_weight.shape[0]
     qkv3 = jnp.transpose(qkv_weight, (1, 0, 2))
-    tok_t, queries, k, v, kt, vt, starts, limits, own = gather_and_project(
-        seq_lengths, post_stream, qkv3, query_bias, value_bias, (up_weight, down_weight, out_weight)
+    tok_t, queries, k, v, kt, vt, starts, limits, own, far_line = gather_and_project(
+        dp_size, seq_lengths, post_stream, qkv3, query_bias, value_bias, (up_weight, down_weight, out_weight)
     )
     across = [(m, (m + 2) % MP) for m in range(MP)]
-    far = lax.ppermute(own, "mp", across)
+    beside = [(d, d + 1 - 2 * (d % 2)) for d in range(dp_size)]
+    corner = [(d * MP + m, e * MP + n) for d, e in beside for m, n in across]
+    far_side = lax.ppermute(far_line, "dp", beside)
     att, lse, tiles, counts = attend(limits, starts, queries, k, vt)
     vectors = (out_bias, norm1_gain, norm1_shift, down_bias, norm2_gain, norm2_shift, up_bias)
-    post_mid, pre_mid, sum1, att_grad, keep, give, small = middle(
-        att, post_stream, pre_stream, post_cotan, pre_cotan, own, far, vectors
+    post_mid, pre_mid, sum1, att_grad, keep, to_across, to_beside, to_corner, small = middle(
+        att, post_stream, pre_stream, post_cotan, pre_cotan, own, far_line, far_side, vectors
     )
-    given = lax.ppermute(give, "mp", across)
+    given = (
+        lax.ppermute(to_across, "mp", across),
+        lax.ppermute(to_beside, "dp", beside),
+        lax.ppermute(to_corner, ("dp", "mp"), corner),
+    )
     dq, dk, dv, post_out, pre_out = attend_back(
         tiles, counts, starts, lse, queries, k, v, kt, att, att_grad, post_mid, pre_mid
     )

time: 192 us -> 184 us (0.958)
  waiting for transfers between devices: 11.4 us -> 0.01 us
  starting transfers between devices: 1.33 us -> 5.54 us
  Pallas kernels: 176 us -> 174 us
    ppermute x2 -> x4, waiting for transfers between devices: 11.4 us -> 0.01 us  [the longest x1 0.01 us: body(): lax.ppermute(to_across, 'mp', across)]
    pallas_call x1, Pallas kernels: 58.8 us -> 51.9 us  [tail(): pl.pallas_call(functools.partial(tail_kernel, dp_size), out_shape=(jax.Sh...]
    pallas_call x1, Pallas kernels: 32.4 us -> 37.6 us  [gather_and_project(): pl.pallas_call(functools.partial(project_kernel, dp_size), out_shape=(jax...]
    ppermute x2 -> x4, starting transfers between devices: 1.33 us -> 5.54 us  [the longest x1 2.45 us: body(): lax.ppermute(to_beside, 'dp', beside)]
  transfers between devices with their start and end apart: 2 -> 4, of which waited for: 2 -> 0; matrix products, arithmetic and copies ran while one was open for 0% -> 0% of each run, Pallas kernels for 23% -> 24%
where the time goes in v3:
time: 184 us; the launch traced here: 183 us
  Pallas kernels  174 us (95%)
  starting transfers between devices  5.54 us (3%)
  local copies, waits for them, and re-layouts  1.99 us (1%)
    pallas_call x1, Pallas kernels, tail(): pl.pallas_call(functools.partial(tail_kernel, dp_size), out_shape=(jax.Sh...  51.9 us
    pallas_call x1, Pallas kernels, gather_and_project(): pl.pallas_call(functools.partial(project_kernel, dp_size), out_shape=(jax...  37.6 us
    pallas_call x1, Pallas kernels, middle(): pl.pallas_call(middle_kernel, out_shape=(f32, f32, f32, jax.ShapeDtypeStr...  35.1 us
    pallas_call x1, Pallas kernels, attend_back(): pl.pallas_call(attend_back_kernel, in_specs=[SMEM, SMEM, VMEM, VMEM] + [A...  27.4 us
    pallas_call x1, Pallas kernels, attend(): pl.pallas_call(attend_kernel, in_specs=[SMEM, VMEM, ANY, ANY, ANY], out_s...  17 us
    pallas_call x1, Pallas kernels, finish(): pl.pallas_call(finish_kernel, out_shape=(jax.ShapeDtypeStruct((rows, widt...  5.25 us
  transfers between devices with their start and end apart: 4, of which 0 were waited for; matrix products, arithmetic and copies ran while one was open for 0% of the time, Pallas kernels for 24%

profile of v3, /device:TPU:0, one launch (start us, length us, event | category | flops | bytes accessed | tf_op | source)
XLA Modules:
  0.0 182.8 jit_solution(1874614629286416460)
XLA Ops:
  0.6 37.6 %gather_project.1 = (bf16[512,4096]{1,0:T(8,128)(2,1)}, bf16[16,512,128]{2,1,0:T(8,128)(2,1)}, bf16[4096,128]{1,0:T(8,128)(2,1)}, bf16[4096,128]{1,0:T(8,128)(2,...) custom-call(s32[1,13]{1,0:T(1,128)} %lengths.1, ...), custom_call_target="tpu_custom_call" | custom-call | flops 1610612736 | bytes 12582912 | tf_op jit(solution)/shard_map/gather_project/pallas_call | solution.py:286
  38.3 1.6 collective-permute-start
  39.9 17.0 %attend.1 = (bf16[4096,128]{1,0:T(8,128)(2,1)}, f32[16,8,512]{2,1,0:T(8,128)}, s32[168]{0:T(256)}, s32[3]{0:T(128)}) custom-call(s32[2,16]{1,0:T(2,128)} %get-tuple-element.61.limits, s32[16,8,512]{2,1,0:T(8,128)} %get-tuple-element.62.starts_ref, bf16[16,512,128]{2,1,0:T(8,128)(2,1)} %get-tuple-element.63.q_ref, bf16[4096,128]{1,0:T(8,128)(2,1)} %get-tuple-element.64.k_ref, ...), custom_call_target="tpu_custom_call" | custom-call | flops 12884901888 | bytes 4194304 | tf_op jit(solution)/shard_map/attend/pallas_call | solution.py:452
  56.9 0.0 collective-permute-done.far_side
  56.9 0.0 copy-start.3
  56.9 0.8 copy-done.3
  57.7 35.1 %middle.1 = (f32[1024,512]{1,0:T(8,128)}, f32[1024,512]{1,0:T(8,128)}, f32[1024,512]{1,0:T(8,128)}, bf16[4096,128]{1,0:T(8,128)(2,1)}, f32[1152,256]{1,0:T(8,128...) custom-call(bf16[4096,128]{1,0:T(8,128)(2,1)} %get-tuple-element.69.at, ...), custom_call_target="tpu_custom_call" | custom-call | flops 16106127360 | bytes 20971520 | tf_op jit(solution)/shard_map/middle/pallas_call | solution.py:867
  92.9 0.6 collective-permute-start.1
  93.4 2.4 %collective-permute-start.2 = (bf16[1152,256]{1,0:T(8,128)(2,1)}, bf16[1152,256]{1,0:T(8,128)(2,1)S(1)}, u32[]{:S(2)}, u32[]{:S(2)}) collective-permute-start(bf16[1152,256]{1,0:T(8,128)(2,1)} %get-tuple-element.86), channel_id=1, source_target_pairs={{0,4},{4,0},{8,12},{12,8},{16,20},{20,16},{24,28},{28,24},{1,5},{5... | collective-permute-start | bytes 1769480 | tf_op jit(solution)/shard_map/ppermute | solution.py:1470
  95.9 0.9 collective-permute-start.3
  96.8 27.4 %attend_back.1 = (bf16[4096,128]{1,0:T(8,128)(2,1)}, bf16[4096,128]{1,0:T(8,128)(2,1)}, bf16[4096,128]{1,0:T(8,128)(2,1)}, f32[1024,512]{1,0:T(8,128)}, f32[1024,512]{1,0:T(8,128)}) custom-call(s32[168]{0:T(256)} %get-tuple-element.66.tiles, s32[3]{0:T(128)} %get-tuple-element.67.counts, s32[16,8,512]{2,1,0:T(8,128)} %get-tuple-element.62.starts_ref, ...), custom_call_target="tpu_custom_call" | custom-call | flops 32212254720 | bytes 9437184 | tf_op jit(solution)/shard_map/attend_back/pallas_call | solution.py:577
  124.2 0.0 collective-permute-done.1.given0
  124.2 0.0 copy-start
  124.2 0.0 collective-permute-done.2.given1
  124.2 0.0 copy-start.1
  124.3 0.0 collective-permute-done.3.given2
  124.3 0.0 copy-start.2
  124.3 0.8 copy-done
  125.0 0.2 copy-done.1
  125.2 0.2 copy-done.2
  125.5 51.9 %tail.1 = (f32[1024,512]{1,0:T(8,128)}, bf16[3072,256]{1,0:T(8,128)(2,1)}, f32[16,512]{1,0:T(8,128)}) custom-call(bf16[4096,128]{1,0:T(8,128)(2,1)} %get-tuple-element.79.dq, bf16[4096,128]{1,0:T(8,128)(2,1)} %get-tuple-element.80.dk, bf16[4096,128]{1,0:T(8,128)(2,1)} %get-tuple-element.81.dv, bf16[512,4096]{1,0:T(8,128)(2,1)} %get-tuple-element.82.tok_t, ...), custom_call_target="tpu_custom_call" | custom-call | flops 4294967296 | bytes 20971520 | tf_op jit(solution)/shard_map/tail/pallas_call | solution.py:1296
  177.4 5.2 %results.1 = (f32[1024,512]{1,0:T(8,128)}, f32[3,512,128]{2,1,0:T(8,128)}, f32[512,512]{1,0:T(8,128)}, f32[512,512]{1,0:T(8,128)}, f32[128,512]{1,0:T(8,128)}, /...) custom-call(f32[1024,512]{1,0:T(8,128)} %get-tuple-element.89.post_s, ...), custom_call_target="tpu_custom_call" | custom-call | tf_op jit(solution)/shard_map/results/pallas_call | solution.py:1407
Async XLA Ops:
  38.3 18.6 %collective-permute-start = (bf16[576,512]{1,0:T(8,128)(2,1)}, bf16[576,512]{1,0:T(8,128)(2,1)S(1)}, u32[]{:S(2)}, u32[]{:S(2)}) collective-permute-start(bf16[576,512]{1,0:T(8,128)(2,1)} %get-tuple-element.71.far_line), channel_id=1, source_target_pairs={{0,4},{4,0},{8,12},{12,8},{16,20},{20,16},{24,28},{28,24},{1,5},{5... | collective-permute-start | bytes 1769480 | tf_op jit(solution)/shard_map/ppermute | solution.py:1462
  56.9 0.8 copy-start.3
  92.9 31.4 %collective-permute-start.1 = (bf16[1152,256]{1,0:T(8,128)(2,1)}, bf16[1152,256]{1,0:T(8,128)(2,1)S(1)}, u32[]{:S(2)}, u32[]{:S(2)}) collective-permute-start(bf16[1152,256]{1,0:T(8,128)(2,1)} %get-tuple-element.85), channel_id=1, source_target_pairs={{0,2},{1,3},{2,0},{3,1},{4,6},{5,7},{6,4},{7,5},{8,10},{9,11},{10,... | collective-permute-start | bytes 1769480 | tf_op jit(solution)/shard_map/ppermute | solution.py:1469
  93.4 30.8 %collective-permute-start.2 = (bf16[1152,256]{1,0:T(8,128)(2,1)}, bf16[1152,256]{1,0:T(8,128)(2,1)S(1)}, u32[]{:S(2)}, u32[]{:S(2)}) collective-permute-start(bf16[1152,256]{1,0:T(8,128)(2,1)} %get-tuple-element.86), channel_id=1, source_target_pairs={{0,4},{4,0},{8,12},{12,8},{16,20},{20,16},{24,28},{28,24},{1,5},{5... | collective-permute-start | bytes 1769480 | tf_op jit(solution)/shard_map/ppermute | solution.py:1470
  95.9 28.4 %collective-permute-start.3 = (bf16[1152,256]{1,0:T(8,128)(2,1)}, bf16[1152,256]{1,0:T(8,128)(2,1)S(1)}, u32[]{:S(2)}, u32[]{:S(2)}) collective-permute-start(bf16[1152,256]{1,0:T(8,128)(2,1)} %get-tuple-element.87), channel_id=1, source_target_pairs={{0,6},{1,7},{2,4},{3,5},{4,2},{5,3},{6,0},{7,1},{8,14},{9,15},{10,... | collective-permute-start | bytes 1769480 | tf_op jit(solution)/shard_map/ppermute | solution.py:1471
  124.2 0.8 copy-start
  124.2 1.0 copy-start.1
  124.3 1.2 copy-start.2
